TPU v7x, 32 devices: a whole 2x2x4 slice. The times are simulated.
32 devices in a mesh: row: 16 (over z, x, core), col: 2 (over y).
Axes of the slice: x: 2, y: 2, z: 4, core: 2. Of those that a mesh axis runs over, the one named last changes fastest.
Arguments:
- pending: bfloat16 [16384, 2, 1024], P('row', 'col'), may hold values from -5 to 5
- panel: bfloat16 [16384, 2, 1024], P('row', None, 'col'), may hold values from -0.1875 to 0.1875
- panel_scale: float32 [16384, 2], P('row'), may hold values from 0.1 to 1
- inverse_blocks: bfloat16 [2, 1024, 1024], P(None, 'col'), as said below
Outputs:
- remaining: bfloat16 [16384, 2, 1024], P('row', 'col')
- solved: bfloat16 [2, 1024, 1024], P(None, 'col')
Inputs may be any that keep to these rules, and one draw needn't show every extreme that they name: `inverse_blocks`: each block is lower triangular with a positive diagonal, the inverse of a diagonal block of a Cholesky factor.
All inputs are finite; a program needn't handle non-finite values.
Results may differ from a plain program's by a relative error of at most 0.023.
Values may be sent and summed in bfloat16 or wider, within the bound.
No kernel may reach another device: no remote copies, remote signals or barrier semaphores. Data moves between devices by JAX's collectives and lax.ppermute only.
A program may use at most 64 MiB of HBM per device.

v0:
```python
import jax
import jax.numpy as jnp
from jax import lax
from jax.sharding import PartitionSpec as P


def spread(shard, axis, root):
    mine = lax.axis_index(axis) == root
    return lax.psum(jnp.where(mine, shard, jnp.zeros_like(shard)), axis)


def body(pending, panel, panel_scale, inverse_blocks):
    row_index = lax.axis_index("row")
    n_row = lax.axis_size("row")
    block = inverse_blocks.shape[2]
    total = pending.shape[0]
    current = pending[:, 0, :]
    slot_of_row = lax.broadcasted_iota(jnp.int32, (total,), 0) // block
    global_ids = slot_of_row * n_row + row_index
    solved_list = []
    for k in range(2):
        head = current.astype(jnp.float32)
        fan = lax.psum(head.astype(jnp.bfloat16), "col")
        local = jnp.dot(inverse_blocks[k], fan, preferred_element_type=jnp.float32).astype(
            jnp.bfloat16
        )
        arrived = spread(local, "row", k)
        solved_list.append(arrived)
        term = jnp.dot(panel[:, k, :], arrived, preferred_element_type=jnp.float32)
        newer = (current.astype(jnp.float32) - panel_scale[:, k : k + 1] * term).astype(
            jnp.bfloat16
        )
        current = jnp.where((global_ids > k)[:, None], newer, current)
    return (current[:, None, :], jnp.stack(solved_list))


def solution(mesh):
    placed = (P("row", "col", None), P("row", None, "col"), P("row", None), P(None, "col", None))
    return jax.shard_map(
        body,
        mesh=mesh,
        in_specs=placed,
        out_specs=(P("row", "col", None), P(None, "col", None)),
        check_vma=False,
    )
```

profile of v0, /device:TPU:0, one launch (start us, length us, event | category | flops | bytes accessed | tf_op | source)
XLA Modules:
  0.0 356.4 jit_solution(1187122413888016079)
XLA Ops:
  7.2 0.0 all-reduce.5.cloned.1.call-start
  7.2 3.9 %copy.9 = bf16[1024,1,1024]{0,2,1:T(8,128)(2,1)} copy(bf16[1024,1,1024]{2,0,1:T(8,128)(2,1)} %param.4) | data formatting | bytes 4194304 | tf_op args[0]
  11.2 0.0 all-reduce.5.cloned.1.call-update
  11.2 0.0 all-reduce.7.cloned.1.call-start
  11.2 65.7 %all-reduce.5.cloned.1.call-done = bf16[1024,1024]{0,1:T(8,128)(2,1)} async-done(((bf16[1024,1024]{0,1:T(8,128)(2,1)}), bf16[1024,1024]{0,1:T(8,128)(2,1)}) %all-reduce.5.cloned.1.call-update) | async-done | bytes 2097168 | tf_op jit(solution)/shard_map/psum | solution.py:23
  76.9 4.3 %fusion.5 = bf16[512,1024]{1,0:T(8,128)(2,1)} fusion(bf16[1024,1024]{0,1:T(8,128)(2,1)} %all-reduce.5.cloned.1.call-done, bf16[2,512,1024]{2,1,0:T(8,128)(2,1)} %param.7, pred[]{:T(512)S(6)} %eq.6), kind=kOutput, calls=%fused_computation.10 | convolution fusion | flops 1074790400 | bytes 4194305 | tf_op jit(solution)/shard_map/dot_general | solution.py:24
  81.3 0.0 all-reduce.7.cloned.1.call-update
  81.3 0.0 copy-start.4
  81.3 0.0 all-reduce.9.cloned.1.call-start
  81.4 0.0 copy-done
  81.4 4.2 %fusion.19 = (bf16[1024,1,512]{2,1,0:T(2,128)(2,1)}, bf16[1024,1,512]{2,1,0:T(2,128)(2,1)}) fusion(bf16[1024,2,512]{2,1,0:T(2,128)(2,1)S(1)} %copy-done), kind=kLoop, calls=%fused_computation.30 | loop fusion | bytes 4194304 | tf_op jit(solution)/shard_map/slice | solution.py:29
  85.5 0.0 copy-done.4
  85.6 89.0 %all-reduce.7.cloned.1.call-done = bf16[512,1024]{1,0:T(8,128)(2,1)} async-done(((bf16[512,1024]{1,0:T(8,128)(2,1)}), bf16[512,1024]{1,0:T(8,128)(2,1)}) %all-reduce.7.cloned.1.call-update) | async-done | bytes 1048592 | tf_op jit(solution)/shard_map/psum | solution.py:9
  174.5 5.3 %fusion.2 = bf16[1024,1024]{0,1:T(8,128)(2,1)} fusion(bf16[512,1024]{1,0:T(8,128)(2,1)} %all-reduce.7.cloned.1.call-done, f32[1024]{0:T(1024)S(1)} %bitcast.44, pred[1024]{0:T(1024)(128)(4,1)S(1)} %fusion.16, bf16[1024,1,512]{2,1,0:T(2,128)(2,1)} %get-tuple-element.7, bf16[1024,1,1024]{0,2,1:T(8,128)(2,1)} %copy.9), kind=kOutput, calls=%fused_computation.4 | convolution fusion | flops 1078984704 | bytes 6296576 | tf_op jit(solution)/shard_map/dot_general | solution.py:29
  179.9 0.0 all-reduce.9.cloned.1.call-update
  179.9 0.0 all-reduce.11.cloned.1.call-start
  179.9 0.0 copy-start.1
  180.0 62.3 %all-reduce.9.cloned.1.call-done = bf16[1024,1024]{0,1:T(8,128)(2,1)} async-done(((bf16[1024,1024]{0,1:T(8,128)(2,1)}), bf16[1024,1024]{0,1:T(8,128)(2,1)}) %all-reduce.9.cloned.1.call-update) | async-done | bytes 2097168 | tf_op jit(solution)/shard_map/psum | solution.py:23
  242.2 4.1 %fusion.7 = bf16[512,1024]{1,0:T(8,128)(2,1)} fusion(bf16[1024,1024]{0,1:T(8,128)(2,1)} %all-reduce.9.cloned.1.call-done, bf16[2,512,1024]{2,1,0:T(8,128)(2,1)} %param.7, pred[]{:T(512)S(6)} %eq.7), kind=kOutput, calls=%fused_computation.12 | convolution fusion | flops 1074790400 | bytes 4194305 | tf_op jit(solution)/shard_map/dot_general | solution.py:24
  246.3 0.0 all-reduce.11.cloned.1.call-update
  246.4 93.2 %all-reduce.11.cloned.1.call-done = bf16[512,1024]{1,0:T(8,128)(2,1)} async-done(((bf16[512,1024]{1,0:T(8,128)(2,1)}), bf16[512,1024]{1,0:T(8,128)(2,1)}) %all-reduce.11.cloned.1.call-update) | async-done | bytes 1048592 | tf_op jit(solution)/shard_map/psum | solution.py:9
  339.6 4.7 %fusion.4 = bf16[1024,1,1024]{0,2,1:T(8,128)(2,1)} fusion(bf16[1024,1024]{0,1:T(8,128)(2,1)S(1)} %copy-done.1, bf16[512,1024]{1,0:T(8,128)(2,1)} %all-reduce.11.cloned.1.call-done, f32[1024]{0:T(1024)S(1)} %bitcast.43, pred[1024]{0:T(1024)(128)(4,1)S(1)} %fusion.17, bf16[1024,1,512]{2,1,0:T(2,128)(2,1)} %get-tuple-element.6), kind=kOutput, calls=%fused_computation.7 | convolution fusion | flops 1078984704 | bytes 6296576 | tf_op jit(solution)/shard_map/dot_general | solution.py:29
  344.3 4.1 %copy.13 = bf16[1024,1,1024]{2,0,1:T(8,128)(2,1)} copy(bf16[1024,1,1024]{0,2,1:T(8,128)(2,1)} %fusion.4) | data formatting | bytes 4194304
  348.4 1.5 pad_maximum_fusion
  (9 shorter events, 0.0 us)
Async XLA Ops:
  7.2 69.8 %all-reduce.5.cloned.1.call-start = ((), (), s32[]{:S(2)}) async-start(), calls=%async_computation | async-start | bytes 4194304 | tf_op jit(solution)/shard_map/psum | solution.py:23
  11.2 163.4 %all-reduce.7.cloned.1.call-start = ((), (), s32[]{:S(2)}) async-start(), calls=%async_computation.1 | async-start | bytes 2097152 | tf_op jit(solution)/shard_map/psum | solution.py:9
  76.9 4.4 %copy-start = (bf16[1024,2,512]{2,1,0:T(2,128)(2,1)S(1)}, bf16[1024,2,512]{2,1,0:T(2,128)(2,1)}, u32[]{:S(2)}) copy-start(bf16[1024,2,512]{2,1,0:T(2,128)(2,1)} %param.5) | copy-start | bytes 6291460
  81.3 4.2 %copy-start.4 = (f32[1024,2]{0,1:T(2,128)S(1)}, f32[1024,2]{0,1:T(2,128)}, u32[]{:S(2)}) copy-start(f32[1024,2]{0,1:T(2,128)} %param.6) | copy-start | bytes 24580
  81.3 160.9 %all-reduce.9.cloned.1.call-start = ((), (), s32[]{:S(2)}) async-start(), calls=%async_computation.2 | async-start | bytes 4194304 | tf_op jit(solution)/shard_map/psum | solution.py:23
  179.9 159.7 %all-reduce.11.cloned.1.call-start = ((), (), s32[]{:S(2)}) async-start(), calls=%async_computation.3 | async-start | bytes 2097152 | tf_op jit(solution)/shard_map/psum | solution.py:9
  179.9 159.6 %copy-start.1 = (bf16[1024,1024]{0,1:T(8,128)(2,1)S(1)}, bf16[1024,1024]{0,1:T(8,128)(2,1)}, u32[]{:S(2)}) copy-start(bf16[1024,1024]{0,1:T(8,128)(2,1)} %fusion.2) | copy-start | bytes 6291460
  344.3 4.1 %copy-start.2 = (bf16[512,1024]{1,0:T(8,128)(2,1)S(1)}, bf16[512,1024]{1,0:T(8,128)(2,1)}, u32[]{:S(2)}) copy-start(bf16[512,1024]{1,0:T(8,128)(2,1)} %all-reduce.7.cloned.1.call-done) | copy-start | bytes 3145732
  344.3 4.1 %copy-start.3 = (bf16[512,1024]{1,0:T(8,128)(2,1)S(1)}, bf16[512,1024]{1,0:T(8,128)(2,1)}, u32[]{:S(2)}) copy-start(bf16[512,1024]{1,0:T(8,128)(2,1)} %all-reduce.11.cloned.1.call-done) | copy-start | bytes 3145732
Sparse Core Ops, SparseCore 0:
  11.3 65.5 all-reduce.4
  81.4 93.0 all-reduce.6
  180.0 62.1 all-reduce.8
  246.5 93.0 all-reduce.10
where the time goes:
time: 357 us; the launch traced here: 356 us
  waiting for transfers between devices  310 us (87%)
  matrix products  18.5 us (5%)
  between operations  13.8 us (4%)
  local copies, waits for them, and re-layouts  12.2 us (3%)
    psum x2, waiting for transfers between devices, spread(): return lax.psum(jnp.where(mine, shard, jnp.zeros_like(shard)), axis)  182 us
    psum x2, waiting for transfers between devices, body(): fan = lax.psum(head.astype(jnp.bfloat16), 'col')  128 us
    dot_general x2, matrix products, body(): term = jnp.dot(panel[:, k, :], arrived, preferred_element_type=jnp.float32)  10 us
    dot_general x2, matrix products, body(): jnp.dot(inverse_blocks[k], fan, preferred_element_type=jnp.float32)  8.45 us
    unnamed x12, local copies, waits for them, and re-layouts  8.05 us
  transfers between devices with their start and end apart: 4, of which 4 were waited for; matrix products, arithmetic and copies ran while one was open for 1% of the time, Pallas kernels for 0%

commit v1 on v0

v1 whole, which is shorter than its diff:
```python
import jax
import jax.numpy as jnp
from jax import lax
from jax.sharding import PartitionSpec as P

AXES = ("row", "col")
BF = jnp.bfloat16


def dot(a, b):
    return jnp.dot(a, b, preferred_element_type=jnp.float32)


def device(x, c, z, k):
    return ((z * 2 + x) * 2 + k) * 2 + c


PLACES = [(x, c, z, k) for z in range(4) for x in range(2) for k in range(2) for c in range(2)]


def paired(wanted):
    mate = {}
    for a, b in wanted:
        mate[a], mate[b] = b, a

    def partners(x, c, z, k):
        return ((x, c, z, 1 - k), (1 - x, c, z, k), (x, 1 - c, z, k), (1 - x, c, z, 1 - k))

    for choice in range(4):
        for place in PLACES:
            other = partners(*place)[choice]
            if place not in mate and other not in mate:
                mate[place], mate[other] = other, place
    assert len(mate) == len(PLACES)
    return [(device(*a), device(*b)) for a, b in mate.items()]


def swap(value, wanted):
    return lax.ppermute(value, AXES, paired(wanted))


def core_swap(value):
    return swap(value, [((x, c, z, 0), (x, c, z, 1)) for x, c, z, k in PLACES if k == 0])


def fan_out(solved, core, x, z, k):
    half = solved.shape[1] // 2
    left, right = solved[:, :half], solved[:, half:]
    hop = swap(right, [((0, c, 0, core), (1, c, 0, core)) for c in range(2)])
    mine = jnp.where(x == 0, left, hop)
    sent = [
        swap(mine, [((s, c, 0, core), (s, c, far, core)) for c in range(2) for s in range(2)])
        for far in (1, 2, 3)
    ]
    for far in (1, 2, 3):
        mine = jnp.where(z == far, sent[far - 1], mine)
    other = swap(mine, [((0, c, far, core), (1, c, far, core)) for c in range(2) for far in range(4)])
    mine = jnp.where(k == core, mine, core_swap(mine))
    other = jnp.where(k == core, other, core_swap(other))
    return jnp.concatenate(
        [jnp.where(x == 0, mine, other), jnp.where(x == 0, other, mine)], axis=1
    )


def update(current, scale, panel, solved, keep):
    newer = (current.astype(jnp.float32) - scale * dot(panel, solved)).astype(BF)
    return jnp.where(keep, newer, current)


def body(pending, panel, panel_scale, inverse_blocks):
    row, c = lax.axis_index("row"), lax.axis_index("col")
    z, x, k = row // 4, (row // 2) % 2, row % 2
    half = inverse_blocks.shape[1]
    share = pending[:, 0, :]
    top, bottom = share[:half], share[half:]
    inv0, inv1 = inverse_blocks[0], inverse_blocks[1]
    roots = [((0, 0, 0, 0), (0, 1, 0, 0))]
    seconds = [((0, 0, 0, 1), (0, 1, 0, 1))]

    far_top = swap(top, roots)
    far_bottom = swap(jnp.where(c == 0, bottom, inv1), roots)
    fan_top = (top.astype(jnp.float32) + far_top.astype(jnp.float32)).astype(BF)
    fan_bottom = (bottom.astype(jnp.float32) + far_bottom.astype(jnp.float32)).astype(BF)
    solved0 = (dot(inv0[:, :half], fan_top) + dot(inv0[:, half:], fan_bottom)).astype(BF)

    solved0_here = core_swap(solved0)
    inv1_far = core_swap(far_bottom)
    after = update(share, panel_scale[:, 0:1], panel[:, 0, :], solved0_here, True)
    message = jnp.where(c == 0, dot(inv1_far, after).astype(BF), after[:half])
    answer = swap(message, seconds)
    after_top = jnp.where(
        c == 0,
        (after[:half].astype(jnp.float32) + answer.astype(jnp.float32)).astype(BF),
        after[:half],
    )
    rest = jnp.where(c == 0, jnp.zeros_like(answer), answer).astype(jnp.float32)
    solved1 = (
        dot(inv1[:, :half], after_top) + dot(inv1[:, half:], after[half:]) + rest
    ).astype(BF)

    solved0 = fan_out(solved0, 0, x, z, k)
    solved1 = fan_out(solved1, 1, x, z, k)
    current = update(share, panel_scale[:, 0:1], panel[:, 0, :], solved0, row > 0)
    current = update(current, panel_scale[:, 1:2], panel[:, 1, :], solved1, row > 1)
    return current[:, None, :], jnp.stack([solved0, solved1])


def body_any(pending, panel, panel_scale, inverse_blocks):
    row = lax.axis_index("row")
    current = pending[:, 0, :]
    solved = []
    for k in range(2):
        fan = lax.psum(current, "col")
        local = dot(inverse_blocks[k], fan).astype(BF)
        arrived = lax.psum(jnp.where(row == k, local, jnp.zeros_like(local)), "row")
        solved.append(arrived)
        current = update(current, panel_scale[:, k : k + 1], panel[:, k, :], arrived, row > k)
    return current[:, None, :], jnp.stack(solved)


def solution(mesh):
    placed = (P("row", "col", None), P("row", None, "col"), P("row", None), P(None, "col", None))
    small = mesh.shape["row"] == 16 and mesh.shape["col"] == 2
    return jax.shard_map(
        body if small else body_any,
        mesh=mesh,
        in_specs=placed,
        out_specs=(P("row", "col", None), P(None, "col", None)),
        check_vma=False,
    )
```

time: 357 us -> 180 us (0.50)
  waiting for transfers between devices: 310 us -> 126 us
  starting transfers between devices: 0.16 us -> 14.3 us
  between operations: 13.8 us -> 0.96 us
  local copies, waits for them, and re-layouts: 12.2 us -> 18.6 us
  matrix products: 18.5 us -> 13 us
  other arithmetic: 1.52 us -> 5.64 us
    psum x4 -> x0, waiting for transfers between devices: 310 us -> none  [the longest x2 182 us: spread(): return lax.psum(jnp.where(mine, shard, jnp.zeros_like(shard)), axis)]
    ppermute x0 -> x19, waiting for transfers between devices: none -> 126 us  [swap(): return lax.ppermute(value, AXES, paired(wanted))]
    ppermute x0 -> x19, starting transfers between devices: none -> 14.3 us  [swap(): return lax.ppermute(value, AXES, paired(wanted))]
    dot_general x4 -> x8, matrix products: 18.5 us -> 13 us  [dot(): return jnp.dot(a, b, preferred_element_type=jnp.float32)]
    unnamed x12 -> x28, local copies, waits for them, and re-layouts: 8.05 us -> 10.4 us
  transfers between devices with their start and end apart: 4 -> 19, of which waited for: 4 -> 9; matrix products, arithmetic and copies ran while one was open for 1% -> 9% of each run, Pallas kernels for 0% -> 0%
where the time goes in v1:
time: 180 us; the launch traced here: 178 us
  waiting for transfers between devices  126 us (70%)
  local copies, waits for them, and re-layouts  18.6 us (10%)
  starting transfers between devices  14.3 us (8%)
  matrix products  13 us (7%)
  other arithmetic  5.64 us (3%)
    ppermute x19, waiting for transfers between devices, swap(): return lax.ppermute(value, AXES, paired(wanted))  126 us
    ppermute x19, starting transfers between devices, swap(): return lax.ppermute(value, AXES, paired(wanted))  14.3 us
    dot_general x8, matrix products, dot(): return jnp.dot(a, b, preferred_element_type=jnp.float32)  13 us
    unnamed x28, local copies, waits for them, and re-layouts  10.4 us
    slice x1, local copies, waits for them, and re-layouts, body(): panel[:, 1, :]  3.78 us
  transfers between devices with their start and end apart: 19, of which 9 were waited for; matrix products, arithmetic and copies ran while one was open for 9% of the time, Pallas kernels for 0%

profile of v1, /device:TPU:0, one launch (start us, length us, event | category | flops | bytes accessed | tf_op | source)
XLA Modules:
  0.0 178.1 jit_solution(16468206899813006867)
XLA Ops:
  0.6 3.9 %copy.12 = bf16[1024,1,1024]{0,2,1:T(8,128)(2,1)} copy(bf16[1024,1,1024]{2,0,1:T(8,128)(2,1)} %param.4) | data formatting | bytes 4194304 | tf_op args[0]
  4.6 2.7 %slice_bitcast_fusion.1 = (bf16[512,1024]{1,0:T(8,128)(2,1)}, bf16[1,512,1024]{2,1,0:T(8,128)(2,1)S(1)}) fusion(bf16[2,512,1024]{2,1,0:T(8,128)(2,1)} %param.7), kind=kLoop, calls=%fused_computation.29 | loop fusion | bytes 4194304 | tf_op jit(solution)/shard_map/squeeze | solution.py:76
  7.8 1.5 broadcast_select_fusion
  9.3 3.0 %collective-permute-start.1 = (bf16[512,1024]{0,1:T(8,128)(2,1)S(1)}, bf16[512,1024]{0,1:T(8,128)(2,1)S(1)}, u32[]{:S(2)}, u32[]{:S(2)}) collective-permute-start(bf16[512,1024]{0,1:T(8,128)(2,1)S(1)} %broadcast_select_fusion), channel_id=1, source_target_pairs={{0,1},{1,0},{4,6},{6,4},{5,7},{7,5},{8,10},{10,8},{9,11},{11,9},{1... | collective-permute-start | bytes 3145736 | tf_op jit(solution)/shard_map/ppermute | solution.py:39
  12.8 23.5 %collective-permute-done.1 = bf16[512,1024]{0,1:T(8,128)(2,1)S(1)} collective-permute-done((bf16[512,1024]{0,1:T(8,128)(2,1)S(1)}, bf16[512,1024]{0,1:T(8,128)(2,1)S(1)}, u32[]{:S(2)}, u32[]{:S(2)}) %collective-permute-start.1) | collective-permute-done | bytes 1048608 | tf_op jit(solution)/shard_map/ppermute | solution.py:39
  37.1 20.8 %collective-permute-done = bf16[512,1024]{1,0:T(8,128)(2,1)S(1)} collective-permute-done((bf16[512,1024]{1,0:T(8,128)(2,1)S(1)}, bf16[512,1024]{1,0:T(8,128)(2,1)S(1)}, u32[]{:S(2)}, u32[]{:S(2)}) %collective-permute-start) | collective-permute-done | bytes 1048608 | tf_op jit(solution)/shard_map/ppermute | solution.py:39
  59.5 3.8 %fusion.27 = (bf16[1024,1,512]{2,1,0:T(2,128)(2,1)}, bf16[1024,1,512]{2,1,0:T(2,128)(2,1)S(1)}) fusion(bf16[1024,2,512]{2,1,0:T(2,128)(2,1)S(1)} %copy-done.1), kind=kLoop, calls=%fused_computation.54 | loop fusion | bytes 4194304 | tf_op jit(solution)/shard_map/slice | solution.py:104
  65.9 1.8 collective-permute-start.11
  68.5 2.1 %fusion.13 = f32[1024,512]{1,0:T(8,128)S(1)} fusion(bf16[1024,1024]{0,1:T(8,128)(2,1)} %copy-done.9, bf16[512,1024]{0,1:T(8,128)(2,1)S(1)} %bitcast.57), kind=kOutput, calls=%fused_computation.22 | convolution fusion | flops 536870912 | bytes 3670016 | tf_op jit(solution)/shard_map/dot_general | solution.py:11
  70.6 20.6 %collective-permute-done.11 = bf16[512,1024]{0,1:T(8,128)(2,1)} collective-permute-done((bf16[512,1024]{0,1:T(8,128)(2,1)S(1)}, bf16[512,1024]{0,1:T(8,128)(2,1)}, u32[]{:S(2)}, u32[]{:S(2)}) %collective-permute-start.11) | collective-permute-done | bytes 1048608 | tf_op jit(solution)/shard_map/ppermute | solution.py:39
  91.2 2.4 %fusion.5 = bf16[512,1024]{0,1:T(8,128)(2,1)S(1)} fusion(f32[1024,512]{1,0:T(8,128)S(1)} %fusion.13, bf16[512,1024]{0,1:T(8,128)(2,1)} %collective-permute-done.11, pred[]{:T(512)S(6)} %eq.20, bf16[1024,1024]{0,1:T(8,128)(2,1)S(1)} %copy-done.10, bf16[512,1024]{0,1:T(8,128)(2,1)S(1)} %bitcast.58), kind=kOutput, calls=%fused_computation.10 | convolution fusion | flops 542113792 | bytes 6816768 | tf_op jit(solution)/shard_map/dot_general | solution.py:11
  94.8 14.7 %collective-permute-done.12 = bf16[512,512]{0,1:T(8,128)(2,1)S(1)} collective-permute-done((bf16[512,512]{0,1:T(8,128)(2,1)}, bf16[512,512]{0,1:T(8,128)(2,1)S(1)}, u32[]{:S(2)}, u32[]{:S(2)}) %collective-permute-start.12) | collective-permute-done | bytes 524320 | tf_op jit(solution)/shard_map/ppermute | solution.py:39
  109.7 2.0 %collective-permute-start.14 = (bf16[512,512]{0,1:T(8,128)(2,1)S(1)}, bf16[512,512]{0,1:T(8,128)(2,1)S(1)}, u32[]{:S(2)}, u32[]{:S(2)}) collective-permute-start(bf16[512,512]{0,1:T(8,128)(2,1)S(1)} %slice_select_fusion), channel_id=1, source_target_pairs={{2,18},{18,2},{6,22},{22,6},{3,19},{19,3},{7,23},{23,7},{8,10},{10... | collective-permute-start | bytes 1572872 | tf_op jit(solution)/shard_map/ppermute | solution.py:39
  111.7 19.0 %collective-permute-done.5 = bf16[512,512]{0,1:T(8,128)(2,1)S(1)} collective-permute-done((bf16[512,512]{0,1:T(8,128)(2,1)S(1)}, bf16[512,512]{0,1:T(8,128)(2,1)S(1)}, u32[]{:S(2)}, u32[]{:S(2)}) %collective-permute-start.5) | collective-permute-done | bytes 524320 | tf_op jit(solution)/shard_map/ppermute | solution.py:39
  130.7 3.1 %collective-permute-start.13 = (bf16[512,512]{0,1:T(8,128)(2,1)S(1)}, bf16[512,512]{0,1:T(8,128)(2,1)S(1)}, u32[]{:S(2)}, u32[]{:S(2)}) collective-permute-start(bf16[512,512]{0,1:T(8,128)(2,1)S(1)} %slice_select_fusion), channel_id=1, source_target_pairs={{2,26},{26,2},{6,30},{30,6},{3,27},{27,3},{7,31},{31,7},{8,10},{10... | collective-permute-start | bytes 1572872 | tf_op jit(solution)/shard_map/ppermute | solution.py:39
  134.0 1.8 collective-permute-done.14
  135.8 8.6 %collective-permute-done.13 = bf16[512,512]{0,1:T(8,128)(2,1)S(1)} collective-permute-done((bf16[512,512]{0,1:T(8,128)(2,1)S(1)}, bf16[512,512]{0,1:T(8,128)(2,1)S(1)}, u32[]{:S(2)}, u32[]{:S(2)}) %collective-permute-start.13) | collective-permute-done | bytes 524320 | tf_op jit(solution)/shard_map/ppermute | solution.py:39
  144.5 2.5 %collective-permute-start.17 = (bf16[512,512]{0,1:T(8,128)(2,1)S(1)}, bf16[512,512]{0,1:T(8,128)(2,1)}, u32[]{:S(2)}, u32[]{:S(2)}) collective-permute-start(bf16[512,512]{0,1:T(8,128)(2,1)S(1)} %select_select_fusion), channel_id=1, source_target_pairs={{2,6},{6,2},{10,14},{14,10},{18,22},{22,18},{26,30},{30,26},{3,7},... | collective-permute-start | bytes 1572872 | tf_op jit(solution)/shard_map/ppermute | solution.py:39
  147.0 8.6 %collective-permute-done.7 = bf16[512,512]{0,1:T(8,128)(2,1)} collective-permute-done((bf16[512,512]{0,1:T(8,128)(2,1)S(1)}, bf16[512,512]{0,1:T(8,128)(2,1)}, u32[]{:S(2)}, u32[]{:S(2)}) %collective-permute-start.7) | collective-permute-done | bytes 524320 | tf_op jit(solution)/shard_map/ppermute | solution.py:39
  156.1 7.9 %collective-permute-done.17 = bf16[512,512]{0,1:T(8,128)(2,1)} collective-permute-done((bf16[512,512]{0,1:T(8,128)(2,1)S(1)}, bf16[512,512]{0,1:T(8,128)(2,1)}, u32[]{:S(2)}, u32[]{:S(2)}) %collective-permute-start.17) | collective-permute-done | bytes 524320 | tf_op jit(solution)/shard_map/ppermute | solution.py:39
  165.2 3.0 %fusion.4 = bf16[1024,1024]{0,1:T(8,128)(2,1)S(1)} fusion(bf16[1024,1,1024]{0,2,1:T(8,128)(2,1)S(1)} %copy-done.3, f32[1024]{0:T(1024)S(1)} %bitcast.61, pred[]{:T(512)S(6)} %gt.7, bf16[512,512]{0,1:T(8,128)(2,1)S(1)} %get-tuple-element.11, bf16[512,512]{0,1:T(8,128)(2,1)S(1)} %get-tuple-element.10, bf16[1024,1,512]{2,1,0:T(2,128)(2,1)} %copy-done.8), kind=kOutput, calls=%fused_computation.7 | convolution fusion | flops 1081081856 | bytes 6295553 | tf_op jit(solution)/shard_map/dot_general | solution.py:11
  171.8 2.6 %copy.18 = bf16[1024,1,1024]{2,0,1:T(8,128)(2,1)} copy(bf16[1024,1,1024]{0,2,1:T(8,128)(2,1)S(1)} %fusion.6) | data formatting | bytes 4194304
  174.3 1.4 pad_maximum_fusion
  175.7 2.4 %copy.19 = bf16[2,512,1024]{2,1,0:T(8,128)(2,1)} copy(bf16[2,512,1024]{1,2,0:T(8,128)(2,1)S(1)} %pad_maximum_fusion) | data formatting | bytes 4194304
  (65 shorter events, 13.4 us)
Async XLA Ops:
  7.8 28.5 %copy-start.2 = (bf16[1024,1,1024]{0,2,1:T(8,128)(2,1)S(1)}, bf16[1024,1,1024]{0,2,1:T(8,128)(2,1)}, u32[]{:S(2)}) copy-start(bf16[1024,1,1024]{0,2,1:T(8,128)(2,1)} %copy.12) | copy-start | bytes 6291460
  7.8 28.5 %copy-start.6 = (bf16[512,1024]{1,0:T(8,128)(2,1)S(1)}, bf16[512,1024]{1,0:T(8,128)(2,1)}, u32[]{:S(2)}) copy-start(bf16[512,1024]{1,0:T(8,128)(2,1)} %get-tuple-element.12) | copy-start | bytes 3145732
  9.3 27.0 %collective-permute-start.1 = (bf16[512,1024]{0,1:T(8,128)(2,1)S(1)}, bf16[512,1024]{0,1:T(8,128)(2,1)S(1)}, u32[]{:S(2)}, u32[]{:S(2)}) collective-permute-start(bf16[512,1024]{0,1:T(8,128)(2,1)S(1)} %broadcast_select_fusion), channel_id=1, source_target_pairs={{0,1},{1,0},{4,6},{6,4},{5,7},{7,5},{8,10},{10,8},{9,11},{11,9},{1... | collective-permute-start | bytes 3145736 | tf_op jit(solution)/shard_map/ppermute | solution.py:39
  12.4 45.6 %collective-permute-start = (bf16[512,1024]{1,0:T(8,128)(2,1)S(1)}, bf16[512,1024]{1,0:T(8,128)(2,1)S(1)}, u32[]{:S(2)}, u32[]{:S(2)}) collective-permute-start(bf16[512,1024]{1,0:T(8,128)(2,1)S(1)} %slice_bitcast_fusion.2), channel_id=1, source_target_pairs={{0,1},{1,0},{4,6},{6,4},{5,7},{7,5},{8,10},{10,8},{9,11},{11,9},{1... | collective-permute-start | bytes 3145736 | tf_op jit(solution)/shard_map/ppermute | solution.py:39
  37.1 21.8 %copy-start.11 = (f32[1024,2]{0,1:T(2,128)S(1)}, f32[1024,2]{0,1:T(2,128)}, u32[]{:S(2)}) copy-start(f32[1024,2]{0,1:T(2,128)} %param.6) | copy-start | bytes 24580
  37.1 22.3 %copy-start.1 = (bf16[1024,2,512]{2,1,0:T(2,128)(2,1)S(1)}, bf16[1024,2,512]{2,1,0:T(2,128)(2,1)}, u32[]{:S(2)}) copy-start(bf16[1024,2,512]{2,1,0:T(2,128)(2,1)} %param.5) | copy-start | bytes 6291460
  58.8 4.4 %collective-permute-start.9 = (bf16[512,1024]{0,1:T(8,128)(2,1)S(1)}, bf16[512,1024]{0,1:T(8,128)(2,1)S(1)}, u32[]{:S(2)}, u32[]{:S(2)}) collective-permute-start(bf16[512,1024]{0,1:T(8,128)(2,1)S(1)} %fusion.8), channel_id=1, source_target_pairs={{0,2},{2,0},{1,3},{3,1},{4,6},{6,4},{5,7},{7,5},{8,10},{10,8},{9,1... | collective-permute-start | bytes 3145736 | tf_op jit(solution)/shard_map/ppermute | solution.py:39
  58.9 5.7 %collective-permute-start.10 = (bf16[512,1024]{0,1:T(8,128)(2,1)S(1)}, bf16[512,1024]{0,1:T(8,128)(2,1)S(1)}, u32[]{:S(2)}, u32[]{:S(2)}) collective-permute-start(bf16[512,1024]{0,1:T(8,128)(2,1)S(1)} %collective-permute-done.1), channel_id=1, source_target_pairs={{0,2},{2,0},{1,3},{3,1},{4,6},{6,4},{5,7},{7,5},{8,10},{10,8},{9,1... | collective-permute-start | bytes 3145736 | tf_op jit(solution)/shard_map/ppermute | solution.py:39
  65.9 25.3 %collective-permute-start.11 = (bf16[512,1024]{0,1:T(8,128)(2,1)S(1)}, bf16[512,1024]{0,1:T(8,128)(2,1)}, u32[]{:S(2)}, u32[]{:S(2)}) collective-permute-start(bf16[512,1024]{0,1:T(8,128)(2,1)S(1)} %fusion.9), channel_id=1, source_target_pairs={{2,3},{3,2},{4,6},{6,4},{5,7},{7,5},{8,10},{10,8},{9,11},{11,9},{1... | collective-permute-start | bytes 3145736 | tf_op jit(solution)/shard_map/ppermute | solution.py:39
  68.5 22.6 %copy-start.10 = (bf16[1024,1024]{0,1:T(8,128)(2,1)S(1)}, bf16[1024,1024]{0,1:T(8,128)(2,1)}, u32[]{:S(2)}) copy-start(bf16[1024,1024]{0,1:T(8,128)(2,1)} %copy-done.9) | copy-start | bytes 6291460
  68.5 25.9 %collective-permute-start.2 = (bf16[512,512]{0,1:T(8,128)(2,1)}, bf16[512,512]{0,1:T(8,128)(2,1)}, u32[]{:S(2)}, u32[]{:S(2)}) collective-permute-start(bf16[512,512]{0,1:T(8,128)(2,1)} %slice.88), channel_id=1, source_target_pairs={{0,4},{4,0},{1,5},{5,1},{8,10},{10,8},{9,11},{11,9},{12,14},{14,12... | collective-permute-start | bytes 1572872 | tf_op jit(solution)/shard_map/ppermute | solution.py:39
  94.5 15.1 %collective-permute-start.12 = (bf16[512,512]{0,1:T(8,128)(2,1)}, bf16[512,512]{0,1:T(8,128)(2,1)S(1)}, u32[]{:S(2)}, u32[]{:S(2)}) collective-permute-start(bf16[512,512]{0,1:T(8,128)(2,1)} %slice.94), channel_id=1, source_target_pairs={{2,6},{6,2},{3,7},{7,3},{8,10},{10,8},{9,11},{11,9},{12,14},{14,12... | collective-permute-start | bytes 1572872 | tf_op jit(solution)/shard_map/ppermute | solution.py:39
  94.5 36.2 %collective-permute-start.5 = (bf16[512,512]{0,1:T(8,128)(2,1)S(1)}, bf16[512,512]{0,1:T(8,128)(2,1)S(1)}, u32[]{:S(2)}, u32[]{:S(2)}) collective-permute-start(bf16[512,512]{0,1:T(8,128)(2,1)S(1)} %slice_select_fusion.1), channel_id=1, source_target_pairs={{0,8},{8,0},{4,12},{12,4},{1,9},{9,1},{5,13},{13,5},{16,18},{18,16... | collective-permute-start | bytes 1572872 | tf_op jit(solution)/shard_map/ppermute | solution.py:39
  94.6 39.2 %collective-permute-start.4 = (bf16[512,512]{0,1:T(8,128)(2,1)S(1)}, bf16[512,512]{0,1:T(8,128)(2,1)S(1)}, u32[]{:S(2)}, u32[]{:S(2)}) collective-permute-start(bf16[512,512]{0,1:T(8,128)(2,1)S(1)} %slice_select_fusion.1), channel_id=1, source_target_pairs={{0,16},{16,0},{4,20},{20,4},{1,17},{17,1},{5,21},{21,5},{8,10},{10... | collective-permute-start | bytes 1572872 | tf_op jit(solution)/shard_map/ppermute | solution.py:39
  94.7 39.1 %collective-permute-start.3 = (bf16[512,512]{0,1:T(8,128)(2,1)S(1)}, bf16[512,512]{0,1:T(8,128)(2,1)}, u32[]{:S(2)}, u32[]{:S(2)}) collective-permute-start(bf16[512,512]{0,1:T(8,128)(2,1)S(1)} %slice_select_fusion.1), channel_id=1, source_target_pairs={{0,24},{24,0},{4,28},{28,4},{1,25},{25,1},{5,29},{29,5},{8,10},{10... | collective-permute-start | bytes 1572872 | tf_op jit(solution)/shard_map/ppermute | solution.py:39
  109.6 24.4 %collective-permute-start.15 = (bf16[512,512]{0,1:T(8,128)(2,1)S(1)}, bf16[512,512]{0,1:T(8,128)(2,1)S(1)}, u32[]{:S(2)}, u32[]{:S(2)}) collective-permute-start(bf16[512,512]{0,1:T(8,128)(2,1)S(1)} %slice_select_fusion), channel_id=1, source_target_pairs={{2,10},{10,2},{6,14},{14,6},{3,11},{11,3},{7,15},{15,7},{16,18},{1... | collective-permute-start | bytes 1572872 | tf_op jit(solution)/shard_map/ppermute | solution.py:39
  109.7 26.1 %collective-permute-start.14 = (bf16[512,512]{0,1:T(8,128)(2,1)S(1)}, bf16[512,512]{0,1:T(8,128)(2,1)S(1)}, u32[]{:S(2)}, u32[]{:S(2)}) collective-permute-start(bf16[512,512]{0,1:T(8,128)(2,1)S(1)} %slice_select_fusion), channel_id=1, source_target_pairs={{2,18},{18,2},{6,22},{22,6},{3,19},{19,3},{7,23},{23,7},{8,10},{10... | collective-permute-start | bytes 1572872 | tf_op jit(solution)/shard_map/ppermute | solution.py:39
  130.7 13.6 %collective-permute-start.13 = (bf16[512,512]{0,1:T(8,128)(2,1)S(1)}, bf16[512,512]{0,1:T(8,128)(2,1)S(1)}, u32[]{:S(2)}, u32[]{:S(2)}) collective-permute-start(bf16[512,512]{0,1:T(8,128)(2,1)S(1)} %slice_select_fusion), channel_id=1, source_target_pairs={{2,26},{26,2},{6,30},{30,6},{3,27},{27,3},{7,31},{31,7},{8,10},{10... | collective-permute-start | bytes 1572872 | tf_op jit(solution)/shard_map/ppermute | solution.py:39
  133.9 21.7 %collective-permute-start.7 = (bf16[512,512]{0,1:T(8,128)(2,1)S(1)}, bf16[512,512]{0,1:T(8,128)(2,1)}, u32[]{:S(2)}, u32[]{:S(2)}) collective-permute-start(bf16[512,512]{0,1:T(8,128)(2,1)S(1)} %select_select_fusion.1), channel_id=1, source_target_pairs={{0,4},{4,0},{8,12},{12,8},{16,20},{20,16},{24,28},{28,24},{1,5},{5... | collective-permute-start | bytes 1572872 | tf_op jit(solution)/shard_map/ppermute | solution.py:39
  144.5 19.5 %collective-permute-start.17 = (bf16[512,512]{0,1:T(8,128)(2,1)S(1)}, bf16[512,512]{0,1:T(8,128)(2,1)}, u32[]{:S(2)}, u32[]{:S(2)}) collective-permute-start(bf16[512,512]{0,1:T(8,128)(2,1)S(1)} %select_select_fusion), channel_id=1, source_target_pairs={{2,6},{6,2},{10,14},{14,10},{18,22},{22,18},{26,30},{30,26},{3,7},... | collective-permute-start | bytes 1572872 | tf_op jit(solution)/shard_map/ppermute | solution.py:39
  147.0 17.0 %collective-permute-start.6 = (bf16[512,512]{0,1:T(8,128)(2,1)S(1)}, bf16[512,512]{0,1:T(8,128)(2,1)}, u32[]{:S(2)}, u32[]{:S(2)}) collective-permute-start(bf16[512,512]{0,1:T(8,128)(2,1)S(1)} %select_select_fusion.1), channel_id=1, source_target_pairs={{0,2},{2,0},{1,3},{3,1},{4,6},{6,4},{5,7},{7,5},{8,10},{10,8},{9,1... | collective-permute-start | bytes 1572872 | tf_op jit(solution)/shard_map/ppermute | solution.py:39
  155.6 8.4 %collective-permute-start.8 = (bf16[512,512]{0,1:T(8,128)(2,1)}, bf16[512,512]{0,1:T(8,128)(2,1)}, u32[]{:S(2)}, u32[]{:S(2)}) collective-permute-start(bf16[512,512]{0,1:T(8,128)(2,1)} %collective-permute-done.7), channel_id=1, source_target_pairs={{0,2},{2,0},{1,3},{3,1},{4,6},{6,4},{5,7},{7,5},{8,10},{10,8},{9,1... | collective-permute-start | bytes 1572872 | tf_op jit(solution)/shard_map/ppermute | solution.py:39
  155.6 12.6 %collective-permute-start.16 = (bf16[512,512]{0,1:T(8,128)(2,1)S(1)}, bf16[512,512]{0,1:T(8,128)(2,1)S(1)}, u32[]{:S(2)}, u32[]{:S(2)}) collective-permute-start(bf16[512,512]{0,1:T(8,128)(2,1)S(1)} %select_select_fusion), channel_id=1, source_target_pairs={{0,2},{2,0},{1,3},{3,1},{4,6},{6,4},{5,7},{7,5},{8,10},{10,8},{9,1... | collective-permute-start | bytes 1572872 | tf_op jit(solution)/shard_map/ppermute | solution.py:39
  164.0 4.2 %collective-permute-start.18 = (bf16[512,512]{0,1:T(8,128)(2,1)}, bf16[512,512]{0,1:T(8,128)(2,1)S(1)}, u32[]{:S(2)}, u32[]{:S(2)}) collective-permute-start(bf16[512,512]{0,1:T(8,128)(2,1)} %collective-permute-done.17), channel_id=1, source_target_pairs={{0,2},{2,0},{1,3},{3,1},{4,6},{6,4},{5,7},{7,5},{8,10},{10,8},{9,1... | collective-permute-start | bytes 1572872 | tf_op jit(solution)/shard_map/ppermute | solution.py:39
  (7 other events, 37.5 us)

commit v2 on v1

v2 whole, which is shorter than its diff:
```python
import jax
import jax.numpy as jnp
from jax import lax
from jax.experimental import pallas as pl
from jax.experimental.pallas import tpu as pltpu
from jax.sharding import PartitionSpec as P

AXES = ("row", "col")
BF = jnp.bfloat16
F32 = jnp.float32
VMEM_BYTES = 40 * 1024 * 1024


def dot(a, b):
    return jnp.dot(a, b, preferred_element_type=F32)


def device(x, c, z, k):
    return ((z * 2 + x) * 2 + k) * 2 + c


PLACES = [(x, c, z, k) for z in range(4) for x in range(2) for k in range(2) for c in range(2)]


def paired(wanted, side):
    mate = {}

    def join(a, b):
        assert a not in mate and b not in mate and a != b
        mate[a], mate[b] = b, a

    def across(place, axis):
        x, c, z, k = place
        return (1 - x, c, z, k) if axis == "x" else (x, 1 - c, z, k)

    def core(place):
        x, c, z, k = place
        return (x, c, z, 1 - k)

    for a, b in wanted:
        join(a, b)
    for axis in (side, "y" if side == "x" else "x"):
        for place in [p for p in PLACES if p not in mate and core(p) in mate]:
            if place not in mate and across(place, axis) not in mate:
                join(place, across(place, axis))
    for place in PLACES:
        if place not in mate:
            join(place, core(place))
    return [(device(*a), device(*b)) for a, b in mate.items()]


def swap(value, wanted, side):
    return lax.ppermute(value, AXES, paired(wanted, side))


def core_swap(value):
    return swap(value, [((x, c, z, 0), (x, c, z, 1)) for x, c, z, k in PLACES if k == 0], "x")


def fan_out(parts, core, x, z, k):
    hop = swap(parts[1], [((0, c, 0, core), (1, c, 0, core)) for c in range(2)], "y")
    mine = jnp.where(x == 0, parts[0], hop)
    sent = [
        swap(mine, [((s, c, 0, core), (s, c, far, core)) for c in range(2) for s in range(2)], "x")
        for far in (1, 2, 3)
    ]
    for far in (1, 2, 3):
        mine = jnp.where(z == far, sent[far - 1], mine)
    other = swap(mine, [((0, c, far, core), (1, c, far, core)) for c in range(2) for far in range(4)], "y")
    mine = jnp.where(k == core, mine, core_swap(mine))
    other = jnp.where(k == core, other, core_swap(other))
    return mine, other


def call(kernel, grid, ins, outs, shapes, scalars, operands, aliases=None):
    return pl.pallas_call(
        kernel,
        grid_spec=pltpu.PrefetchScalarGridSpec(
            num_scalar_prefetch=1, grid=grid, in_specs=ins, out_specs=outs
        ),
        out_shape=shapes,
        input_output_aliases=aliases or {},
        compiler_params=pltpu.CompilerParams(vmem_limit_bytes=VMEM_BYTES),
    )(scalars, *operands)


def solve_first(flags, share, far_top, far_bottom, inverse, half):
    n = share.shape[1]
    tile = half // 2

    def kernel(flags, top, bottom, far_t, far_b, inv, out):
        fan_t = (top[...].astype(F32) + far_t[...].astype(F32)).astype(BF)
        fan_b = (bottom[...].astype(F32) + far_b[...].astype(F32)).astype(BF)
        fan_b = jnp.where(flags[1] == 0, bottom[...], fan_b)
        whole = dot(inv[0, :, :half], fan_t) + dot(inv[0, :, half:], fan_b)
        out[0] = whole.astype(BF)

    block = lambda which: pl.BlockSpec((half, tile), lambda j, f: (which, j))
    return call(
        kernel,
        (n // tile,),
        [block(0), block(1), block(0), block(0), pl.BlockSpec((1, half, n), lambda j, f: (0, 0, 0))],
        pl.BlockSpec((1, half, tile), lambda j, f: (j // 2, 0, j % 2)),
        jax.ShapeDtypeStruct((2, half, half), BF),
        flags,
        (share, share, far_top, far_bottom, inverse),
    )


def second_block(flags, share, scale, panel, solved, inverse_far, half):
    n = share.shape[1]
    tile = half // 2

    def kernel(flags, cur, scl, pan, sol, inv, after, message):
        term = dot(pan[...], sol[0])
        newer = (cur[...].astype(F32) - scl[...] * term).astype(BF)
        after[...] = newer

        @pl.when(flags[1] == 0)
        def _():
            message[...] = dot(inv[...], newer).astype(BF)

        @pl.when(flags[1] != 0)
        def _():
            message[...] = newer[:half]

    return call(
        kernel,
        (n // tile,),
        [
            pl.BlockSpec((n, tile), lambda j, f: (0, j)),
            pl.BlockSpec((n, 1), lambda j, f: (0, 0)),
            pl.BlockSpec((n, half), lambda j, f: (0, 0)),
            pl.BlockSpec((1, half, tile), lambda j, f: (j // 2, 0, j % 2)),
            pl.BlockSpec((half, n), lambda j, f: (0, 0)),
        ],
        [pl.BlockSpec((n, tile), lambda j, f: (0, j)), pl.BlockSpec((half, tile), lambda j, f: (0, j))],
        [jax.ShapeDtypeStruct((n, n), BF), jax.ShapeDtypeStruct((half, n), BF)],
        flags,
        (share, scale, panel, solved, inverse_far),
    )


def solve_second(flags, after, answer, inverse, half):
    n = after.shape[1]
    tile = half // 2

    def kernel(flags, cur, ans, inv, out):
        upper = flags[1] == 0
        got = ans[...].astype(F32)
        top = cur[:half]
        top = jnp.where(upper, (top.astype(F32) + got).astype(BF), top)
        whole = dot(inv[0, :, :half], top) + dot(inv[0, :, half:], cur[half:])
        out[0] = jnp.where(upper, whole, whole + got).astype(BF)

    return call(
        kernel,
        (n // tile,),
        [
            pl.BlockSpec((n, tile), lambda j, f: (0, j)),
            pl.BlockSpec((half, tile), lambda j, f: (0, j)),
            pl.BlockSpec((1, half, n), lambda j, f: (1, 0, 0)),
        ],
        pl.BlockSpec((1, half, tile), lambda j, f: (j // 2, 0, j % 2)),
        jax.ShapeDtypeStruct((2, half, half), BF),
        flags,
        (after, answer, inverse),
    )


def update_first(flags, share, scale, panel, mine, other, half):
    n = share.shape[1]
    tile = n // 4

    def kernel(flags, cur, scl, pan, a, b, out, solved):
        j, i = pl.program_id(0), pl.program_id(1)
        rows = half // 4

        def one(sol):
            newer = (cur[...].astype(F32) - scl[...] * dot(pan[...], sol[...])).astype(BF)
            out[...] = jnp.where(flags[0] > 0, newer, cur[...])
            solved[0] = sol[pl.ds(pl.multiple_of(i * rows, rows), rows), :]

        pl.when(j == flags[2])(lambda: one(a))
        pl.when(j != flags[2])(lambda: one(b))

    whole = pl.BlockSpec((half, half), lambda j, i, f: (0, 0))
    return call(
        kernel,
        (2, 4),
        [
            pl.BlockSpec((tile, half), lambda j, i, f: (i, j)),
            pl.BlockSpec((tile, 1), lambda j, i, f: (i, 0)),
            pl.BlockSpec((tile, half), lambda j, i, f: (i, 0)),
            whole,
            whole,
        ],
        [
            pl.BlockSpec((tile, half), lambda j, i, f: (i, j)),
            pl.BlockSpec((1, half // 4, half), lambda j, i, f: (0, i, j)),
        ],
        [jax.ShapeDtypeStruct((n, n), BF), jax.ShapeDtypeStruct((2, half, n), BF)],
        flags,
        (share, scale, panel, mine, other),
    )


def update_half(flags, current, solved, scale, panel, part, half):
    n = current.shape[1]
    tile = n // 4

    def kernel(flags, cur, _, scl, pan, sol, out, solved):
        rows = half // 4
        newer = (cur[...].astype(F32) - scl[...] * dot(pan[...], sol[...])).astype(BF)
        out[...] = jnp.where(flags[0] > 1, newer, cur[...])
        start = pl.multiple_of(pl.program_id(0) * rows, rows)
        solved[0] = sol[pl.ds(start, rows), :]

    return call(
        kernel,
        (4,),
        [
            pl.BlockSpec((tile, half), lambda i, f: (i, f[2])),
            pl.BlockSpec(memory_space=pl.ANY),
            pl.BlockSpec((tile, 1), lambda i, f: (i, 0)),
            pl.BlockSpec((tile, half), lambda i, f: (i, 0)),
            pl.BlockSpec((half, half), lambda i, f: (0, 0)),
        ],
        [
            pl.BlockSpec((tile, half), lambda i, f: (i, f[2])),
            pl.BlockSpec((1, half // 4, half), lambda i, f: (1, i, f[2])),
        ],
        [jax.ShapeDtypeStruct((n, n), BF), jax.ShapeDtypeStruct((2, half, n), BF)],
        flags,
        (current, solved, scale, panel, part),
        {1: 0, 2: 1},
    )


def body(pending, panel, panel_scale, inverse_blocks):
    row, c = lax.axis_index("row"), lax.axis_index("col")
    z, x, k = row // 4, (row // 2) % 2, row % 2
    half = inverse_blocks.shape[1]
    flags = jnp.stack([row, c, x]).astype(jnp.int32)
    flipped = jnp.stack([row, c, 1 - x]).astype(jnp.int32)
    share = pending[:, 0, :]
    roots = [((0, 0, 0, 0), (0, 1, 0, 0))]
    seconds = [((0, 0, 0, 1), (0, 1, 0, 1))]

    far_top = swap(share[:half], roots, "x")
    far_bottom = swap(jnp.where(c == 0, share[half:], inverse_blocks[1]), roots, "x")
    panel0, panel1, scale0, scale1, far_top = lax.optimization_barrier(
        (panel[:, 0, :], panel[:, 1, :], panel_scale[:, 0:1], panel_scale[:, 1:2], far_top)
    )
    first = solve_first(flags, share, far_top, far_bottom, inverse_blocks, half)
    first_here = core_swap(first)
    inverse_far = core_swap(far_bottom)
    after, message = second_block(flags, share, scale0, panel0, first_here, inverse_far, half)
    answer = swap(message, seconds, "x")
    second = solve_second(flags, after, answer, inverse_blocks, half)

    mine0, other0 = fan_out(first, 0, x, z, k)
    current, solved = update_first(flags, share, scale0, panel0, mine0, other0, half)
    mine1, other1 = fan_out(second, 1, x, z, k)
    current, solved = update_half(flags, current, solved, scale1, panel1, mine1, half)
    current, solved = update_half(flipped, current, solved, scale1, panel1, other1, half)
    return current[:, None, :], solved


def body_any(pending, panel, panel_scale, inverse_blocks):
    row = lax.axis_index("row")
    current = pending[:, 0, :]
    solved = []
    for k in range(2):
        fan = lax.psum(current, "col")
        local = dot(inverse_blocks[k], fan).astype(BF)
        arrived = lax.psum(jnp.where(row == k, local, jnp.zeros_like(local)), "row")
        solved.append(arrived)
        term = dot(panel[:, k, :], arrived)
        newer = (current.astype(F32) - panel_scale[:, k : k + 1] * term).astype(BF)
        current = jnp.where(row > k, newer, current)
    return current[:, None, :], jnp.stack(solved)


def solution(mesh):
    placed = (P("row", "col", None), P("row", None, "col"), P("row", None), P(None, "col", None))
    small = mesh.shape["row"] == 16 and mesh.shape["col"] == 2
    return jax.shard_map(
        body if small else body_any,
        mesh=mesh,
        in_specs=placed,
        out_specs=(P("row", "col", None), P(None, "col", None)),
        check_vma=False,
    )
```

time: 180 us -> 143 us (0.79)
  waiting for transfers between devices: 126 us -> 76.2 us
  Pallas kernels: 0 us -> 27 us
  matrix products: 13 us -> 0 us
  local copies, waits for them, and re-layouts: 18.6 us -> 13.4 us
  other arithmetic: 5.64 us -> 10.7 us
  starting transfers between devices: 14.3 us -> 12.3 us
    ppermute x19, waiting for transfers between devices: 126 us -> 76.2 us  [swap(): return lax.ppermute(value, AXES, paired(wanted, side))]
    pallas_call x0 -> x6, Pallas kernels: none -> 27 us  [call(): pl.pallas_call(kernel, grid_spec=pltpu.PrefetchScalarGridSpec(num_scalar_...]
    dot_general x8 -> x0, matrix products: 13 us -> none  [dot(): return jnp.dot(a, b, preferred_element_type=jnp.float32)]
    unnamed x28 -> x20, local copies, waits for them, and re-layouts: 10.4 us -> 1.02 us
    select_n x5 -> x7, other arithmetic: 2.93 us -> 7.67 us  [the longest x2 2.99 us: fan_out(): mine = jnp.where(x == 0, parts[0], hop)]
    select_n x2, other arithmetic: 0.19 us -> 2.84 us  [fan_out(): mine = jnp.where(z == far, sent[far - 1], mine)]
    another operation x2, other arithmetic: 2.52 us -> 0.15 us  [the longest x1 0.08 us: body(): flags = jnp.stack([row, c, x]).astype(jnp.int32)]
    optimization_barrier x0 -> x2, local copies, waits for them, and re-layouts: none -> 2.06 us  [body(): lax.optimization_barrier((panel[:, 0, :], panel[:, 1, :], panel_scale[:,...]
  transfers between devices with their start and end apart: 19 -> 19, of which waited for: 9 -> 10; matrix products, arithmetic and copies ran while one was open for 9% -> 15% of each run, Pallas kernels for 0% -> 12%
where the time goes in v2:
time: 143 us; the launch traced here: 140 us
  waiting for transfers between devices  76.2 us (53%)
  Pallas kernels  27 us (19%)
  local copies, waits for them, and re-layouts  13.4 us (9%)
  starting transfers between devices  12.3 us (9%)
  other arithmetic  10.7 us (7%)
    ppermute x19, waiting for transfers between devices, swap(): return lax.ppermute(value, AXES, paired(wanted, side))  76.2 us
    pallas_call x6, Pallas kernels, call(): pl.pallas_call(kernel, grid_spec=pltpu.PrefetchScalarGridSpec(num_scalar_...  27 us
    ppermute x19, starting transfers between devices, swap(): return lax.ppermute(value, AXES, paired(wanted, side))  12.3 us
    slice x1, local copies, waits for them, and re-layouts, body(): panel[:, 1, :]  5.63 us
    select_n x2, other arithmetic, fan_out(): mine = jnp.where(x == 0, parts[0], hop)  2.99 us
  transfers between devices with their start and end apart: 19, of which 10 were waited for; matrix products, arithmetic and copies ran while one was open for 15% of the time, Pallas kernels for 12%

profile of v2, /device:TPU:0, one launch (start us, length us, event | category | flops | bytes accessed | tf_op | source)
XLA Modules:
  0.0 140.5 jit_solution(4427995195307143150)
XLA Ops:
  0.6 2.4 %slice_bitcast_fusion = bf16[512,1024]{1,0:T(8,128)(2,1)} fusion(bf16[1024,1,1024]{2,0,1:T(8,128)(2,1)} %param.4), kind=kLoop, calls=%fused_computation.3 | loop fusion | bytes 2097152 | tf_op jit(solution)/shard_map/slice | solution.py:250
  3.1 3.0 %collective-permute-start = (bf16[512,1024]{1,0:T(8,128)(2,1)}, bf16[512,1024]{1,0:T(8,128)(2,1)}, u32[]{:S(2)}, u32[]{:S(2)}) collective-permute-start(bf16[512,1024]{1,0:T(8,128)(2,1)} %slice_bitcast_fusion), channel_id=1, source_target_pairs={{0,1},{1,0},{2,6},{6,2},{3,7},{7,3},{4,5},{5,4},{8,10},{10,8},{9,1... | collective-permute-start | bytes 3145736 | tf_op jit(solution)/shard_map/ppermute | solution.py:53
  6.0 2.3 %bitcast_select_fusion = bf16[512,1024]{1,0:T(8,128)(2,1)} fusion(bf16[2,512,1024]{2,1,0:T(8,128)(2,1)} %inv.3, bf16[1024,1,1024]{2,0,1:T(8,128)(2,1)S(1)} %copy-done, pred[]{:T(512)S(6)} %eq.33), kind=kLoop, calls=%fused_computation.2 | loop fusion | flops 524288 | bytes 3145729 | tf_op jit(solution)/shard_map/jit(_where)/select_n | solution.py:251
  10.5 5.6 %fusion.2 = (bf16[1024,1,512]{2,1,0:T(2,128)(2,1)S(1)}, bf16[1024,1,512]{2,1,0:T(2,128)(2,1)S(1)}) fusion(bf16[1024,2,512]{2,1,0:T(2,128)(2,1)} %param.5), kind=kLoop, calls=%fused_computation.19 | loop fusion | bytes 4194304 | tf_op jit(solution)/shard_map/slice | solution.py:253
  16.8 2.3 %collective-permute-done.far_t = bf16[512,1024]{1,0:T(8,128)(2,1)} collective-permute-done((bf16[512,1024]{1,0:T(8,128)(2,1)}, bf16[512,1024]{1,0:T(8,128)(2,1)}, u32[]{:S(2)}, u32[]{:S(2)}) %collective-permute-start) | collective-permute-done | bytes 1048608 | tf_op jit(solution)/shard_map/ppermute | solution.py:53
  19.1 11.2 %collective-permute-done.1.far_b = bf16[512,1024]{1,0:T(8,128)(2,1)} collective-permute-done((bf16[512,1024]{1,0:T(8,128)(2,1)}, bf16[512,1024]{1,0:T(8,128)(2,1)}, u32[]{:S(2)}, u32[]{:S(2)}) %collective-permute-start.1) | collective-permute-done | bytes 1048608 | tf_op jit(solution)/shard_map/ppermute | solution.py:53
  30.4 4.5 %shard_map.59 = bf16[2,512,512]{2,1,0:T(8,128)(2,1)S(1)} custom-call(s32[3]{0:T(128)S(1)} %pad_add_fusion.2.flags, bf16[1024,1024]{1,0:T(8,128)(2,1)S(1)} %bitcast.28, bf16[1024,1024]{1,0:T(8,128)(2,1)S(1)} %bitcast.29, bf16[512,1024]{1,0:T(8,128)(2,1)} %collective-permute-done.far_t, bf16[512,1024]{1,0:T(8,128)(2,1)} %collective-permute-done.1.far_b, ...), custom_call_target="tpu_custom_call" | custom-call | tf_op jit(solution)/shard_map/pallas_call | solution.py:76
  35.5 2.3 %collective-permute-done.9.sol = bf16[2,512,512]{2,1,0:T(8,128)(2,1)S(1)} collective-permute-done((bf16[2,512,512]{2,1,0:T(8,128)(2,1)S(1)}, bf16[2,512,512]{2,1,0:T(8,128)(2,1)S(1)}, u32[]{:S(2)}, u32[]{:S(2)}) %collective-permute-start.9) | collective-permute-done | bytes 1048608 | tf_op jit(solution)/shard_map/ppermute | solution.py:53
  37.8 5.0 %shard_map.61 = (bf16[1024,1024]{1,0:T(8,128)(2,1)S(1)}, bf16[512,1024]{1,0:T(8,128)(2,1)S(1)}) custom-call(s32[3]{0:T(128)S(1)} %pad_add_fusion.2.flags, bf16[1024,1024]{1,0:T(8,128)(2,1)S(1)} %bitcast.30, f32[1024,1]{1,0:T(8,128)S(1)} %copy-done.5, bf16[1024,512]{1,0:T(8,128)(2,1)S(1)} %get-tuple-element.16.pan, ...), custom_call_target="tpu_custom_call" | custom-call | tf_op jit(solution)/shard_map/pallas_call | solution.py:76
  42.8 2.1 %collective-permute-start.11 = (bf16[512,1024]{1,0:T(8,128)(2,1)S(1)}, bf16[512,1024]{1,0:T(8,128)(2,1)S(1)}, u32[]{:S(2)}, u32[]{:S(2)}) collective-permute-start(bf16[512,1024]{1,0:T(8,128)(2,1)S(1)} %get-tuple-element.23), channel_id=1, source_target_pairs={{2,3},{3,2},{0,4},{4,0},{1,5},{5,1},{6,7},{7,6},{8,10},{10,8},{9,1... | collective-permute-start | bytes 3145736 | tf_op jit(solution)/shard_map/ppermute | solution.py:53
  45.7 11.9 %collective-permute-done.11.ans = bf16[512,1024]{1,0:T(8,128)(2,1)S(1)} collective-permute-done((bf16[512,1024]{1,0:T(8,128)(2,1)S(1)}, bf16[512,1024]{1,0:T(8,128)(2,1)S(1)}, u32[]{:S(2)}, u32[]{:S(2)}) %collective-permute-start.11) | collective-permute-done | bytes 1048608 | tf_op jit(solution)/shard_map/ppermute | solution.py:53
  57.7 3.0 %shard_map.62 = bf16[2,512,512]{2,1,0:T(8,128)(2,1)S(1)} custom-call(s32[3]{0:T(128)S(1)} %pad_add_fusion.2.flags, bf16[1024,1024]{1,0:T(8,128)(2,1)S(1)} %get-tuple-element.22.cur, bf16[512,1024]{1,0:T(8,128)(2,1)S(1)} %collective-permute-done.11.ans, bf16[2,512,1024]{2,1,0:T(8,128)(2,1)S(1)} %copy-done.1), custom_call_target="tpu_custom_call" | custom-call | tf_op jit(solution)/shard_map/pallas_call | solution.py:76
  63.4 1.9 %fusion.1 = bf16[512,512]{1,0:T(8,128)(2,1)} fusion(bf16[512,512]{1,0:T(8,128)(2,1)} %collective-permute-done.2, bf16[2,512,512]{2,1,0:T(8,128)(2,1)} %copy-done.8, pred[]{:T(512)S(6)} %eq.32), kind=kLoop, calls=%fused_computation.9 | loop fusion | flops 262144 | bytes 1572865 | tf_op jit(solution)/shard_map/jit(_where)/select_n | solution.py:62
  65.3 6.7 %collective-permute-done.12 = bf16[512,512]{1,0:T(8,128)(2,1)} collective-permute-done((bf16[512,512]{1,0:T(8,128)(2,1)}, bf16[512,512]{1,0:T(8,128)(2,1)}, u32[]{:S(2)}, u32[]{:S(2)}) %collective-permute-start.12) | collective-permute-done | bytes 524320 | tf_op jit(solution)/shard_map/ppermute | solution.py:53
  73.1 2.2 %collective-permute-start.15 = (bf16[512,512]{1,0:T(8,128)(2,1)S(1)}, bf16[512,512]{1,0:T(8,128)(2,1)S(1)}, u32[]{:S(2)}, u32[]{:S(2)}) collective-permute-start(bf16[512,512]{1,0:T(8,128)(2,1)S(1)} %fusion), channel_id=1, source_target_pairs={{2,10},{10,2},{6,14},{14,6},{3,11},{11,3},{7,15},{15,7},{0,4},{4,0... | collective-permute-start | bytes 1572872 | tf_op jit(solution)/shard_map/ppermute | solution.py:53
  75.4 26.4 %collective-permute-done.5 = bf16[512,512]{1,0:T(8,128)(2,1)} collective-permute-done((bf16[512,512]{1,0:T(8,128)(2,1)}, bf16[512,512]{1,0:T(8,128)(2,1)}, u32[]{:S(2)}, u32[]{:S(2)}) %collective-permute-start.5) | collective-permute-done | bytes 524320 | tf_op jit(solution)/shard_map/ppermute | solution.py:53
  101.8 2.2 %collective-permute-start.13 = (bf16[512,512]{1,0:T(8,128)(2,1)S(1)}, bf16[512,512]{1,0:T(8,128)(2,1)S(1)}, u32[]{:S(2)}, u32[]{:S(2)}) collective-permute-start(bf16[512,512]{1,0:T(8,128)(2,1)S(1)} %fusion), channel_id=1, source_target_pairs={{2,26},{26,2},{6,30},{30,6},{3,27},{27,3},{7,31},{31,7},{0,4},{4,0... | collective-permute-start | bytes 1572872 | tf_op jit(solution)/shard_map/ppermute | solution.py:53
  104.0 1.9 %select_select_fusion.1 = bf16[512,512]{1,0:T(8,128)(2,1)} fusion(bf16[512,512]{1,0:T(8,128)(2,1)} %collective-permute-done.3, bf16[512,512]{1,0:T(8,128)(2,1)} %collective-permute-done.4, bf16[512,512]{1,0:T(8,128)(2,1)} %collective-permute-done.5, bf16[512,512]{1,0:T(8,128)(2,1)} %fusion.1, pred[]{:T(512)S(6)} %eq.35, pred[]{:T(512)S(6)} %eq.34, pred[]{:T(512)S(6)} %eq.31), kind=kLoop, calls=%fused_computation.11 | loop fusion | flops 786432 | bytes 2621443 | tf_op jit(solution)/shard_map/jit(_where)/select_n | solution.py:68
  105.9 5.8 %collective-permute-done.13 = bf16[512,512]{1,0:T(8,128)(2,1)S(1)} collective-permute-done((bf16[512,512]{1,0:T(8,128)(2,1)S(1)}, bf16[512,512]{1,0:T(8,128)(2,1)S(1)}, u32[]{:S(2)}, u32[]{:S(2)}) %collective-permute-start.13) | collective-permute-done | bytes 524320 | tf_op jit(solution)/shard_map/ppermute | solution.py:53
  112.6 1.2 collective-permute-start.17
  113.8 8.6 %collective-permute-done.7 = bf16[512,512]{1,0:T(8,128)(2,1)} collective-permute-done((bf16[512,512]{1,0:T(8,128)(2,1)}, bf16[512,512]{1,0:T(8,128)(2,1)}, u32[]{:S(2)}, u32[]{:S(2)}) %collective-permute-start.7) | collective-permute-done | bytes 524320 | tf_op jit(solution)/shard_map/ppermute | solution.py:53
  125.8 5.4 %shard_map.60 = (bf16[1024,1024]{1,0:T(8,128)(2,1)}, bf16[2,512,1024]{2,1,0:T(8,128)(2,1)}) custom-call(s32[3]{0:T(128)S(1)} %pad_add_fusion.2.flags, bf16[1024,1024]{1,0:T(8,128)(2,1)S(1)} %bitcast.31, f32[1024,1]{1,0:T(8,128)S(1)} %copy-done.6, bf16[1024,512]{1,0:T(8,128)(2,1)S(1)} %copy-done.3, bf16[512,512]{1,0:T(8,128)(2,1)S(1)} %broadcast_select_fusion.3.a, ...), custom_call_target="tpu_custom_call" | custom-call | tf_op jit(solution)/shard_map/pallas_call | solution.py:76
  131.3 4.5 %shard_map.63 = (bf16[1024,1024]{1,0:T(8,128)(2,1)}, bf16[2,512,1024]{2,1,0:T(8,128)(2,1)}) custom-call(s32[3]{0:T(128)S(1)} %pad_add_fusion.2.flags, bf16[1024,1024]{1,0:T(8,128)(2,1)} %get-tuple-element.18.cur, bf16[2,512,1024]{2,1,0:T(8,128)(2,1)} %get-tuple-element.19._, f32[1024,1]{1,0:T(8,128)S(1)} %copy-done.4, ...), custom_call_target="tpu_custom_call", output_to_operand_aliasing={{0}: (1, {}), {1}: (2, {})} | custom-call | tf_op jit(solution)/shard_map/pallas_call | solution.py:76
  135.9 4.5 %shard_map.64 = (bf16[1024,1024]{1,0:T(8,128)(2,1)}, bf16[2,512,1024]{2,1,0:T(8,128)(2,1)}) custom-call(s32[3]{0:T(128)S(1)} %pad_add_fusion.flags, bf16[1024,1024]{1,0:T(8,128)(2,1)} %get-tuple-element.24.cur, bf16[2,512,1024]{2,1,0:T(8,128)(2,1)} %get-tuple-element.25._, f32[1024,1]{1,0:T(8,128)S(1)} %copy-done.4, ...), custom_call_target="tpu_custom_call", output_to_operand_aliasing={{0}: (1, {}), {1}: (2, {})} | custom-call | tf_op jit(solution)/shard_map/pallas_call | solution.py:76
  (59 shorter events, 12.5 us)
Async XLA Ops:
  3.1 16.1 %collective-permute-start = (bf16[512,1024]{1,0:T(8,128)(2,1)}, bf16[512,1024]{1,0:T(8,128)(2,1)}, u32[]{:S(2)}, u32[]{:S(2)}) collective-permute-start(bf16[512,1024]{1,0:T(8,128)(2,1)} %slice_bitcast_fusion), channel_id=1, source_target_pairs={{0,1},{1,0},{2,6},{6,2},{3,7},{7,3},{4,5},{5,4},{8,10},{10,8},{9,1... | collective-permute-start | bytes 3145736 | tf_op jit(solution)/shard_map/ppermute | solution.py:53
  8.3 22.0 %collective-permute-start.1 = (bf16[512,1024]{1,0:T(8,128)(2,1)}, bf16[512,1024]{1,0:T(8,128)(2,1)}, u32[]{:S(2)}, u32[]{:S(2)}) collective-permute-start(bf16[512,1024]{1,0:T(8,128)(2,1)} %bitcast_select_fusion), channel_id=1, source_target_pairs={{0,1},{1,0},{2,6},{6,2},{3,7},{7,3},{4,5},{5,4},{8,10},{10,8},{9,1... | collective-permute-start | bytes 3145736 | tf_op jit(solution)/shard_map/ppermute | solution.py:53
  16.1 14.2 %copy-start.1 = (bf16[2,512,1024]{2,1,0:T(8,128)(2,1)S(1)}, bf16[2,512,1024]{2,1,0:T(8,128)(2,1)}, u32[]{:S(2)}) copy-start(bf16[2,512,1024]{2,1,0:T(8,128)(2,1)} %inv.3) | copy-start | bytes 6291460
  16.8 21.0 %copy-start.2 = (bf16[1024,512]{1,0:T(8,128)(2,1)}, bf16[1024,512]{1,0:T(8,128)(2,1)S(1)}, u32[]{:S(2)}) copy-start(bf16[1024,512]{1,0:T(8,128)(2,1)S(1)} %get-tuple-element.16.pan) | copy-start | bytes 3145732
  30.3 5.1 %collective-permute-start.10 = (bf16[512,1024]{1,0:T(8,128)(2,1)}, bf16[512,1024]{1,0:T(8,128)(2,1)S(1)}, u32[]{:S(2)}, u32[]{:S(2)}) collective-permute-start(bf16[512,1024]{1,0:T(8,128)(2,1)} %collective-permute-done.1.far_b), channel_id=1, source_target_pairs={{0,2},{2,0},{1,3},{3,1},{4,6},{6,4},{5,7},{7,5},{8,10},{10,8},{9,1... | collective-permute-start | bytes 3145736 | tf_op jit(solution)/shard_map/ppermute | solution.py:53
  30.4 7.4 %copy-start.5 = (f32[1024,1]{1,0:T(8,128)S(1)}, f32[1024,1]{1,0:T(8,128)}, u32[]{:S(2)}) copy-start(f32[1024,1]{1,0:T(8,128)} %copy.16.scl) | copy-start | bytes 12292
  34.9 10.0 %copy-start.8 = (bf16[2,512,512]{2,1,0:T(8,128)(2,1)}, bf16[2,512,512]{2,1,0:T(8,128)(2,1)S(1)}, u32[]{:S(2)}) copy-start(bf16[2,512,512]{2,1,0:T(8,128)(2,1)S(1)} %shard_map.59) | copy-start | bytes 3145732
  34.9 2.8 %collective-permute-start.9 = (bf16[2,512,512]{2,1,0:T(8,128)(2,1)S(1)}, bf16[2,512,512]{2,1,0:T(8,128)(2,1)S(1)}, u32[]{:S(2)}, u32[]{:S(2)}) collective-permute-start(bf16[2,512,512]{2,1,0:T(8,128)(2,1)S(1)} %shard_map.59), channel_id=1, source_target_pairs={{0,2},{2,0},{1,3},{3,1},{4,6},{6,4},{5,7},{7,5},{8,10},{10,8},{9,1... | collective-permute-start | bytes 3145736 | tf_op jit(solution)/shard_map/ppermute | solution.py:53
  42.8 14.9 %collective-permute-start.11 = (bf16[512,1024]{1,0:T(8,128)(2,1)S(1)}, bf16[512,1024]{1,0:T(8,128)(2,1)S(1)}, u32[]{:S(2)}, u32[]{:S(2)}) collective-permute-start(bf16[512,1024]{1,0:T(8,128)(2,1)S(1)} %get-tuple-element.23), channel_id=1, source_target_pairs={{2,3},{3,2},{0,4},{4,0},{1,5},{5,1},{6,7},{7,6},{8,10},{10,8},{9,1... | collective-permute-start | bytes 3145736 | tf_op jit(solution)/shard_map/ppermute | solution.py:53
  45.7 17.7 %collective-permute-start.2 = (bf16[512,512]{1,0:T(8,128)(2,1)}, bf16[512,512]{1,0:T(8,128)(2,1)}, u32[]{:S(2)}, u32[]{:S(2)}) collective-permute-start(bf16[512,512]{1,0:T(8,128)(2,1)} %slice_bitcast_fusion.3), channel_id=1, source_target_pairs={{0,4},{4,0},{1,5},{5,1},{2,3},{3,2},{6,7},{7,6},{8,10},{10,8},{9,1... | collective-permute-start | bytes 1572872 | tf_op jit(solution)/shard_map/ppermute | solution.py:53
  62.5 9.5 %collective-permute-start.12 = (bf16[512,512]{1,0:T(8,128)(2,1)}, bf16[512,512]{1,0:T(8,128)(2,1)}, u32[]{:S(2)}, u32[]{:S(2)}) collective-permute-start(bf16[512,512]{1,0:T(8,128)(2,1)} %slice_bitcast_fusion.1), channel_id=1, source_target_pairs={{2,6},{6,2},{3,7},{7,3},{0,1},{1,0},{4,5},{5,4},{8,10},{10,8},{9,1... | collective-permute-start | bytes 1572872 | tf_op jit(solution)/shard_map/ppermute | solution.py:53
  65.3 36.5 %collective-permute-start.5 = (bf16[512,512]{1,0:T(8,128)(2,1)}, bf16[512,512]{1,0:T(8,128)(2,1)}, u32[]{:S(2)}, u32[]{:S(2)}) collective-permute-start(bf16[512,512]{1,0:T(8,128)(2,1)} %fusion.1), channel_id=1, source_target_pairs={{0,8},{8,0},{4,12},{12,4},{1,9},{9,1},{5,13},{13,5},{2,6},{6,2},{3... | collective-permute-start | bytes 1572872 | tf_op jit(solution)/shard_map/ppermute | solution.py:53
  65.3 38.7 %collective-permute-start.4 = (bf16[512,512]{1,0:T(8,128)(2,1)}, bf16[512,512]{1,0:T(8,128)(2,1)}, u32[]{:S(2)}, u32[]{:S(2)}) collective-permute-start(bf16[512,512]{1,0:T(8,128)(2,1)} %fusion.1), channel_id=1, source_target_pairs={{0,16},{16,0},{4,20},{20,4},{1,17},{17,1},{5,21},{21,5},{2,6},{6,2... | collective-permute-start | bytes 1572872 | tf_op jit(solution)/shard_map/ppermute | solution.py:53
  65.3 38.7 %collective-permute-start.3 = (bf16[512,512]{1,0:T(8,128)(2,1)}, bf16[512,512]{1,0:T(8,128)(2,1)}, u32[]{:S(2)}, u32[]{:S(2)}) collective-permute-start(bf16[512,512]{1,0:T(8,128)(2,1)} %fusion.1), channel_id=1, source_target_pairs={{0,24},{24,0},{4,28},{28,4},{1,25},{25,1},{5,29},{29,5},{2,6},{6,2... | collective-permute-start | bytes 1572872 | tf_op jit(solution)/shard_map/ppermute | solution.py:53
  73.1 32.8 %collective-permute-start.15 = (bf16[512,512]{1,0:T(8,128)(2,1)S(1)}, bf16[512,512]{1,0:T(8,128)(2,1)S(1)}, u32[]{:S(2)}, u32[]{:S(2)}) collective-permute-start(bf16[512,512]{1,0:T(8,128)(2,1)S(1)} %fusion), channel_id=1, source_target_pairs={{2,10},{10,2},{6,14},{14,6},{3,11},{11,3},{7,15},{15,7},{0,4},{4,0... | collective-permute-start | bytes 1572872 | tf_op jit(solution)/shard_map/ppermute | solution.py:53
  75.3 30.6 %collective-permute-start.14 = (bf16[512,512]{1,0:T(8,128)(2,1)S(1)}, bf16[512,512]{1,0:T(8,128)(2,1)S(1)}, u32[]{:S(2)}, u32[]{:S(2)}) collective-permute-start(bf16[512,512]{1,0:T(8,128)(2,1)S(1)} %fusion), channel_id=1, source_target_pairs={{2,18},{18,2},{6,22},{22,6},{3,19},{19,3},{7,23},{23,7},{0,4},{4,0... | collective-permute-start | bytes 1572872 | tf_op jit(solution)/shard_map/ppermute | solution.py:53
  101.8 9.9 %collective-permute-start.13 = (bf16[512,512]{1,0:T(8,128)(2,1)S(1)}, bf16[512,512]{1,0:T(8,128)(2,1)S(1)}, u32[]{:S(2)}, u32[]{:S(2)}) collective-permute-start(bf16[512,512]{1,0:T(8,128)(2,1)S(1)} %fusion), channel_id=1, source_target_pairs={{2,26},{26,2},{6,30},{30,6},{3,27},{27,3},{7,31},{31,7},{0,4},{4,0... | collective-permute-start | bytes 1572872 | tf_op jit(solution)/shard_map/ppermute | solution.py:53
  105.9 16.5 %collective-permute-start.7 = (bf16[512,512]{1,0:T(8,128)(2,1)}, bf16[512,512]{1,0:T(8,128)(2,1)}, u32[]{:S(2)}, u32[]{:S(2)}) collective-permute-start(bf16[512,512]{1,0:T(8,128)(2,1)} %select_select_fusion.1), channel_id=1, source_target_pairs={{0,4},{4,0},{8,12},{12,8},{16,20},{20,16},{24,28},{28,24},{1,5},{5... | collective-permute-start | bytes 1572872 | tf_op jit(solution)/shard_map/ppermute | solution.py:53
  105.9 17.1 %collective-permute-start.6 = (bf16[512,512]{1,0:T(8,128)(2,1)}, bf16[512,512]{1,0:T(8,128)(2,1)}, u32[]{:S(2)}, u32[]{:S(2)}) collective-permute-start(bf16[512,512]{1,0:T(8,128)(2,1)} %select_select_fusion.1), channel_id=1, source_target_pairs={{0,2},{2,0},{1,3},{3,1},{4,6},{6,4},{5,7},{7,5},{8,10},{10,8},{9,1... | collective-permute-start | bytes 1572872 | tf_op jit(solution)/shard_map/ppermute | solution.py:53
  112.6 11.5 %collective-permute-start.17 = (bf16[512,512]{1,0:T(8,128)(2,1)}, bf16[512,512]{1,0:T(8,128)(2,1)}, u32[]{:S(2)}, u32[]{:S(2)}) collective-permute-start(bf16[512,512]{1,0:T(8,128)(2,1)} %select_select_fusion), channel_id=1, source_target_pairs={{2,6},{6,2},{10,14},{14,10},{18,22},{22,18},{26,30},{30,26},{3,7},... | collective-permute-start | bytes 1572872 | tf_op jit(solution)/shard_map/ppermute | solution.py:53
  122.5 2.3 %collective-permute-start.8 = (bf16[512,512]{1,0:T(8,128)(2,1)}, bf16[512,512]{1,0:T(8,128)(2,1)}, u32[]{:S(2)}, u32[]{:S(2)}) collective-permute-start(bf16[512,512]{1,0:T(8,128)(2,1)} %collective-permute-done.7), channel_id=1, source_target_pairs={{0,2},{2,0},{1,3},{3,1},{4,6},{6,4},{5,7},{7,5},{8,10},{10,8},{9,1... | collective-permute-start | bytes 1572872 | tf_op jit(solution)/shard_map/ppermute | solution.py:53
  122.5 8.7 %collective-permute-start.16 = (bf16[512,512]{1,0:T(8,128)(2,1)}, bf16[512,512]{1,0:T(8,128)(2,1)S(1)}, u32[]{:S(2)}, u32[]{:S(2)}) collective-permute-start(bf16[512,512]{1,0:T(8,128)(2,1)} %select_select_fusion), channel_id=1, source_target_pairs={{0,2},{2,0},{1,3},{3,1},{4,6},{6,4},{5,7},{7,5},{8,10},{10,8},{9,1... | collective-permute-start | bytes 1572872 | tf_op jit(solution)/shard_map/ppermute | solution.py:53
  124.2 11.7 %collective-permute-start.18 = (bf16[512,512]{1,0:T(8,128)(2,1)}, bf16[512,512]{1,0:T(8,128)(2,1)S(1)}, u32[]{:S(2)}, u32[]{:S(2)}) collective-permute-start(bf16[512,512]{1,0:T(8,128)(2,1)} %collective-permute-done.17), channel_id=1, source_target_pairs={{0,2},{2,0},{1,3},{3,1},{4,6},{6,4},{5,7},{7,5},{8,10},{10,8},{9,1... | collective-permute-start | bytes 1572872 | tf_op jit(solution)/shard_map/ppermute | solution.py:53
  125.8 5.5 %copy-start.4 = (f32[1024,1]{1,0:T(8,128)S(1)}, f32[1024,1]{1,0:T(8,128)}, u32[]{:S(2)}) copy-start(f32[1024,1]{1,0:T(8,128)} %copy.17.scl) | copy-start | bytes 12292
  (5 other events, 18.4 us)

commit v3 on v0

v3 whole, which is shorter than its diff:
```python
import jax
import jax.numpy as jnp
from jax import lax
from jax.experimental import pallas as pl
from jax.experimental.pallas import tpu as pltpu
from jax.sharding import PartitionSpec as P

AXES = ("row", "col")
BF = jnp.bfloat16
F32 = jnp.float32
VMEM_BYTES = 12 * 1024 * 1024
TILE = 256


def dot(a, b):
    return jnp.dot(a, b, preferred_element_type=F32)


def after(value, *others):
    return lax.optimization_barrier((value, *others))[0]


def device(x, c, z, k):
    return ((z * 2 + x) * 2 + k) * 2 + c


PLACES = [(x, c, z, k) for z in range(4) for x in range(2) for k in range(2) for c in range(2)]


def paired(wanted, side):
    mate = {}

    def join(a, b):
        assert a not in mate and b not in mate and a != b
        mate[a], mate[b] = b, a

    def across(place, axis):
        x, c, z, k = place
        return (1 - x, c, z, k) if axis == "x" else (x, 1 - c, z, k)

    def core(place):
        x, c, z, k = place
        return (x, c, z, 1 - k)

    for a, b in wanted:
        join(a, b)
    for axis in (side, "y" if side == "x" else "x"):
        for place in [p for p in PLACES if p not in mate and core(p) in mate]:
            if place not in mate and across(place, axis) not in mate:
                join(place, across(place, axis))
    for place in PLACES:
        if place not in mate:
            join(place, core(place))
    return [(device(*a), device(*b)) for a, b in mate.items()]


def swap(value, wanted, side):
    return lax.ppermute(value, AXES, paired(wanted, side))


def swap_some(value, wanted):
    return lax.ppermute(value, AXES, [(device(*p), device(*q)) for a, b in wanted for p, q in ((a, b), (b, a))])


def send(value, wanted):
    return lax.ppermute(value, AXES, [(device(*a), device(*b)) for a, b in wanted])


def core_swap(value):
    return swap(value, [((x, c, z, 0), (x, c, z, 1)) for x, c, z, k in PLACES if k == 0], "x")


COLS = (0, 1)


def far_step(core):
    return [((x, c, 0, core), (x, c, 2, core)) for c in COLS for x in (0, 1)]


def near_step(core):
    return [((x, c, z, core), (x, c, z + 1, core)) for c in COLS for x in (0, 1) for z in (0, 2)]


def side_step(core):
    return [((0, c, z, core), (1, c, z, core)) for c in COLS for z in range(4)]


VMEM = pl.BlockSpec(memory_space=pltpu.VMEM)
SMEM = pl.BlockSpec(memory_space=pltpu.SMEM)
ANY = pl.BlockSpec(memory_space=pl.ANY)


def call(kernel, operands, shapes, ins, outs, scratch=(), aliases=None):
    return pl.pallas_call(
        kernel,
        in_specs=ins,
        out_specs=outs,
        out_shape=shapes,
        scratch_shapes=list(scratch),
        input_output_aliases=aliases or {},
        compiler_params=pltpu.CompilerParams(vmem_limit_bytes=VMEM_BYTES),
    )(*operands)


def columns(share, start):
    n = share.shape[1]
    width, parts = n // 2, 4
    rows = n // parts

    def kernel(source, target, sems):
        copies = [
            pltpu.make_async_copy(
                source.at[pl.ds(i * rows, rows), pl.ds(start, width)], target.at[pl.ds(i * rows, rows)], sems.at[i]
            )
            for i in range(parts)
        ]
        for copy in copies:
            copy.start()
        for copy in copies:
            copy.wait()

    return call(
        kernel, (share,), jax.ShapeDtypeStruct((n, width), BF), [ANY], VMEM, [pltpu.SemaphoreType.DMA((parts,))]
    )


def solve_first(flags, share, far, inverse, start):
    half, n = inverse.shape

    def kernel(flags, cur, got, inv, out):
        @pl.when(flags[0] == 0)
        def _():
            for t in range(0, half, TILE):
                here = cur[:, start + t : start + t + TILE]
                fan = (here.astype(F32) + got[:, t : t + TILE].astype(F32)).astype(BF)
                out[:, t : t + TILE] = dot(inv[...], fan).astype(BF)

    return call(
        kernel, (flags, share, far, inverse), jax.ShapeDtypeStruct((half, half), BF), [SMEM] + [VMEM] * 3, VMEM
    )


def second_block(flags, share, scale, panel, solved, matrix, start):
    half, n = matrix.shape

    def kernel(flags, cur, scl, pan, sol, mat, own, message):
        @pl.when(flags[0] == 1)
        def _():
            for t in range(0, half, TILE):
                cols = slice(t, t + TILE)
                here = cur[:, start + t : start + t + TILE]
                newer = (here.astype(F32) - scl[:, 0:1] * dot(pan[...], sol[:, cols])).astype(BF)
                product = dot(mat[...], newer).astype(BF)
                upper = flags[1] == 0
                own[:, cols] = jnp.where(upper, newer[:half], product)
                message[:, cols] = jnp.where(upper, product, newer[:half])

    return call(
        kernel,
        (flags, share, scale, panel, solved, matrix),
        [jax.ShapeDtypeStruct((half, half), BF)] * 2,
        [SMEM] + [VMEM] * 5,
        [VMEM] * 2,
    )


def solve_second(flags, right, left, inverse):
    half, n = inverse.shape

    def kernel(flags, a0, b0, a1, b1, inv, out):
        def one(a, b):
            out[...] = (a[...].astype(F32) + b[...].astype(F32)).astype(BF)

        pl.when(flags[0] == 1)(lambda: one(a0, b0))
        pl.when(flags[0] == 3)(lambda: one(a1, b1))

        @pl.when(jnp.logical_and(flags[1] == 0, jnp.logical_or(flags[0] == 1, flags[0] == 3)))
        def _():
            for t in range(0, half, TILE):
                cols = slice(t, t + TILE)
                out[:, cols] = dot(inv[:, :half], out[:, cols]).astype(BF)

    return call(
        kernel,
        (flags, *right, *left, inverse),
        jax.ShapeDtypeStruct((half, half), BF),
        [SMEM] + [VMEM] * 5,
        VMEM,
    )


def gather(pieces, target):
    rows = target.shape[0] // len(pieces)
    for i, piece in enumerate(pieces):
        target[i * rows : (i + 1) * rows] = piece[...]


def update_first(flags, share, scale, panel, mine, other):
    n, half = panel.shape
    lists = [list(some) for pair in (mine, other) for some in pair]
    counts = [len(some) for some in lists]

    def kernel(flags, cur, scl, pan, *refs):
        refs = list(refs)
        parts = [[refs.pop(0) for _ in range(count)] for count in counts]
        out, solved, sol, sems = refs
        for at, side in ((0, 1 - flags[2]), (2, flags[2])):
            pl.when(flags[3] == 0)(lambda: gather(parts[at], sol.at[side]))
            pl.when(flags[3] != 0)(lambda: gather(parts[at + 1], sol.at[side]))
        copies = [
            pltpu.make_async_copy(sol.at[s], solved.at[0, :, pl.ds(s * half, half)], sems.at[s]) for s in range(2)
        ]
        for copy in copies:
            copy.start()
        for s in range(2):
            cols = slice(s * half, (s + 1) * half)
            for t in range(0, n, TILE):
                rows = slice(t, t + TILE)
                old = cur[rows, cols]
                newer = (old.astype(F32) - scl[rows, 0:1] * dot(pan[rows], sol[s])).astype(BF)
                out[rows, cols] = jnp.where(flags[0] > 0, newer, old)
        for copy in copies:
            copy.wait()

    operands = [flags, share, scale, panel, *sum(lists, [])]
    return call(
        kernel,
        operands,
        [jax.ShapeDtypeStruct((n, n), BF), jax.ShapeDtypeStruct((2, half, n), BF)],
        [SMEM] + [VMEM] * (len(operands) - 1),
        [VMEM, ANY],
        [pltpu.VMEM((2, half, half), BF), pltpu.SemaphoreType.DMA((2,))],
    )


def update_second(flags, current, scale, panel, parts, swapped, solved, remaining=None):
    n, half = panel.shape
    steps = n // TILE
    pieces = len(parts)

    def kernel(flags, cur, scl, pan, *refs):
        mine, theirs = refs[:pieces], refs[pieces : 2 * pieces]
        out, solved, sol, tile, sems = refs[-5:]
        cols = pl.ds(pl.multiple_of(flags[2] * half, half), half)
        pl.when(flags[3] == 1)(lambda: gather(mine, sol))
        pl.when(flags[3] != 1)(lambda: gather(theirs, sol))
        copies = [pltpu.make_async_copy(sol, solved.at[1, :, cols], sems.at[steps])]
        copies[0].start()
        for i in range(steps):
            rows = slice(i * TILE, (i + 1) * TILE)
            old = cur[rows, cols]
            newer = (old.astype(F32) - scl[rows, 1:2] * dot(pan[rows], sol[...])).astype(BF)
            tile[rows] = jnp.where(flags[0] > 1, newer, old)
            copy = pltpu.make_async_copy(tile.at[rows], out.at[rows, cols], sems.at[i])
            copy.start()
            copies.append(copy)
        for copy in copies:
            copy.wait()

    operands = [flags, current, scale, panel, *parts, *swapped, solved]
    aliases = {len(operands) - 1: 1}
    if remaining is not None:
        operands.append(remaining)
        aliases[len(operands) - 1] = 0
    return call(
        kernel,
        operands,
        [jax.ShapeDtypeStruct((n, n), BF), jax.ShapeDtypeStruct((2, half, n), BF)],
        [SMEM] + [VMEM] * (3 + 2 * pieces) + [ANY] * len(aliases),
        [ANY, ANY],
        [pltpu.VMEM((half, half), BF), pltpu.VMEM((n, half), BF), pltpu.SemaphoreType.DMA((steps + 1,))],
        aliases,
    )


def body(pending, panel, panel_scale, inverse_blocks):
    row, c = lax.axis_index("row"), lax.axis_index("col")
    z, x, k = lax.shift_right_logical(row, 2), lax.shift_right_logical(row, 1) & 1, row & 1
    half = inverse_blocks.shape[1]
    quarter = half // 2
    flags = jnp.stack([row, c, x, k]).astype(jnp.int32)
    flipped = jnp.stack([row, c, 1 - x, k]).astype(jnp.int32)
    roots = [((0, 0, 0, 0), (0, 1, 0, 0))]
    seconds = [((0, 0, 0, 1), (0, 1, 0, 1))]
    share, flags, flipped, upper, near, middle, odd, first_core = lax.optimization_barrier(
        (pending[:, 0, :], flags, flipped, c == 0, x == 0, z == 2, (z & 1) == 1, k == 0)
    )

    left = columns(share, 0)
    far_left = swap_some(left, roots)
    later, inverse = lax.optimization_barrier((share, inverse_blocks, left))[:2]
    inv1 = jnp.where(near, inverse[1, quarter:], inverse[1, :quarter])
    crossed = swap_some(inv1, [((1, 0, 0, 1), (1, 1, 0, 1)), ((0, 0, 1, 0), (0, 1, 1, 0))])
    panel0, panel1, later = lax.optimization_barrier((panel[:, 0, :], panel[:, 1, :], later))
    far_right = swap_some(columns(later, half), roots)
    matrix_top = send(
        crossed,
        [((1, c_, 0, 1), (0, c_, 0, 1)) for c_ in COLS] + [((0, c_, 1, 0), (0, c_, 0, 0)) for c_ in COLS],
    )
    inv0, inv1, scale = inverse[0], inverse[1], panel_scale

    first_left = solve_first(flags, share, far_left, inv0, 0)
    left_here = core_swap(first_left)
    first_hop = swap_some(first_left, [((0, c_, 0, 0), (1, c_, 0, 0)) for c_ in COLS])
    matrix_bottom = core_swap(after(matrix_top, first_left))
    matrix = jnp.where(upper, jnp.concatenate([matrix_top, matrix_bottom]), inv1)
    own, message = second_block(flags, share, scale, panel0, left_here, matrix, 0)
    own_hop = send(own, [((0, c_, 0, 1), (1, c_, 0, 1)) for c_ in COLS])
    message_hop = send(message, [((0, c_, 0, 1), (1, 1 - c_, 0, 1)) for c_ in COLS])

    first_right = solve_first(flags, share, after(far_right, own), inv0, half)
    right_here = core_swap(first_right)
    mine0 = jnp.where(near, first_right, first_hop)
    got0 = swap_some(mine0, far_step(0))
    own, message = second_block(flags, share, scale, panel0, right_here, matrix, half)
    answer = swap_some(message, seconds)

    mine0 = jnp.where(middle, got0, mine0)
    got0 = swap_some(mine0, near_step(0))

    second = solve_second(flags, (own, after(answer, mine0)), (own_hop, message_hop), inv1)

    rows = [slice(0, quarter), slice(quarter, half)]
    heads = [second[r] for r in rows]
    far = [swap(h, far_step(1), "y") for h in heads]
    mine0 = jnp.where(odd, got0, mine0)
    heads = [jnp.where(middle, f, h) for f, h in zip(far, heads)]
    step = [
        swap(jnp.where(first_core, mine0[r], h), near_step(1) + side_step(0), "y") for h, r in zip(heads, rows)
    ]
    mine1 = [jnp.where(odd, s, h) for s, h in zip(step, heads)]
    other1 = [swap(m, side_step(1), "y") for m in mine1]

    current, solved = update_first(
        flags, share, scale, panel0, ([mine0], [core_swap(mine0)]), (step, [core_swap(s) for s in step])
    )
    remaining, solved = update_second(flipped, current, scale, panel1, mine1, [core_swap(m) for m in mine1], solved)
    other1 = [after(m, remaining) for m in other1]
    remaining, solved = update_second(
        flags, current, scale, panel1, other1, [core_swap(m) for m in other1], solved, remaining
    )
    return remaining[:, None, :], solved


def body_any(pending, panel, panel_scale, inverse_blocks):
    row = lax.axis_index("row")
    current = pending[:, 0, :]
    solved = []
    for k in range(2):
        fan = lax.psum(current, "col")
        local = dot(inverse_blocks[k], fan).astype(BF)
        arrived = lax.psum(jnp.where(row == k, local, jnp.zeros_like(local)), "row")
        solved.append(arrived)
        term = dot(panel[:, k, :], arrived)
        newer = (current.astype(F32) - panel_scale[:, k : k + 1] * term).astype(BF)
        current = jnp.where(row > k, newer, current)
    return current[:, None, :], jnp.stack(solved)


def solution(mesh):
    placed = (P("row", "col", None), P("row", None, "col"), P("row", None), P(None, "col", None))
    small = mesh.shape["row"] == 16 and mesh.shape["col"] == 2
    return jax.shard_map(
        body if small else body_any,
        mesh=mesh,
        in_specs=placed,
        out_specs=(P("row", "col", None), P(None, "col", None)),
        check_vma=False,
    )
```

time: 357 us -> 91.5 us (0.26)
  waiting for transfers between devices: 310 us -> 39.6 us
  starting transfers between devices: 0.16 us -> 25.5 us
  matrix products: 18.5 us -> 0 us
  Pallas kernels: 0 us -> 13.3 us
  between operations: 13.8 us -> 1.04 us
  local copies, waits for them, and re-layouts: 12.2 us -> 7.98 us
    psum x4 -> x0, waiting for transfers between devices: 310 us -> none  [the longest x2 182 us: spread(): return lax.psum(jnp.where(mine, shard, jnp.zeros_like(shard)), axis)]
    ppermute x0 -> x26, waiting for transfers between devices: none -> 39.6 us  [the longest x7 22.4 us: swap_some(): lax.ppermute(value, AXES, [(device(*p), device(*q)) for a, b in wanted fo...]
    ppermute x0 -> x26, starting transfers between devices: none -> 25.5 us  [the longest x7 14.2 us: swap_some(): lax.ppermute(value, AXES, [(device(*p), device(*q)) for a, b in wanted fo...]
    dot_general x4 -> x0, matrix products: 18.5 us -> none  [the longest x2 10 us: body(): term = jnp.dot(panel[:, k, :], arrived, preferred_element_type=jnp.float32)]
    pallas_call x0 -> x10, Pallas kernels: none -> 13.3 us  [call(): pl.pallas_call(kernel, in_specs=ins, out_specs=outs, out_shape=shapes, sc...]
    unnamed x12 -> x21, local copies, waits for them, and re-layouts: 8.05 us -> 1.85 us
    select_n x0 -> x7, other arithmetic: none -> 3.59 us  [the longest x1 1.98 us: body(): jnp.where(upper, jnp.concatenate([matrix_top, matrix_bottom]), inv1)]
  transfers between devices with their start and end apart: 4 -> 26, of which waited for: 4 -> 12; matrix products, arithmetic and copies ran while one was open for 1% -> 11% of each run, Pallas kernels for 0% -> 12%
where the time goes in v3:
time: 91.5 us; the launch traced here: 91 us
  waiting for transfers between devices  39.6 us (43%)
  starting transfers between devices  25.5 us (28%)
  Pallas kernels  13.3 us (15%)
  local copies, waits for them, and re-layouts  7.98 us (9%)
  other arithmetic  3.67 us (4%)
  between operations  1.04 us (1%)
    ppermute x7, waiting for transfers between devices, swap_some(): lax.ppermute(value, AXES, [(device(*p), device(*q)) for a, b in wanted fo...  22.4 us
    ppermute x7, starting transfers between devices, swap_some(): lax.ppermute(value, AXES, [(device(*p), device(*q)) for a, b in wanted fo...  14.2 us
    pallas_call x10, Pallas kernels, call(): pl.pallas_call(kernel, in_specs=ins, out_specs=outs, out_shape=shapes, sc...  13.3 us
    ppermute x16, waiting for transfers between devices, swap(): return lax.ppermute(value, AXES, paired(wanted, side))  11.5 us
    ppermute x16, starting transfers between devices, swap(): return lax.ppermute(value, AXES, paired(wanted, side))  8.62 us
    ppermute x3, waiting for transfers between devices, send(): lax.ppermute(value, AXES, [(device(*a), device(*b)) for a, b in wanted])  5.66 us
    slice x1, local copies, waits for them, and re-layouts, body(): panel[:, 1, :]  2.98 us
    ppermute x3, starting transfers between devices, send(): lax.ppermute(value, AXES, [(device(*a), device(*b)) for a, b in wanted])  2.68 us
  transfers between devices with their start and end apart: 26, of which 12 were waited for; matrix products, arithmetic and copies ran while one was open for 11% of the time, Pallas kernels for 12%

profile of v3, /device:TPU:0, one launch (start us, length us, event | category | flops | bytes accessed | tf_op | source)
XLA Modules:
  0.0 91.0 jit_solution(8985640282779780628)
XLA Ops:
  0.7 1.6 %copy-done = bf16[1024,1,1024]{2,0,1:T(8,128)(2,1)S(1)} copy-done((bf16[1024,1,1024]{2,0,1:T(8,128)(2,1)S(1)}, bf16[1024,1,1024]{2,0,1:T(8,128)(2,1)}, u32[]{:S(2)}) %copy-start) | copy-done | bytes 2097176
  2.4 5.0 %collective-permute-start.1 = (bf16[1024,512]{1,0:T(8,128)(2,1)S(1)}, bf16[1024,512]{1,0:T(8,128)(2,1)S(1)}, u32[]{:S(2)}, u32[]{:S(2)}) collective-permute-start(bf16[1024,512]{1,0:T(8,128)(2,1)S(1)} %shard_map.59), channel_id=1, source_target_pairs={{0,1},{1,0}} | collective-permute-start | bytes 3145736 | tf_op jit(solution)/shard_map/ppermute | solution.py:62
  9.4 3.0 %fusion = (bf16[1024,1,512]{2,1,0:T(2,128)(2,1)S(1)}, bf16[1024,1,512]{2,1,0:T(2,128)(2,1)S(1)}) fusion(bf16[1024,2,512]{2,1,0:T(2,128)(2,1)S(1)} %copy-done.7), kind=kLoop, calls=%fused_computation.18 | loop fusion | bytes 4194304 | tf_op jit(solution)/shard_map/slice | solution.py:294
  12.4 1.3 %collective-permute-start.4 = (bf16[256,1024]{1,0:T(8,128)(2,1)S(1)}, bf16[256,1024]{1,0:T(8,128)(2,1)}, u32[]{:S(2)}, u32[]{:S(2)}) collective-permute-start(bf16[256,1024]{1,0:T(8,128)(2,1)S(1)} %collective-permute-done.3), channel_id=1, source_target_pairs={{6,2},{7,3},{8,0},{9,1}} | collective-permute-start | bytes 1572872 | tf_op jit(solution)/shard_map/ppermute | solution.py:66
  13.7 1.9 %copy_bitcast_fusion = (bf16[1024,512]{1,0:T(8,128)(2,1)}, bf16[1024,512]{1,0:T(8,128)(2,1)}) fusion(bf16[1024,1,512]{2,1,0:T(2,128)(2,1)S(1)} %get-tuple-element.60, bf16[1024,1,512]{2,1,0:T(2,128)(2,1)S(1)} %get-tuple-element.61), kind=kLoop, calls=%fused_computation.1 | loop fusion | bytes 4194304 | tf_op jit(solution)/shard_map/squeeze | solution.py:294
  16.8 1.9 %collective-permute-start = (bf16[1024,512]{1,0:T(8,128)(2,1)}, bf16[1024,512]{1,0:T(8,128)(2,1)}, u32[]{:S(2)}, u32[]{:S(2)}) collective-permute-start(bf16[1024,512]{1,0:T(8,128)(2,1)} %shard_map.60), channel_id=1, source_target_pairs={{0,1},{1,0}} | collective-permute-start | bytes 3145736 | tf_op jit(solution)/shard_map/ppermute | solution.py:62
  20.2 1.3 %shard_map.61 = bf16[512,512]{1,0:T(8,128)(2,1)S(1)} custom-call(s32[4]{0:T(128)S(1)} %get-tuple-element.30.flags, bf16[1024,1024]{1,0:T(8,128)(2,1)S(1)} %bitcast.21, bf16[1024,512]{1,0:T(8,128)(2,1)S(1)} %collective-permute-done.1.got, bf16[512,1024]{1,0:T(8,128)(2,1)S(1)} %get-tuple-element.59.inv), custom_call_target="tpu_custom_call" | custom-call | tf_op jit(solution)/shard_map/pallas_call | solution.py:94
  21.5 5.7 %collective-permute-done.4 = bf16[256,1024]{1,0:T(8,128)(2,1)} collective-permute-done((bf16[256,1024]{1,0:T(8,128)(2,1)S(1)}, bf16[256,1024]{1,0:T(8,128)(2,1)}, u32[]{:S(2)}, u32[]{:S(2)}) %collective-permute-start.4) | collective-permute-done | bytes 524320 | tf_op jit(solution)/shard_map/ppermute | solution.py:66
  27.7 1.9 %collective-permute-start.6 = (bf16[512,512]{1,0:T(8,128)(2,1)S(1)}, bf16[512,512]{1,0:T(8,128)(2,1)}, u32[]{:S(2)}, u32[]{:S(2)}) collective-permute-start(bf16[512,512]{1,0:T(8,128)(2,1)S(1)} %shard_map.61), channel_id=1, source_target_pairs={{0,4},{4,0},{1,5},{5,1}} | collective-permute-start | bytes 1572872 | tf_op jit(solution)/shard_map/ppermute | solution.py:62
  30.2 2.0 %maximum_select_fusion.mat = bf16[512,1024]{1,0:T(8,128)(2,1)S(1)} fusion(bf16[256,1024]{1,0:T(8,128)(2,1)} %collective-permute-done.5, bf16[256,1024]{1,0:T(8,128)(2,1)} %collective-permute-done.4, pred[]{:T(512)S(6)} %eq.15, bf16[2,512,1024]{2,1,0:T(8,128)(2,1)} %param.7), kind=kLoop, calls=%fused_computation | loop fusion | flops 2621440 | bytes 3145729 | tf_op jit(solution)/shard_map/jit(_where)/select_n | solution.py:306
  33.8 2.0 %shard_map.63 = bf16[512,512]{1,0:T(8,128)(2,1)S(1)} custom-call(s32[4]{0:T(128)S(1)} %get-tuple-element.30.flags, bf16[1024,1024]{1,0:T(8,128)(2,1)S(1)} %bitcast.23, bf16[1024,512]{1,0:T(8,128)(2,1)} %collective-permute-done.got, bf16[512,1024]{1,0:T(8,128)(2,1)S(1)} %copy-done.4), custom_call_target="tpu_custom_call" | custom-call | tf_op jit(solution)/shard_map/pallas_call | solution.py:94
  36.5 2.4 %collective-permute-done.6 = bf16[512,512]{1,0:T(8,128)(2,1)} collective-permute-done((bf16[512,512]{1,0:T(8,128)(2,1)S(1)}, bf16[512,512]{1,0:T(8,128)(2,1)}, u32[]{:S(2)}, u32[]{:S(2)}) %collective-permute-start.6) | collective-permute-done | bytes 524320 | tf_op jit(solution)/shard_map/ppermute | solution.py:62
  39.0 1.9 %collective-permute-start.7 = (bf16[512,512]{1,0:T(8,128)(2,1)S(1)}, bf16[512,512]{1,0:T(8,128)(2,1)S(1)}, u32[]{:S(2)}, u32[]{:S(2)}) collective-permute-start(bf16[512,512]{1,0:T(8,128)(2,1)S(1)} %broadcast_select_fusion), channel_id=1, source_target_pairs={{0,16},{16,0},{4,20},{20,4},{1,17},{17,1},{5,21},{21,5}} | collective-permute-start | bytes 1572872 | tf_op jit(solution)/shard_map/ppermute | solution.py:62
  43.7 7.2 %collective-permute-done.7 = bf16[512,512]{1,0:T(8,128)(2,1)S(1)} collective-permute-done((bf16[512,512]{1,0:T(8,128)(2,1)S(1)}, bf16[512,512]{1,0:T(8,128)(2,1)S(1)}, u32[]{:S(2)}, u32[]{:S(2)}) %collective-permute-start.7) | collective-permute-done | bytes 524320 | tf_op jit(solution)/shard_map/ppermute | solution.py:62
  51.0 1.9 %collective-permute-start.8 = (bf16[512,512]{1,0:T(8,128)(2,1)S(1)}, bf16[512,512]{1,0:T(8,128)(2,1)S(1)}, u32[]{:S(2)}, u32[]{:S(2)}) collective-permute-start(bf16[512,512]{1,0:T(8,128)(2,1)S(1)} %broadcast_select_fusion.1), channel_id=1, source_target_pairs={{0,8},{8,0},{16,24},{24,16},{4,12},{12,4},{20,28},{28,20},{1,9},{9... | collective-permute-start | bytes 1572872 | tf_op jit(solution)/shard_map/ppermute | solution.py:62
  53.6 1.6 %collective-permute-start.16 = (bf16[256,512]{1,0:T(8,128)(2,1)S(1)}, bf16[256,512]{1,0:T(8,128)(2,1)S(1)}, u32[]{:S(2)}, u32[]{:S(2)}) collective-permute-start(bf16[256,512]{1,0:T(8,128)(2,1)S(1)} %get-tuple-element.66), channel_id=1, source_target_pairs={{2,18},{18,2},{6,22},{22,6},{3,19},{19,3},{7,23},{23,7},{0,1},{1,0... | collective-permute-start | bytes 786440 | tf_op jit(solution)/shard_map/ppermute | solution.py:58
  55.7 12.0 %collective-permute-done.8 = bf16[512,512]{1,0:T(8,128)(2,1)S(1)} collective-permute-done((bf16[512,512]{1,0:T(8,128)(2,1)S(1)}, bf16[512,512]{1,0:T(8,128)(2,1)S(1)}, u32[]{:S(2)}, u32[]{:S(2)}) %collective-permute-start.8) | collective-permute-done | bytes 524320 | tf_op jit(solution)/shard_map/ppermute | solution.py:62
  70.0 4.3 %collective-permute-done.17.refs_3_ = bf16[256,512]{1,0:T(8,128)(2,1)S(1)} collective-permute-done((bf16[256,512]{1,0:T(8,128)(2,1)S(1)}, bf16[256,512]{1,0:T(8,128)(2,1)S(1)}, u32[]{:S(2)}, u32[]{:S(2)}) %collective-permute-start.17) | collective-permute-done | bytes 262176 | tf_op jit(solution)/shard_map/ppermute | solution.py:58
  74.3 2.8 %collective-permute-done.15.refs_2_ = bf16[256,512]{1,0:T(8,128)(2,1)S(1)} collective-permute-done((bf16[256,512]{1,0:T(8,128)(2,1)S(1)}, bf16[256,512]{1,0:T(8,128)(2,1)S(1)}, u32[]{:S(2)}, u32[]{:S(2)}) %collective-permute-start.15) | collective-permute-done | bytes 262176 | tf_op jit(solution)/shard_map/ppermute | solution.py:58
  77.9 1.5 %collective-permute-start.23 = (bf16[256,512]{1,0:T(8,128)(2,1)S(1)}, bf16[256,512]{1,0:T(8,128)(2,1)S(1)}, u32[]{:S(2)}, u32[]{:S(2)}) collective-permute-start(bf16[256,512]{1,0:T(8,128)(2,1)S(1)} %get-tuple-element.64.refs_1_), channel_id=1, source_target_pairs={{2,6},{6,2},{10,14},{14,10},{18,22},{22,18},{26,30},{30,26},{3,7},... | collective-permute-start | bytes 786440 | tf_op jit(solution)/shard_map/ppermute | solution.py:58
  79.9 2.3 %shard_map.66 = (bf16[1024,1024]{1,0:T(8,128)(2,1)S(1)}, bf16[2,512,1024]{2,1,0:T(8,128)(2,1)}) custom-call(s32[4]{0:T(128)S(1)} %get-tuple-element.30.flags, bf16[1024,1024]{1,0:T(8,128)(2,1)S(1)} %bitcast.25, f32[1024,2]{1,0:T(8,128)S(1)} %copy.13.scl, bf16[1024,512]{1,0:T(8,128)(2,1)S(1)} %copy-done.2, ...), custom_call_target="tpu_custom_call" | custom-call | tf_op jit(solution)/shard_map/pallas_call | solution.py:94
  82.2 2.1 %shard_map.67 = (bf16[1024,1024]{1,0:T(8,128)(2,1)}, bf16[2,512,1024]{2,1,0:T(8,128)(2,1)}) custom-call(s32[4]{0:T(128)S(1)} %get-tuple-element.50.flags, bf16[1024,1024]{1,0:T(8,128)(2,1)S(1)} %get-tuple-element.48.cur, f32[1024,2]{1,0:T(8,128)S(1)} %copy.13.scl, bf16[1024,512]{1,0:T(8,128)(2,1)S(1)} %copy-done.5, ...), custom_call_target="tpu_custom_call", output_to_operand_aliasing={{1}: (8, {})} | custom-call | tf_op jit(solution)/shard_map/pallas_call | solution.py:94
  84.4 2.7 %collective-permute-done.20.refs_0_ = bf16[256,512]{1,0:T(8,128)(2,1)S(1)} collective-permute-done((bf16[256,512]{1,0:T(8,128)(2,1)S(1)}, bf16[256,512]{1,0:T(8,128)(2,1)S(1)}, u32[]{:S(2)}, u32[]{:S(2)}) %collective-permute-start.20) | collective-permute-done | bytes 262176 | tf_op jit(solution)/shard_map/ppermute | solution.py:58
  88.9 2.1 %shard_map.68 = (bf16[1024,1024]{1,0:T(8,128)(2,1)}, bf16[2,512,1024]{2,1,0:T(8,128)(2,1)}) custom-call(s32[4]{0:T(128)S(1)} %get-tuple-element.30.flags, bf16[1024,1024]{1,0:T(8,128)(2,1)S(1)} %get-tuple-element.48.cur, f32[1024,2]{1,0:T(8,128)S(1)} %copy.13.scl, bf16[1024,512]{1,0:T(8,128)(2,1)S(1)} %copy-done.5, ...), custom_call_target="tpu_custom_call", output_to_operand_aliasing={{1}: (8, {}), {0}: (9, {})} | custom-call | tf_op jit(solution)/shard_map/pallas_call | solution.py:94
  (71 shorter events, 17.5 us)
Async XLA Ops:
  2.4 17.8 %collective-permute-start.1 = (bf16[1024,512]{1,0:T(8,128)(2,1)S(1)}, bf16[1024,512]{1,0:T(8,128)(2,1)S(1)}, u32[]{:S(2)}, u32[]{:S(2)}) collective-permute-start(bf16[1024,512]{1,0:T(8,128)(2,1)S(1)} %shard_map.59), channel_id=1, source_target_pairs={{0,1},{1,0}} | collective-permute-start | bytes 3145736 | tf_op jit(solution)/shard_map/ppermute | solution.py:62
  8.7 3.7 %collective-permute-start.3 = (bf16[256,1024]{1,0:T(8,128)(2,1)S(1)}, bf16[256,1024]{1,0:T(8,128)(2,1)S(1)}, u32[]{:S(2)}, u32[]{:S(2)}) collective-permute-start(bf16[256,1024]{1,0:T(8,128)(2,1)S(1)} %select_bitcast_fusion), channel_id=1, source_target_pairs={{6,7},{7,6},{8,9},{9,8}} | collective-permute-start | bytes 1572872 | tf_op jit(solution)/shard_map/ppermute | solution.py:62
  12.4 14.8 %collective-permute-start.4 = (bf16[256,1024]{1,0:T(8,128)(2,1)S(1)}, bf16[256,1024]{1,0:T(8,128)(2,1)}, u32[]{:S(2)}, u32[]{:S(2)}) collective-permute-start(bf16[256,1024]{1,0:T(8,128)(2,1)S(1)} %collective-permute-done.3), channel_id=1, source_target_pairs={{6,2},{7,3},{8,0},{9,1}} | collective-permute-start | bytes 1572872 | tf_op jit(solution)/shard_map/ppermute | solution.py:66
  16.8 17.0 %collective-permute-start = (bf16[1024,512]{1,0:T(8,128)(2,1)}, bf16[1024,512]{1,0:T(8,128)(2,1)}, u32[]{:S(2)}, u32[]{:S(2)}) collective-permute-start(bf16[1024,512]{1,0:T(8,128)(2,1)} %shard_map.60), channel_id=1, source_target_pairs={{0,1},{1,0}} | collective-permute-start | bytes 3145736 | tf_op jit(solution)/shard_map/ppermute | solution.py:62
  27.2 3.0 %collective-permute-start.5 = (bf16[256,1024]{1,0:T(8,128)(2,1)}, bf16[256,1024]{1,0:T(8,128)(2,1)}, u32[]{:S(2)}, u32[]{:S(2)}) collective-permute-start(bf16[256,1024]{1,0:T(8,128)(2,1)} %collective-permute-done.4), channel_id=1, source_target_pairs={{0,2},{2,0},{1,3},{3,1},{4,6},{6,4},{5,7},{7,5},{8,10},{10,8},{9,1... | collective-permute-start | bytes 1572872 | tf_op jit(solution)/shard_map/ppermute | solution.py:58
  27.2 5.0 %collective-permute-start.2 = (bf16[512,512]{1,0:T(8,128)(2,1)S(1)}, bf16[512,512]{1,0:T(8,128)(2,1)}, u32[]{:S(2)}, u32[]{:S(2)}) collective-permute-start(bf16[512,512]{1,0:T(8,128)(2,1)S(1)} %shard_map.61), channel_id=1, source_target_pairs={{0,2},{2,0},{1,3},{3,1},{4,6},{6,4},{5,7},{7,5},{8,10},{10,8},{9,1... | collective-permute-start | bytes 1572872 | tf_op jit(solution)/shard_map/ppermute | solution.py:58
  27.7 11.2 %collective-permute-start.6 = (bf16[512,512]{1,0:T(8,128)(2,1)S(1)}, bf16[512,512]{1,0:T(8,128)(2,1)}, u32[]{:S(2)}, u32[]{:S(2)}) collective-permute-start(bf16[512,512]{1,0:T(8,128)(2,1)S(1)} %shard_map.61), channel_id=1, source_target_pairs={{0,4},{4,0},{1,5},{5,1}} | collective-permute-start | bytes 1572872 | tf_op jit(solution)/shard_map/ppermute | solution.py:62
  35.8 6.5 %collective-permute-start.10 = (bf16[512,512]{1,0:T(8,128)(2,1)S(1)}, bf16[512,512]{1,0:T(8,128)(2,1)S(1)}, u32[]{:S(2)}, u32[]{:S(2)}) collective-permute-start(bf16[512,512]{1,0:T(8,128)(2,1)S(1)} %shard_map.63), channel_id=1, source_target_pairs={{0,2},{2,0},{1,3},{3,1},{4,6},{6,4},{5,7},{7,5},{8,10},{10,8},{9,1... | collective-permute-start | bytes 1572872 | tf_op jit(solution)/shard_map/ppermute | solution.py:58
  39.0 12.0 %collective-permute-start.7 = (bf16[512,512]{1,0:T(8,128)(2,1)S(1)}, bf16[512,512]{1,0:T(8,128)(2,1)S(1)}, u32[]{:S(2)}, u32[]{:S(2)}) collective-permute-start(bf16[512,512]{1,0:T(8,128)(2,1)S(1)} %broadcast_select_fusion), channel_id=1, source_target_pairs={{0,16},{16,0},{4,20},{20,4},{1,17},{17,1},{5,21},{21,5}} | collective-permute-start | bytes 1572872 | tf_op jit(solution)/shard_map/ppermute | solution.py:62
  40.9 12.1 %collective-permute-start.12 = (bf16[512,512]{1,0:T(8,128)(2,1)S(1)}, bf16[512,512]{1,0:T(8,128)(2,1)S(1)}, u32[]{:S(2)}, u32[]{:S(2)}) collective-permute-start(bf16[512,512]{1,0:T(8,128)(2,1)S(1)} %get-tuple-element.41), channel_id=1, source_target_pairs={{2,6},{3,7}} | collective-permute-start | bytes 1572872 | tf_op jit(solution)/shard_map/ppermute | solution.py:66
  41.6 11.3 %collective-permute-start.13 = (bf16[512,512]{1,0:T(8,128)(2,1)S(1)}, bf16[512,512]{1,0:T(8,128)(2,1)S(1)}, u32[]{:S(2)}, u32[]{:S(2)}) collective-permute-start(bf16[512,512]{1,0:T(8,128)(2,1)S(1)} %get-tuple-element.47), channel_id=1, source_target_pairs={{2,7},{3,6}} | collective-permute-start | bytes 1572872 | tf_op jit(solution)/shard_map/ppermute | solution.py:66
  42.9 10.1 %collective-permute-start.11 = (bf16[512,512]{1,0:T(8,128)(2,1)S(1)}, bf16[512,512]{1,0:T(8,128)(2,1)S(1)}, u32[]{:S(2)}, u32[]{:S(2)}) collective-permute-start(bf16[512,512]{1,0:T(8,128)(2,1)S(1)} %get-tuple-element.45), channel_id=1, source_target_pairs={{2,3},{3,2}} | collective-permute-start | bytes 1572872 | tf_op jit(solution)/shard_map/ppermute | solution.py:62
  51.0 16.7 %collective-permute-start.8 = (bf16[512,512]{1,0:T(8,128)(2,1)S(1)}, bf16[512,512]{1,0:T(8,128)(2,1)S(1)}, u32[]{:S(2)}, u32[]{:S(2)}) collective-permute-start(bf16[512,512]{1,0:T(8,128)(2,1)S(1)} %broadcast_select_fusion.1), channel_id=1, source_target_pairs={{0,8},{8,0},{16,24},{24,16},{4,12},{12,4},{20,28},{28,20},{1,9},{9... | collective-permute-start | bytes 1572872 | tf_op jit(solution)/shard_map/ppermute | solution.py:62
  53.6 14.2 %collective-permute-start.16 = (bf16[256,512]{1,0:T(8,128)(2,1)S(1)}, bf16[256,512]{1,0:T(8,128)(2,1)S(1)}, u32[]{:S(2)}, u32[]{:S(2)}) collective-permute-start(bf16[256,512]{1,0:T(8,128)(2,1)S(1)} %get-tuple-element.66), channel_id=1, source_target_pairs={{2,18},{18,2},{6,22},{22,6},{3,19},{19,3},{7,23},{23,7},{0,1},{1,0... | collective-permute-start | bytes 786440 | tf_op jit(solution)/shard_map/ppermute | solution.py:58
  55.2 12.6 %collective-permute-start.14 = (bf16[256,512]{1,0:T(8,128)(2,1)S(1)}, bf16[256,512]{1,0:T(8,128)(2,1)S(1)}, u32[]{:S(2)}, u32[]{:S(2)}) collective-permute-start(bf16[256,512]{1,0:T(8,128)(2,1)S(1)} %get-tuple-element.67), channel_id=1, source_target_pairs={{2,18},{18,2},{6,22},{22,6},{3,19},{19,3},{7,23},{23,7},{0,1},{1,0... | collective-permute-start | bytes 786440 | tf_op jit(solution)/shard_map/ppermute | solution.py:58
  67.9 6.4 %collective-permute-start.17 = (bf16[256,512]{1,0:T(8,128)(2,1)S(1)}, bf16[256,512]{1,0:T(8,128)(2,1)S(1)}, u32[]{:S(2)}, u32[]{:S(2)}) collective-permute-start(bf16[256,512]{1,0:T(8,128)(2,1)S(1)} %get-tuple-element.62), channel_id=1, source_target_pairs={{2,10},{10,2},{18,26},{26,18},{6,14},{14,6},{22,30},{30,22},{3,11}... | collective-permute-start | bytes 786440 | tf_op jit(solution)/shard_map/ppermute | solution.py:58
  69.0 8.1 %collective-permute-start.15 = (bf16[256,512]{1,0:T(8,128)(2,1)S(1)}, bf16[256,512]{1,0:T(8,128)(2,1)S(1)}, u32[]{:S(2)}, u32[]{:S(2)}) collective-permute-start(bf16[256,512]{1,0:T(8,128)(2,1)S(1)} %get-tuple-element.63), channel_id=1, source_target_pairs={{2,10},{10,2},{18,26},{26,18},{6,14},{14,6},{22,30},{30,22},{3,11}... | collective-permute-start | bytes 786440 | tf_op jit(solution)/shard_map/ppermute | solution.py:58
  70.0 7.9 %collective-permute-start.9 = (bf16[512,512]{1,0:T(8,128)(2,1)S(1)}, bf16[512,512]{1,0:T(8,128)(2,1)S(1)}, u32[]{:S(2)}, u32[]{:S(2)}) collective-permute-start(bf16[512,512]{1,0:T(8,128)(2,1)S(1)} %broadcast_select_fusion.2.refs_0_), channel_id=1, source_target_pairs={{0,2},{2,0},{1,3},{3,1},{4,6},{6,4},{5,7},{7,5},{8,10},{10,8},{9,1... | collective-permute-start | bytes 1572872 | tf_op jit(solution)/shard_map/ppermute | solution.py:58
  74.3 5.1 %collective-permute-start.19 = (bf16[256,512]{1,0:T(8,128)(2,1)S(1)}, bf16[256,512]{1,0:T(8,128)(2,1)S(1)}, u32[]{:S(2)}, u32[]{:S(2)}) collective-permute-start(bf16[256,512]{1,0:T(8,128)(2,1)S(1)} %collective-permute-done.17.refs_3_), channel_id=1, source_target_pairs={{0,2},{2,0},{1,3},{3,1},{4,6},{6,4},{5,7},{7,5},{8,10},{10,8},{9,1... | collective-permute-start | bytes 786440 | tf_op jit(solution)/shard_map/ppermute | solution.py:58
  77.1 2.8 %collective-permute-start.18 = (bf16[256,512]{1,0:T(8,128)(2,1)S(1)}, bf16[256,512]{1,0:T(8,128)(2,1)S(1)}, u32[]{:S(2)}, u32[]{:S(2)}) collective-permute-start(bf16[256,512]{1,0:T(8,128)(2,1)S(1)} %collective-permute-done.15.refs_2_), channel_id=1, source_target_pairs={{0,2},{2,0},{1,3},{3,1},{4,6},{6,4},{5,7},{7,5},{8,10},{10,8},{9,1... | collective-permute-start | bytes 786440 | tf_op jit(solution)/shard_map/ppermute | solution.py:58
  77.2 5.0 %collective-permute-start.22 = (bf16[256,512]{1,0:T(8,128)(2,1)S(1)}, bf16[256,512]{1,0:T(8,128)(2,1)S(1)}, u32[]{:S(2)}, u32[]{:S(2)}) collective-permute-start(bf16[256,512]{1,0:T(8,128)(2,1)S(1)} %get-tuple-element.64.refs_1_), channel_id=1, source_target_pairs={{0,2},{2,0},{1,3},{3,1},{4,6},{6,4},{5,7},{7,5},{8,10},{10,8},{9,1... | collective-permute-start | bytes 786440 | tf_op jit(solution)/shard_map/ppermute | solution.py:58
  77.8 4.5 %collective-permute-start.21 = (bf16[256,512]{1,0:T(8,128)(2,1)S(1)}, bf16[256,512]{1,0:T(8,128)(2,1)S(1)}, u32[]{:S(2)}, u32[]{:S(2)}) collective-permute-start(bf16[256,512]{1,0:T(8,128)(2,1)S(1)} %get-tuple-element.65.refs_0_), channel_id=1, source_target_pairs={{0,2},{2,0},{1,3},{3,1},{4,6},{6,4},{5,7},{7,5},{8,10},{10,8},{9,1... | collective-permute-start | bytes 786440 | tf_op jit(solution)/shard_map/ppermute | solution.py:58
  77.9 6.5 %collective-permute-start.23 = (bf16[256,512]{1,0:T(8,128)(2,1)S(1)}, bf16[256,512]{1,0:T(8,128)(2,1)S(1)}, u32[]{:S(2)}, u32[]{:S(2)}) collective-permute-start(bf16[256,512]{1,0:T(8,128)(2,1)S(1)} %get-tuple-element.64.refs_1_), channel_id=1, source_target_pairs={{2,6},{6,2},{10,14},{14,10},{18,22},{22,18},{26,30},{30,26},{3,7},... | collective-permute-start | bytes 786440 | tf_op jit(solution)/shard_map/ppermute | solution.py:58
  79.4 7.7 %collective-permute-start.20 = (bf16[256,512]{1,0:T(8,128)(2,1)S(1)}, bf16[256,512]{1,0:T(8,128)(2,1)S(1)}, u32[]{:S(2)}, u32[]{:S(2)}) collective-permute-start(bf16[256,512]{1,0:T(8,128)(2,1)S(1)} %get-tuple-element.65.refs_0_), channel_id=1, source_target_pairs={{2,6},{6,2},{10,14},{14,10},{18,22},{22,18},{26,30},{30,26},{3,7},... | collective-permute-start | bytes 786440 | tf_op jit(solution)/shard_map/ppermute | solution.py:58
  (12 other events, 46.7 us)

commit v4 on v3

--- a/solution.py
+++ b/solution.py
@@ -125,7 +125,7 @@
 
 
 def solve_first(flags, share, far, inverse, start):
-    half, n = inverse.shape
+    half, n = inverse.shape[1:]
 
     def kernel(flags, cur, got, inv, out):
         @pl.when(flags[0] == 0)
@@ -133,60 +133,80 @@
             for t in range(0, half, TILE):
                 here = cur[:, start + t : start + t + TILE]
                 fan = (here.astype(F32) + got[:, t : t + TILE].astype(F32)).astype(BF)
-                out[:, t : t + TILE] = dot(inv[...], fan).astype(BF)
+                out[:, t : t + TILE] = dot(inv[0], fan).astype(BF)
 
     return call(
         kernel, (flags, share, far, inverse), jax.ShapeDtypeStruct((half, half), BF), [SMEM] + [VMEM] * 3, VMEM
     )
 
 
-def second_block(flags, share, scale, panel, solved, matrix, start):
-    half, n = matrix.shape
-
-    def kernel(flags, cur, scl, pan, sol, mat, own, message):
+def second_block(flags, share, scale, panel, solved, inverse, far_top, far_bottom, start):
+    half, n = inverse.shape[1:]
+    quarter = half // 2
+
+    def kernel(flags, cur, scl, pan, sol, inv, top, bottom, own, message):
         @pl.when(flags[0] == 1)
         def _():
+            factor = column(scl[...], 0)
             for t in range(0, half, TILE):
                 cols = slice(t, t + TILE)
                 here = cur[:, start + t : start + t + TILE]
-                newer = (here.astype(F32) - scl[:, 0:1] * dot(pan[...], sol[:, cols])).astype(BF)
-                product = dot(mat[...], newer).astype(BF)
-                upper = flags[1] == 0
-                own[:, cols] = jnp.where(upper, newer[:half], product)
-                message[:, cols] = jnp.where(upper, product, newer[:half])
-
-    return call(
-        kernel,
-        (flags, share, scale, panel, solved, matrix),
+                newer = (here.astype(F32) - factor * dot(pan[...], sol[:, cols])).astype(BF)
+
+                @pl.when(flags[1] == 0)
+                def _():
+                    own[:, cols] = newer[:half]
+                    message[:quarter, cols] = dot(top[...], newer).astype(BF)
+                    message[quarter:, cols] = dot(bottom[...], newer).astype(BF)
+
+                @pl.when(flags[1] != 0)
+                def _():
+                    own[:, cols] = dot(inv[1], newer).astype(BF)
+                    message[:, cols] = newer[:half]
+
+    return call(
+        kernel,
+        (flags, share, scale, panel, solved, inverse, far_top, far_bottom),
         [jax.ShapeDtypeStruct((half, half), BF)] * 2,
+        [SMEM] + [VMEM] * 7,
+        [VMEM] * 2,
+    )
+
+
+def solve_second(flags, right, left, inverse):
+    half, n = inverse.shape[1:]
+    quarter = half // 2
+
+    def kernel(flags, a0, b0, a1, b1, inv, upper, lower, both):
+        def one(a, b):
+            both[...] = (a[...].astype(F32) + b[...].astype(F32)).astype(BF)
+
+        pl.when(flags[0] == 1)(lambda: one(a0, b0))
+        pl.when(flags[0] == 3)(lambda: one(a1, b1))
+        here = jnp.logical_or(flags[0] == 1, flags[0] == 3)
+
+        @pl.when(jnp.logical_and(flags[1] == 0, here))
+        def _():
+            upper[...] = dot(inv[1, :quarter, :half], both[...]).astype(BF)
+            lower[...] = dot(inv[1, quarter:, :half], both[...]).astype(BF)
+
+        @pl.when(jnp.logical_and(flags[1] != 0, here))
+        def _():
+            upper[...] = both[:quarter]
+            lower[...] = both[quarter:]
+
+    return call(
+        kernel,
+        (flags, *right, *left, inverse),
+        [jax.ShapeDtypeStruct((quarter, half), BF)] * 2,
         [SMEM] + [VMEM] * 5,
         [VMEM] * 2,
-    )
-
-
-def solve_second(flags, right, left, inverse):
-    half, n = inverse.shape
-
-    def kernel(flags, a0, b0, a1, b1, inv, out):
-        def one(a, b):
-            out[...] = (a[...].astype(F32) + b[...].astype(F32)).astype(BF)
-
-        pl.when(flags[0] == 1)(lambda: one(a0, b0))
-        pl.when(flags[0] == 3)(lambda: one(a1, b1))
-
-        @pl.when(jnp.logical_and(flags[1] == 0, jnp.logical_or(flags[0] == 1, flags[0] == 3)))
-        def _():
-            for t in range(0, half, TILE):
-                cols = slice(t, t + TILE)
-                out[:, cols] = dot(inv[:, :half], out[:, cols]).astype(BF)
-
-    return call(
-        kernel,
-        (flags, *right, *left, inverse),
-        jax.ShapeDtypeStruct((half, half), BF),
-        [SMEM] + [VMEM] * 5,
-        VMEM,
-    )
+        [pltpu.VMEM((half, half), BF)],
+    )
+
+
+def column(scale, which):
+    return jnp.transpose(jnp.concatenate([scale] * 4))[:, which : which + 1]
 
 
 def gather(pieces, target):
@@ -212,12 +232,13 @@
         ]
         for copy in copies:
             copy.start()
+        factor = column(scl[...], 0)
         for s in range(2):
             cols = slice(s * half, (s + 1) * half)
             for t in range(0, n, TILE):
                 rows = slice(t, t + TILE)
                 old = cur[rows, cols]
-                newer = (old.astype(F32) - scl[rows, 0:1] * dot(pan[rows], sol[s])).astype(BF)
+                newer = (old.astype(F32) - factor[rows] * dot(pan[rows], sol[s])).astype(BF)
                 out[rows, cols] = jnp.where(flags[0] > 0, newer, old)
         for copy in copies:
             copy.wait()
@@ -246,10 +267,11 @@
         pl.when(flags[3] != 1)(lambda: gather(theirs, sol))
         copies = [pltpu.make_async_copy(sol, solved.at[1, :, cols], sems.at[steps])]
         copies[0].start()
+        factor = column(scl[...], 1)
         for i in range(steps):
             rows = slice(i * TILE, (i + 1) * TILE)
             old = cur[rows, cols]
-            newer = (old.astype(F32) - scl[rows, 1:2] * dot(pan[rows], sol[...])).astype(BF)
+            newer = (old.astype(F32) - factor[rows] * dot(pan[rows], sol[...])).astype(BF)
             tile[rows] = jnp.where(flags[0] > 1, newer, old)
             copy = pltpu.make_async_copy(tile.at[rows], out.at[rows, cols], sems.at[i])
             copy.start()
@@ -282,57 +304,63 @@
     flipped = jnp.stack([row, c, 1 - x, k]).astype(jnp.int32)
     roots = [((0, 0, 0, 0), (0, 1, 0, 0))]
     seconds = [((0, 0, 0, 1), (0, 1, 0, 1))]
-    share, flags, flipped, upper, near, middle, odd, first_core = lax.optimization_barrier(
-        (pending[:, 0, :], flags, flipped, c == 0, x == 0, z == 2, (z & 1) == 1, k == 0)
+    share, flags, flipped, near, middle, odd, outer, first_core = lax.optimization_barrier(
+        (pending[:, 0, :], flags, flipped, x == 0, z == 2, (z & 1) == 1, z == 3, k == 0)
     )
 
     left = columns(share, 0)
     far_left = swap_some(left, roots)
     later, inverse = lax.optimization_barrier((share, inverse_blocks, left))[:2]
-    inv1 = jnp.where(near, inverse[1, quarter:], inverse[1, :quarter])
-    crossed = swap_some(inv1, [((1, 0, 0, 1), (1, 1, 0, 1)), ((0, 0, 1, 0), (0, 1, 1, 0))])
+    rows = jnp.where(near, inverse[1, quarter:], inverse[1, :quarter])
+    crossed = send(rows, [((1, 1, 0, 1), (1, 0, 0, 1)), ((0, 1, 1, 1), (0, 0, 1, 1))])
     panel0, panel1, later = lax.optimization_barrier((panel[:, 0, :], panel[:, 1, :], later))
     far_right = swap_some(columns(later, half), roots)
-    matrix_top = send(
-        crossed,
-        [((1, c_, 0, 1), (0, c_, 0, 1)) for c_ in COLS] + [((0, c_, 1, 0), (0, c_, 0, 0)) for c_ in COLS],
-    )
-    inv0, inv1, scale = inverse[0], inverse[1], panel_scale
-
-    first_left = solve_first(flags, share, far_left, inv0, 0)
+    far_top = send(crossed, [((1, 0, 0, 1), (0, 0, 0, 1))])
+    far_bottom = send(crossed, [((0, 0, 1, 1), (0, 0, 0, 1))])
+    scale = panel_scale.T
+
+    first_left = solve_first(flags, share, far_left, inverse, 0)
     left_here = core_swap(first_left)
     first_hop = swap_some(first_left, [((0, c_, 0, 0), (1, c_, 0, 0)) for c_ in COLS])
-    matrix_bottom = core_swap(after(matrix_top, first_left))
-    matrix = jnp.where(upper, jnp.concatenate([matrix_top, matrix_bottom]), inv1)
-    own, message = second_block(flags, share, scale, panel0, left_here, matrix, 0)
-    own_hop = send(own, [((0, c_, 0, 1), (1, c_, 0, 1)) for c_ in COLS])
-    message_hop = send(message, [((0, c_, 0, 1), (1, 1 - c_, 0, 1)) for c_ in COLS])
-
-    first_right = solve_first(flags, share, after(far_right, own), inv0, half)
-    right_here = core_swap(first_right)
+    far_top, far_bottom = lax.optimization_barrier((far_top, far_bottom, first_left))[:2]
+    own, message = second_block(flags, share, scale, panel0, left_here, inverse, far_top, far_bottom, 0)
+
+    first_right = solve_first(flags, share, after(far_right, own, first_hop), inverse, half)
+    inward = send(
+        jnp.where(first_core, first_right, own),
+        [((0, c_, 0, 0), (0, c_, 0, 1)) for c_ in COLS] + [((0, c_, 0, 1), (1, c_, 0, 1)) for c_ in COLS],
+    )
     mine0 = jnp.where(near, first_right, first_hop)
-    got0 = swap_some(mine0, far_step(0))
-    own, message = second_block(flags, share, scale, panel0, right_here, matrix, half)
-    answer = swap_some(message, seconds)
-
-    mine0 = jnp.where(middle, got0, mine0)
-    got0 = swap_some(mine0, near_step(0))
-
-    second = solve_second(flags, (own, after(answer, mine0)), (own_hop, message_hop), inv1)
+    across = send(
+        jnp.where(first_core, mine0, message),
+        [((x_, c_, 0, 0), (x_, c_, 2, 0)) for x_ in (0, 1) for c_ in COLS]
+        + [((0, c_, 0, 1), (1, 1 - c_, 0, 1)) for c_ in COLS],
+    )
+    own, message = second_block(flags, share, scale, panel0, inward, inverse, far_top, far_bottom, half)
+    answer = send(
+        jnp.where(first_core, mine0, message),
+        [((x_, c_, 0, 0), (x_, c_, 1, 0)) for x_ in (0, 1) for c_ in COLS]
+        + [((0, c_, 0, 1), (0, 1 - c_, 0, 1)) for c_ in COLS],
+    )
+    last = send(after(across, message), [((x_, c_, 2, 0), (x_, c_, 3, 0)) for x_ in (0, 1) for c_ in COLS])
+
+    second = solve_second(flags, (own, answer), (inward, across), inverse)
 
     rows = [slice(0, quarter), slice(quarter, half)]
-    heads = [second[r] for r in rows]
-    far = [swap(h, far_step(1), "y") for h in heads]
-    mine0 = jnp.where(odd, got0, mine0)
-    heads = [jnp.where(middle, f, h) for f, h in zip(far, heads)]
-    step = [
-        swap(jnp.where(first_core, mine0[r], h), near_step(1) + side_step(0), "y") for h, r in zip(heads, rows)
-    ]
-    mine1 = [jnp.where(odd, s, h) for s, h in zip(step, heads)]
-    other1 = [swap(m, side_step(1), "y") for m in mine1]
+    mine0 = jnp.where(odd, jnp.where(outer, last, answer), jnp.where(middle, across, mine0))
+    far = [swap(part, far_step(1), "y") for part in second]
+    heads, step, mine1, other1 = [], [], [], []
+    for part, r, head in zip(far, rows, second):
+        heads.append(jnp.where(middle, after(part, *heads), head))
+        step.append(swap(jnp.where(first_core, mine0[r], heads[-1]), near_step(1) + side_step(0), "y"))
+    for part, head in zip(step, heads):
+        mine1.append(jnp.where(odd, after(part, *mine1), head))
+        other1.append(swap(mine1[-1], side_step(1), "y"))
+    mine0_here = core_swap(mine0)
+    step_here = [core_swap(s) for s in step]
 
     current, solved = update_first(
-        flags, share, scale, panel0, ([mine0], [core_swap(mine0)]), (step, [core_swap(s) for s in step])
+        flags, share, scale, panel0, ([mine0], [mine0_here]), (step, step_here)
     )
     remaining, solved = update_second(flipped, current, scale, panel1, mine1, [core_swap(m) for m in mine1], solved)
     other1 = [after(m, remaining) for m in other1]

time: 91.5 us -> 82.3 us (0.90)
  other arithmetic: 3.67 us -> 0.7 us
  starting transfers between devices: 25.5 us -> 23.3 us
  local copies, waits for them, and re-layouts: 7.98 us -> 6.16 us
  Pallas kernels: 13.3 us -> 11.9 us
    ppermute x7 -> x3, waiting for transfers between devices: 22.4 us -> 12.5 us  [swap_some(): lax.ppermute(value, AXES, [(device(*p), device(*q)) for a, b in wanted fo...]
    ppermute x3 -> x7, waiting for transfers between devices: 5.66 us -> 11.7 us  [send(): lax.ppermute(value, AXES, [(device(*a), device(*b)) for a, b in wanted])]
    ppermute x7 -> x3, starting transfers between devices: 14.2 us -> 8.98 us  [swap_some(): lax.ppermute(value, AXES, [(device(*p), device(*q)) for a, b in wanted fo...]
    ppermute x3 -> x7, starting transfers between devices: 2.68 us -> 6.73 us  [send(): lax.ppermute(value, AXES, [(device(*a), device(*b)) for a, b in wanted])]
    ppermute x16 -> x14, waiting for transfers between devices: 11.5 us -> 14.7 us  [swap(): return lax.ppermute(value, AXES, paired(wanted, side))]
    select_n x7 -> x9, other arithmetic: 3.59 us -> 0.62 us  [the longest x2 0.15 us: body(): jnp.where(first_core, mine0, message)]
    pallas_call x10, Pallas kernels: 13.3 us -> 11.9 us  [call(): pl.pallas_call(kernel, in_specs=ins, out_specs=outs, out_shape=shapes, sc...]
    squeeze x1, local copies, waits for them, and re-layouts: 1.93 us -> 0.61 us  [body(): panel[:, 1, :]]
  transfers between devices with their start and end apart: 26 -> 24, of which waited for: 12 -> 13; matrix products, arithmetic and copies ran while one was open for 11% -> 5% of each run, Pallas kernels for 12% -> 9%
where the time goes in v4:
time: 82.3 us; the launch traced here: 81.9 us
  waiting for transfers between devices  38.9 us (47%)
  starting transfers between devices  23.3 us (28%)
  Pallas kernels  11.9 us (14%)
  local copies, waits for them, and re-layouts  6.16 us (7%)
  between operations  0.98 us (1%)
    ppermute x14, waiting for transfers between devices, swap(): return lax.ppermute(value, AXES, paired(wanted, side))  14.7 us
    ppermute x3, waiting for transfers between devices, swap_some(): lax.ppermute(value, AXES, [(device(*p), device(*q)) for a, b in wanted fo...  12.5 us
    pallas_call x10, Pallas kernels, call(): pl.pallas_call(kernel, in_specs=ins, out_specs=outs, out_shape=shapes, sc...  11.9 us
    ppermute x7, waiting for transfers between devices, send(): lax.ppermute(value, AXES, [(device(*a), device(*b)) for a, b in wanted])  11.7 us
    ppermute x3, starting transfers between devices, swap_some(): lax.ppermute(value, AXES, [(device(*p), device(*q)) for a, b in wanted fo...  8.98 us
    ppermute x14, starting transfers between devices, swap(): return lax.ppermute(value, AXES, paired(wanted, side))  7.62 us
    ppermute x7, starting transfers between devices, send(): lax.ppermute(value, AXES, [(device(*a), device(*b)) for a, b in wanted])  6.73 us
    slice x1, local copies, waits for them, and re-layouts, body(): panel[:, 1, :]  2.98 us
  transfers between devices with their start and end apart: 24, of which 13 were waited for; matrix products, arithmetic and copies ran while one was open for 5% of the time, Pallas kernels for 9%

profile of v4, /device:TPU:0, one launch (start us, length us, event | category | flops | bytes accessed | tf_op | source)
XLA Modules:
  0.0 81.9 jit_solution(8867895144707506722)
XLA Ops:
  0.7 1.6 %copy-done = bf16[1024,1,1024]{2,0,1:T(8,128)(2,1)S(1)} copy-done((bf16[1024,1,1024]{2,0,1:T(8,128)(2,1)S(1)}, bf16[1024,1,1024]{2,0,1:T(8,128)(2,1)}, u32[]{:S(2)}) %copy-start) | copy-done | bytes 2097176
  2.4 5.1 %collective-permute-start.1 = (bf16[1024,512]{1,0:T(8,128)(2,1)S(1)}, bf16[1024,512]{1,0:T(8,128)(2,1)S(1)}, u32[]{:S(2)}, u32[]{:S(2)}) collective-permute-start(bf16[1024,512]{1,0:T(8,128)(2,1)S(1)} %shard_map.59), channel_id=1, source_target_pairs={{0,1},{1,0}} | collective-permute-start | bytes 3145736 | tf_op jit(solution)/shard_map/ppermute | solution.py:62
  8.4 3.0 %fusion = (bf16[1024,1,512]{2,1,0:T(2,128)(2,1)S(1)}, bf16[1024,1,512]{2,1,0:T(2,128)(2,1)S(1)}) fusion(bf16[1024,2,512]{2,1,0:T(2,128)(2,1)S(1)} %copy-done.4), kind=kLoop, calls=%fused_computation.17 | loop fusion | bytes 4194304 | tf_op jit(solution)/shard_map/slice | solution.py:316
  13.1 1.9 %collective-permute-start = (bf16[1024,512]{1,0:T(8,128)(2,1)S(1)}, bf16[1024,512]{1,0:T(8,128)(2,1)S(1)}, u32[]{:S(2)}, u32[]{:S(2)}) collective-permute-start(bf16[1024,512]{1,0:T(8,128)(2,1)S(1)} %shard_map.60), channel_id=1, source_target_pairs={{0,1},{1,0}} | collective-permute-start | bytes 3145736 | tf_op jit(solution)/shard_map/ppermute | solution.py:62
  16.4 3.9 %collective-permute-done.1.got = bf16[1024,512]{1,0:T(8,128)(2,1)S(1)} collective-permute-done((bf16[1024,512]{1,0:T(8,128)(2,1)S(1)}, bf16[1024,512]{1,0:T(8,128)(2,1)S(1)}, u32[]{:S(2)}, u32[]{:S(2)}) %collective-permute-start.1) | collective-permute-done | bytes 1048608 | tf_op jit(solution)/shard_map/ppermute | solution.py:62
  20.4 1.3 %shard_map.61 = bf16[512,512]{1,0:T(8,128)(2,1)S(1)} custom-call(s32[4]{0:T(128)S(1)} %get-tuple-element.35.flags, bf16[1024,1024]{1,0:T(8,128)(2,1)S(1)} %bitcast.16, bf16[1024,512]{1,0:T(8,128)(2,1)S(1)} %collective-permute-done.1.got, bf16[2,512,1024]{2,1,0:T(8,128)(2,1)S(1)} %copy-done.2), custom_call_target="tpu_custom_call" | custom-call | tf_op jit(solution)/shard_map/pallas_call | solution.py:94
  21.7 1.9 %collective-permute-start.6 = (bf16[512,512]{1,0:T(8,128)(2,1)S(1)}, bf16[512,512]{1,0:T(8,128)(2,1)S(1)}, u32[]{:S(2)}, u32[]{:S(2)}) collective-permute-start(bf16[512,512]{1,0:T(8,128)(2,1)S(1)} %shard_map.61), channel_id=1, source_target_pairs={{0,4},{4,0},{1,5},{5,1}} | collective-permute-start | bytes 1572872 | tf_op jit(solution)/shard_map/ppermute | solution.py:62
  24.3 7.3 %collective-permute-done.got = bf16[1024,512]{1,0:T(8,128)(2,1)S(1)} collective-permute-done((bf16[1024,512]{1,0:T(8,128)(2,1)S(1)}, bf16[1024,512]{1,0:T(8,128)(2,1)S(1)}, u32[]{:S(2)}, u32[]{:S(2)}) %collective-permute-start) | collective-permute-done | bytes 1048608 | tf_op jit(solution)/shard_map/ppermute | solution.py:62
  32.8 1.3 %shard_map.63 = bf16[512,512]{1,0:T(8,128)(2,1)S(1)} custom-call(s32[4]{0:T(128)S(1)} %get-tuple-element.35.flags, bf16[1024,1024]{1,0:T(8,128)(2,1)S(1)} %bitcast.18, bf16[1024,512]{1,0:T(8,128)(2,1)S(1)} %collective-permute-done.got, bf16[2,512,1024]{2,1,0:T(8,128)(2,1)S(1)} %copy-done.2), custom_call_target="tpu_custom_call" | custom-call | tf_op jit(solution)/shard_map/pallas_call | solution.py:94
  34.2 1.3 %collective-permute-start.8 = (bf16[512,512]{1,0:T(8,128)(2,1)S(1)}, bf16[512,512]{1,0:T(8,128)(2,1)S(1)}, u32[]{:S(2)}, u32[]{:S(2)}) collective-permute-start(bf16[512,512]{1,0:T(8,128)(2,1)S(1)} %broadcast_select_fusion.2), channel_id=1, source_target_pairs={{0,2},{1,3},{2,6},{3,7}} | collective-permute-start | bytes 1572872 | tf_op jit(solution)/shard_map/ppermute | solution.py:66
  35.5 1.5 %collective-permute-done.8.sol.a1 = bf16[512,512]{1,0:T(8,128)(2,1)S(1)} collective-permute-done((bf16[512,512]{1,0:T(8,128)(2,1)S(1)}, bf16[512,512]{1,0:T(8,128)(2,1)S(1)}, u32[]{:S(2)}, u32[]{:S(2)}) %collective-permute-start.8) | collective-permute-done | bytes 524320 | tf_op jit(solution)/shard_map/ppermute | solution.py:66
  37.7 1.3 %collective-permute-start.7 = (bf16[512,512]{1,0:T(8,128)(2,1)S(1)}, bf16[512,512]{1,0:T(8,128)(2,1)S(1)}, u32[]{:S(2)}, u32[]{:S(2)}) collective-permute-start(bf16[512,512]{1,0:T(8,128)(2,1)S(1)} %broadcast_select_fusion.3), channel_id=1, source_target_pairs={{0,16},{1,17},{4,20},{5,21},{2,7},{3,6}} | collective-permute-start | bytes 1572872 | tf_op jit(solution)/shard_map/ppermute | solution.py:66
  39.0 1.3 %collective-permute-start.10 = (bf16[512,512]{1,0:T(8,128)(2,1)S(1)}, bf16[512,512]{1,0:T(8,128)(2,1)S(1)}, u32[]{:S(2)}, u32[]{:S(2)}) collective-permute-start(bf16[512,512]{1,0:T(8,128)(2,1)S(1)} %get-tuple-element.70), channel_id=1, source_target_pairs={{0,8},{1,9},{4,12},{5,13},{2,3},{3,2}} | collective-permute-start | bytes 1572872 | tf_op jit(solution)/shard_map/ppermute | solution.py:66
  40.4 5.3 %collective-permute-done.7.b1 = bf16[512,512]{1,0:T(8,128)(2,1)S(1)} collective-permute-done((bf16[512,512]{1,0:T(8,128)(2,1)S(1)}, bf16[512,512]{1,0:T(8,128)(2,1)S(1)}, u32[]{:S(2)}, u32[]{:S(2)}) %collective-permute-start.7) | collective-permute-done | bytes 524320 | tf_op jit(solution)/shard_map/ppermute | solution.py:66
  46.4 4.9 %collective-permute-done.10.b0 = bf16[512,512]{1,0:T(8,128)(2,1)S(1)} collective-permute-done((bf16[512,512]{1,0:T(8,128)(2,1)S(1)}, bf16[512,512]{1,0:T(8,128)(2,1)S(1)}, u32[]{:S(2)}, u32[]{:S(2)}) %collective-permute-start.10) | collective-permute-done | bytes 524320 | tf_op jit(solution)/shard_map/ppermute | solution.py:66
  51.9 2.1 %collective-permute-start.12 = (bf16[256,512]{1,0:T(8,128)(2,1)S(1)}, bf16[256,512]{1,0:T(8,128)(2,1)S(1)}, u32[]{:S(2)}, u32[]{:S(2)}) collective-permute-start(bf16[256,512]{1,0:T(8,128)(2,1)S(1)} %get-tuple-element.54), channel_id=1, source_target_pairs={{2,18},{18,2},{6,22},{22,6},{3,19},{19,3},{7,23},{23,7},{0,1},{1,0... | collective-permute-start | bytes 786440 | tf_op jit(solution)/shard_map/ppermute | solution.py:58
  54.0 4.3 %collective-permute-done.12 = bf16[256,512]{1,0:T(8,128)(2,1)S(1)} collective-permute-done((bf16[256,512]{1,0:T(8,128)(2,1)S(1)}, bf16[256,512]{1,0:T(8,128)(2,1)S(1)}, u32[]{:S(2)}, u32[]{:S(2)}) %collective-permute-start.12) | collective-permute-done | bytes 262176 | tf_op jit(solution)/shard_map/ppermute | solution.py:58
  58.6 2.5 %collective-permute-done.14 = bf16[256,512]{1,0:T(8,128)(2,1)S(1)} collective-permute-done((bf16[256,512]{1,0:T(8,128)(2,1)S(1)}, bf16[256,512]{1,0:T(8,128)(2,1)S(1)}, u32[]{:S(2)}, u32[]{:S(2)}) %collective-permute-start.14) | collective-permute-done | bytes 262176 | tf_op jit(solution)/shard_map/ppermute | solution.py:58
  62.3 2.6 %collective-permute-done.13.refs_2_ = bf16[256,512]{1,0:T(8,128)(2,1)S(1)} collective-permute-done((bf16[256,512]{1,0:T(8,128)(2,1)S(1)}, bf16[256,512]{1,0:T(8,128)(2,1)S(1)}, u32[]{:S(2)}, u32[]{:S(2)}) %collective-permute-start.13) | collective-permute-done | bytes 262176 | tf_op jit(solution)/shard_map/ppermute | solution.py:58
  65.2 2.6 %collective-permute-done.15.refs_3_ = bf16[256,512]{1,0:T(8,128)(2,1)S(1)} collective-permute-done((bf16[256,512]{1,0:T(8,128)(2,1)S(1)}, bf16[256,512]{1,0:T(8,128)(2,1)S(1)}, u32[]{:S(2)}, u32[]{:S(2)}) %collective-permute-start.15) | collective-permute-done | bytes 262176 | tf_op jit(solution)/shard_map/ppermute | solution.py:58
  68.7 2.0 %collective-permute-start.21 = (bf16[256,512]{1,0:T(8,128)(2,1)S(1)}, bf16[256,512]{1,0:T(8,128)(2,1)S(1)}, u32[]{:S(2)}, u32[]{:S(2)}) collective-permute-start(bf16[256,512]{1,0:T(8,128)(2,1)S(1)} %broadcast_select_fusion.4.refs_1_), channel_id=1, source_target_pairs={{2,6},{6,2},{10,14},{14,10},{18,22},{22,18},{26,30},{30,26},{3,7},... | collective-permute-start | bytes 786440 | tf_op jit(solution)/shard_map/ppermute | solution.py:58
  71.3 3.0 %shard_map.66 = (bf16[1024,1024]{1,0:T(8,128)(2,1)S(1)}, bf16[2,512,1024]{2,1,0:T(8,128)(2,1)}) custom-call(s32[4]{0:T(128)S(1)} %get-tuple-element.35.flags, bf16[1024,1024]{1,0:T(8,128)(2,1)S(1)} %bitcast.20, f32[2,1024]{1,0:T(2,128)S(1)} %bitcast.23, bf16[1024,512]{1,0:T(8,128)(2,1)S(1)} %get-tuple-element.38.pan, ...), custom_call_target="tpu_custom_call" | custom-call | tf_op jit(solution)/shard_map/pallas_call | solution.py:94
  74.4 2.2 %shard_map.67 = (bf16[1024,1024]{1,0:T(8,128)(2,1)}, bf16[2,512,1024]{2,1,0:T(8,128)(2,1)}) custom-call(s32[4]{0:T(128)S(1)} %get-tuple-element.59.flags, bf16[1024,1024]{1,0:T(8,128)(2,1)S(1)} %get-tuple-element.57.cur, f32[2,1024]{1,0:T(2,128)S(1)} %bitcast.24, bf16[1024,512]{1,0:T(8,128)(2,1)S(1)} %get-tuple-element.58.pan, ...), custom_call_target="tpu_custom_call", output_to_operand_aliasing={{1}: (8, {})} | custom-call | tf_op jit(solution)/shard_map/pallas_call | solution.py:94
  79.7 2.2 %shard_map.68 = (bf16[1024,1024]{1,0:T(8,128)(2,1)}, bf16[2,512,1024]{2,1,0:T(8,128)(2,1)}) custom-call(s32[4]{0:T(128)S(1)} %get-tuple-element.35.flags, bf16[1024,1024]{1,0:T(8,128)(2,1)S(1)} %get-tuple-element.57.cur, f32[2,1024]{1,0:T(2,128)S(1)} %bitcast.25, ...), custom_call_target="tpu_custom_call", output_to_operand_aliasing={{1}: (8, {}), {0}: (9, {})} | custom-call | tf_op jit(solution)/shard_map/pallas_call | solution.py:94
  (56 shorter events, 14.4 us)
Async XLA Ops:
  2.4 17.9 %collective-permute-start.1 = (bf16[1024,512]{1,0:T(8,128)(2,1)S(1)}, bf16[1024,512]{1,0:T(8,128)(2,1)S(1)}, u32[]{:S(2)}, u32[]{:S(2)}) collective-permute-start(bf16[1024,512]{1,0:T(8,128)(2,1)S(1)} %shard_map.59), channel_id=1, source_target_pairs={{0,1},{1,0}} | collective-permute-start | bytes 3145736 | tf_op jit(solution)/shard_map/ppermute | solution.py:62
  7.7 7.4 %collective-permute-start.3 = (bf16[256,1024]{1,0:T(8,128)(2,1)S(1)}, bf16[256,1024]{1,0:T(8,128)(2,1)S(1)}, u32[]{:S(2)}, u32[]{:S(2)}) collective-permute-start(bf16[256,1024]{1,0:T(8,128)(2,1)S(1)} %select_bitcast_fusion), channel_id=1, source_target_pairs={{7,6},{11,10}} | collective-permute-start | bytes 1572872 | tf_op jit(solution)/shard_map/ppermute | solution.py:66
  13.1 18.5 %collective-permute-start = (bf16[1024,512]{1,0:T(8,128)(2,1)S(1)}, bf16[1024,512]{1,0:T(8,128)(2,1)S(1)}, u32[]{:S(2)}, u32[]{:S(2)}) collective-permute-start(bf16[1024,512]{1,0:T(8,128)(2,1)S(1)} %shard_map.60), channel_id=1, source_target_pairs={{0,1},{1,0}} | collective-permute-start | bytes 3145736 | tf_op jit(solution)/shard_map/ppermute | solution.py:62
  15.0 8.6 %collective-permute-start.5 = (bf16[256,1024]{1,0:T(8,128)(2,1)S(1)}, bf16[256,1024]{1,0:T(8,128)(2,1)S(1)}, u32[]{:S(2)}, u32[]{:S(2)}) collective-permute-start(bf16[256,1024]{1,0:T(8,128)(2,1)S(1)} %collective-permute-done.3), channel_id=1, source_target_pairs={{10,2}} | collective-permute-start | bytes 1572872 | tf_op jit(solution)/shard_map/ppermute | solution.py:66
  15.7 7.9 %collective-permute-start.4 = (bf16[256,1024]{1,0:T(8,128)(2,1)S(1)}, bf16[256,1024]{1,0:T(8,128)(2,1)S(1)}, u32[]{:S(2)}, u32[]{:S(2)}) collective-permute-start(bf16[256,1024]{1,0:T(8,128)(2,1)S(1)} %collective-permute-done.3), channel_id=1, source_target_pairs={{6,2}} | collective-permute-start | bytes 1572872 | tf_op jit(solution)/shard_map/ppermute | solution.py:66
  21.7 2.0 %collective-permute-start.2 = (bf16[512,512]{1,0:T(8,128)(2,1)S(1)}, bf16[512,512]{1,0:T(8,128)(2,1)S(1)}, u32[]{:S(2)}, u32[]{:S(2)}) collective-permute-start(bf16[512,512]{1,0:T(8,128)(2,1)S(1)} %shard_map.61), channel_id=1, source_target_pairs={{0,2},{2,0},{1,3},{3,1},{4,6},{6,4},{5,7},{7,5},{8,10},{10,8},{9,1... | collective-permute-start | bytes 1572872 | tf_op jit(solution)/shard_map/ppermute | solution.py:58
  21.7 11.1 %collective-permute-start.6 = (bf16[512,512]{1,0:T(8,128)(2,1)S(1)}, bf16[512,512]{1,0:T(8,128)(2,1)S(1)}, u32[]{:S(2)}, u32[]{:S(2)}) collective-permute-start(bf16[512,512]{1,0:T(8,128)(2,1)S(1)} %shard_map.61), channel_id=1, source_target_pairs={{0,4},{4,0},{1,5},{5,1}} | collective-permute-start | bytes 1572872 | tf_op jit(solution)/shard_map/ppermute | solution.py:62
  34.2 2.8 %collective-permute-start.8 = (bf16[512,512]{1,0:T(8,128)(2,1)S(1)}, bf16[512,512]{1,0:T(8,128)(2,1)S(1)}, u32[]{:S(2)}, u32[]{:S(2)}) collective-permute-start(bf16[512,512]{1,0:T(8,128)(2,1)S(1)} %broadcast_select_fusion.2), channel_id=1, source_target_pairs={{0,2},{1,3},{2,6},{3,7}} | collective-permute-start | bytes 1572872 | tf_op jit(solution)/shard_map/ppermute | solution.py:66
  37.7 8.0 %collective-permute-start.7 = (bf16[512,512]{1,0:T(8,128)(2,1)S(1)}, bf16[512,512]{1,0:T(8,128)(2,1)S(1)}, u32[]{:S(2)}, u32[]{:S(2)}) collective-permute-start(bf16[512,512]{1,0:T(8,128)(2,1)S(1)} %broadcast_select_fusion.3), channel_id=1, source_target_pairs={{0,16},{1,17},{4,20},{5,21},{2,7},{3,6}} | collective-permute-start | bytes 1572872 | tf_op jit(solution)/shard_map/ppermute | solution.py:66
  39.0 12.3 %collective-permute-start.10 = (bf16[512,512]{1,0:T(8,128)(2,1)S(1)}, bf16[512,512]{1,0:T(8,128)(2,1)S(1)}, u32[]{:S(2)}, u32[]{:S(2)}) collective-permute-start(bf16[512,512]{1,0:T(8,128)(2,1)S(1)} %get-tuple-element.70), channel_id=1, source_target_pairs={{0,8},{1,9},{4,12},{5,13},{2,3},{3,2}} | collective-permute-start | bytes 1572872 | tf_op jit(solution)/shard_map/ppermute | solution.py:66
  45.7 12.6 %collective-permute-start.9 = (bf16[512,512]{1,0:T(8,128)(2,1)S(1)}, bf16[512,512]{1,0:T(8,128)(2,1)S(1)}, u32[]{:S(2)}, u32[]{:S(2)}) collective-permute-start(bf16[512,512]{1,0:T(8,128)(2,1)S(1)} %collective-permute-done.7.b1), channel_id=1, source_target_pairs={{16,24},{17,25},{20,28},{21,29}} | collective-permute-start | bytes 1572872 | tf_op jit(solution)/shard_map/ppermute | solution.py:66
  51.9 6.4 %collective-permute-start.12 = (bf16[256,512]{1,0:T(8,128)(2,1)S(1)}, bf16[256,512]{1,0:T(8,128)(2,1)S(1)}, u32[]{:S(2)}, u32[]{:S(2)}) collective-permute-start(bf16[256,512]{1,0:T(8,128)(2,1)S(1)} %get-tuple-element.54), channel_id=1, source_target_pairs={{2,18},{18,2},{6,22},{22,6},{3,19},{19,3},{7,23},{23,7},{0,1},{1,0... | collective-permute-start | bytes 786440 | tf_op jit(solution)/shard_map/ppermute | solution.py:58
  54.0 7.2 %collective-permute-start.14 = (bf16[256,512]{1,0:T(8,128)(2,1)S(1)}, bf16[256,512]{1,0:T(8,128)(2,1)S(1)}, u32[]{:S(2)}, u32[]{:S(2)}) collective-permute-start(bf16[256,512]{1,0:T(8,128)(2,1)S(1)} %get-tuple-element.55), channel_id=1, source_target_pairs={{2,18},{18,2},{6,22},{22,6},{3,19},{19,3},{7,23},{23,7},{0,1},{1,0... | collective-permute-start | bytes 786440 | tf_op jit(solution)/shard_map/ppermute | solution.py:58
  58.6 6.4 %collective-permute-start.13 = (bf16[256,512]{1,0:T(8,128)(2,1)S(1)}, bf16[256,512]{1,0:T(8,128)(2,1)S(1)}, u32[]{:S(2)}, u32[]{:S(2)}) collective-permute-start(bf16[256,512]{1,0:T(8,128)(2,1)S(1)} %get-tuple-element.68), channel_id=1, source_target_pairs={{2,10},{10,2},{18,26},{26,18},{6,14},{14,6},{22,30},{30,22},{3,11}... | collective-permute-start | bytes 786440 | tf_op jit(solution)/shard_map/ppermute | solution.py:58
  61.2 6.6 %collective-permute-start.15 = (bf16[256,512]{1,0:T(8,128)(2,1)S(1)}, bf16[256,512]{1,0:T(8,128)(2,1)S(1)}, u32[]{:S(2)}, u32[]{:S(2)}) collective-permute-start(bf16[256,512]{1,0:T(8,128)(2,1)S(1)} %slice_select_fusion), channel_id=1, source_target_pairs={{2,10},{10,2},{18,26},{26,18},{6,14},{14,6},{22,30},{30,22},{3,11}... | collective-permute-start | bytes 786440 | tf_op jit(solution)/shard_map/ppermute | solution.py:58
  61.3 10.1 %collective-permute-start.11 = (bf16[512,512]{1,0:T(8,128)(2,1)S(1)}, bf16[512,512]{1,0:T(8,128)(2,1)S(1)}, u32[]{:S(2)}, u32[]{:S(2)}) collective-permute-start(bf16[512,512]{1,0:T(8,128)(2,1)S(1)} %select_select_fusion.refs_0_), channel_id=1, source_target_pairs={{0,2},{2,0},{1,3},{3,1},{4,6},{6,4},{5,7},{7,5},{8,10},{10,8},{9,1... | collective-permute-start | bytes 1572872 | tf_op jit(solution)/shard_map/ppermute | solution.py:58
  65.0 3.7 %collective-permute-start.16 = (bf16[256,512]{1,0:T(8,128)(2,1)S(1)}, bf16[256,512]{1,0:T(8,128)(2,1)S(1)}, u32[]{:S(2)}, u32[]{:S(2)}) collective-permute-start(bf16[256,512]{1,0:T(8,128)(2,1)S(1)} %collective-permute-done.13.refs_2_), channel_id=1, source_target_pairs={{0,2},{2,0},{1,3},{3,1},{4,6},{6,4},{5,7},{7,5},{8,10},{10,8},{9,1... | collective-permute-start | bytes 786440 | tf_op jit(solution)/shard_map/ppermute | solution.py:58
  67.8 2.8 %collective-permute-start.17 = (bf16[256,512]{1,0:T(8,128)(2,1)S(1)}, bf16[256,512]{1,0:T(8,128)(2,1)S(1)}, u32[]{:S(2)}, u32[]{:S(2)}) collective-permute-start(bf16[256,512]{1,0:T(8,128)(2,1)S(1)} %collective-permute-done.15.refs_3_), channel_id=1, source_target_pairs={{0,2},{2,0},{1,3},{3,1},{4,6},{6,4},{5,7},{7,5},{8,10},{10,8},{9,1... | collective-permute-start | bytes 786440 | tf_op jit(solution)/shard_map/ppermute | solution.py:58
  67.9 6.4 %collective-permute-start.19 = (bf16[256,512]{1,0:T(8,128)(2,1)S(1)}, bf16[256,512]{1,0:T(8,128)(2,1)S(1)}, u32[]{:S(2)}, u32[]{:S(2)}) collective-permute-start(bf16[256,512]{1,0:T(8,128)(2,1)S(1)} %broadcast_select_fusion.5.refs_0_), channel_id=1, source_target_pairs={{0,2},{2,0},{1,3},{3,1},{4,6},{6,4},{5,7},{7,5},{8,10},{10,8},{9,1... | collective-permute-start | bytes 786440 | tf_op jit(solution)/shard_map/ppermute | solution.py:58
  68.5 5.9 %collective-permute-start.20 = (bf16[256,512]{1,0:T(8,128)(2,1)S(1)}, bf16[256,512]{1,0:T(8,128)(2,1)S(1)}, u32[]{:S(2)}, u32[]{:S(2)}) collective-permute-start(bf16[256,512]{1,0:T(8,128)(2,1)S(1)} %broadcast_select_fusion.4.refs_1_), channel_id=1, source_target_pairs={{0,2},{2,0},{1,3},{3,1},{4,6},{6,4},{5,7},{7,5},{8,10},{10,8},{9,1... | collective-permute-start | bytes 786440 | tf_op jit(solution)/shard_map/ppermute | solution.py:58
  68.7 7.9 %collective-permute-start.21 = (bf16[256,512]{1,0:T(8,128)(2,1)S(1)}, bf16[256,512]{1,0:T(8,128)(2,1)S(1)}, u32[]{:S(2)}, u32[]{:S(2)}) collective-permute-start(bf16[256,512]{1,0:T(8,128)(2,1)S(1)} %broadcast_select_fusion.4.refs_1_), channel_id=1, source_target_pairs={{2,6},{6,2},{10,14},{14,10},{18,22},{22,18},{26,30},{30,26},{3,7},... | collective-permute-start | bytes 786440 | tf_op jit(solution)/shard_map/ppermute | solution.py:58
  70.6 7.2 %collective-permute-start.18 = (bf16[256,512]{1,0:T(8,128)(2,1)S(1)}, bf16[256,512]{1,0:T(8,128)(2,1)S(1)}, u32[]{:S(2)}, u32[]{:S(2)}) collective-permute-start(bf16[256,512]{1,0:T(8,128)(2,1)S(1)} %broadcast_select_fusion.5.refs_0_), channel_id=1, source_target_pairs={{2,6},{6,2},{10,14},{14,10},{18,22},{22,18},{26,30},{30,26},{3,7},... | collective-permute-start | bytes 786440 | tf_op jit(solution)/shard_map/ppermute | solution.py:58
  77.8 1.5 %collective-permute-start.22 = (bf16[256,512]{1,0:T(8,128)(2,1)S(1)}, bf16[256,512]{1,0:T(8,128)(2,1)S(1)}, u32[]{:S(2)}, u32[]{:S(2)}) collective-permute-start(bf16[256,512]{1,0:T(8,128)(2,1)S(1)} %collective-permute-done.18.refs_0_), channel_id=1, source_target_pairs={{0,2},{2,0},{1,3},{3,1},{4,6},{6,4},{5,7},{7,5},{8,10},{10,8},{9,1... | collective-permute-start | bytes 786440 | tf_op jit(solution)/shard_map/ppermute | solution.py:58
  77.8 1.9 %collective-permute-start.23 = (bf16[256,512]{1,0:T(8,128)(2,1)S(1)}, bf16[256,512]{1,0:T(8,128)(2,1)S(1)}, u32[]{:S(2)}, u32[]{:S(2)}) collective-permute-start(bf16[256,512]{1,0:T(8,128)(2,1)S(1)} %collective-permute-done.21.refs_1_), channel_id=1, source_target_pairs={{0,2},{2,0},{1,3},{3,1},{4,6},{6,4},{5,7},{7,5},{8,10},{10,8},{9,1... | collective-permute-start | bytes 786440 | tf_op jit(solution)/shard_map/ppermute | solution.py:58
  (5 other events, 25.1 us)

commit v5 on v4

--- a/solution.py
+++ b/solution.py
@@ -147,11 +147,10 @@
     def kernel(flags, cur, scl, pan, sol, inv, top, bottom, own, message):
         @pl.when(flags[0] == 1)
         def _():
-            factor = column(scl[...], 0)
             for t in range(0, half, TILE):
                 cols = slice(t, t + TILE)
                 here = cur[:, start + t : start + t + TILE]
-                newer = (here.astype(F32) - factor * dot(pan[...], sol[:, cols])).astype(BF)
+                newer = (here.astype(F32) - scl[...] * dot(pan[...], sol[:, cols])).astype(BF)
 
                 @pl.when(flags[1] == 0)
                 def _():
@@ -205,8 +204,15 @@
     )
 
 
-def column(scale, which):
-    return jnp.transpose(jnp.concatenate([scale] * 4))[:, which : which + 1]
+def scale_columns(scale):
+    n = scale.shape[1]
+
+    def kernel(scl, first, second):
+        both = jnp.transpose(jnp.concatenate([scl[...]] * 4))
+        first[...] = both[:, 0:1]
+        second[...] = both[:, 1:2]
+
+    return call(kernel, (scale,), [jax.ShapeDtypeStruct((n, 1), F32)] * 2, [VMEM], [VMEM] * 2)
 
 
 def gather(pieces, target):
@@ -232,13 +238,12 @@
         ]
         for copy in copies:
             copy.start()
-        factor = column(scl[...], 0)
         for s in range(2):
             cols = slice(s * half, (s + 1) * half)
             for t in range(0, n, TILE):
                 rows = slice(t, t + TILE)
                 old = cur[rows, cols]
-                newer = (old.astype(F32) - factor[rows] * dot(pan[rows], sol[s])).astype(BF)
+                newer = (old.astype(F32) - scl[rows] * dot(pan[rows], sol[s])).astype(BF)
                 out[rows, cols] = jnp.where(flags[0] > 0, newer, old)
         for copy in copies:
             copy.wait()
@@ -267,11 +272,10 @@
         pl.when(flags[3] != 1)(lambda: gather(theirs, sol))
         copies = [pltpu.make_async_copy(sol, solved.at[1, :, cols], sems.at[steps])]
         copies[0].start()
-        factor = column(scl[...], 1)
         for i in range(steps):
             rows = slice(i * TILE, (i + 1) * TILE)
             old = cur[rows, cols]
-            newer = (old.astype(F32) - factor[rows] * dot(pan[rows], sol[...])).astype(BF)
+            newer = (old.astype(F32) - scl[rows] * dot(pan[rows], sol[...])).astype(BF)
             tile[rows] = jnp.where(flags[0] > 1, newer, old)
             copy = pltpu.make_async_copy(tile.at[rows], out.at[rows, cols], sems.at[i])
             copy.start()
@@ -309,7 +313,8 @@
     )
 
     left = columns(share, 0)
-    far_left = swap_some(left, roots)
+    idle = [((0, c_, 0, 1), (0, c_, 1, 1)) for c_ in COLS] + [((0, c_, 1, 0), (1, c_, 1, 0)) for c_ in COLS]
+    far_left = swap(left, roots + idle, "y")
     later, inverse = lax.optimization_barrier((share, inverse_blocks, left))[:2]
     rows = jnp.where(near, inverse[1, quarter:], inverse[1, :quarter])
     crossed = send(rows, [((1, 1, 0, 1), (1, 0, 0, 1)), ((0, 1, 1, 1), (0, 0, 1, 1))])
@@ -317,55 +322,55 @@
     far_right = swap_some(columns(later, half), roots)
     far_top = send(crossed, [((1, 0, 0, 1), (0, 0, 0, 1))])
     far_bottom = send(crossed, [((0, 0, 1, 1), (0, 0, 0, 1))])
-    scale = panel_scale.T
+    scale0, scale1 = scale_columns(after(panel_scale.T, panel0))
 
     first_left = solve_first(flags, share, far_left, inverse, 0)
     left_here = core_swap(first_left)
-    first_hop = swap_some(first_left, [((0, c_, 0, 0), (1, c_, 0, 0)) for c_ in COLS])
+    first_hop = send(first_left, [((0, c_, 0, 0), (1, c_, 0, 0)) for c_ in COLS])
     far_top, far_bottom = lax.optimization_barrier((far_top, far_bottom, first_left))[:2]
-    own, message = second_block(flags, share, scale, panel0, left_here, inverse, far_top, far_bottom, 0)
+    own, message = second_block(flags, share, scale0, panel0, left_here, inverse, far_top, far_bottom, 0)
 
     first_right = solve_first(flags, share, after(far_right, own, first_hop), inverse, half)
-    inward = send(
-        jnp.where(first_core, first_right, own),
-        [((0, c_, 0, 0), (0, c_, 0, 1)) for c_ in COLS] + [((0, c_, 0, 1), (1, c_, 0, 1)) for c_ in COLS],
-    )
-    mine0 = jnp.where(near, first_right, first_hop)
+    own_hop = send(own, [((0, c_, 0, 1), (1, c_, 0, 1)) for c_ in COLS])
+    inward = core_swap(first_right)
+    mine0 = lax.optimization_barrier(jnp.where(near, first_right, first_hop))
+    outward = jnp.where(first_core, mine0, message)
     across = send(
-        jnp.where(first_core, mine0, message),
+        outward,
         [((x_, c_, 0, 0), (x_, c_, 2, 0)) for x_ in (0, 1) for c_ in COLS]
         + [((0, c_, 0, 1), (1, 1 - c_, 0, 1)) for c_ in COLS],
     )
-    own, message = second_block(flags, share, scale, panel0, inward, inverse, far_top, far_bottom, half)
+    own, message = second_block(flags, share, scale0, after(panel0, outward), inward, inverse, far_top, far_bottom, half)
     answer = send(
-        jnp.where(first_core, mine0, message),
+        jnp.where(first_core, mine0, after(message, own_hop)),
         [((x_, c_, 0, 0), (x_, c_, 1, 0)) for x_ in (0, 1) for c_ in COLS]
         + [((0, c_, 0, 1), (0, 1 - c_, 0, 1)) for c_ in COLS],
     )
     last = send(after(across, message), [((x_, c_, 2, 0), (x_, c_, 3, 0)) for x_ in (0, 1) for c_ in COLS])
 
-    second = solve_second(flags, (own, answer), (inward, across), inverse)
+    second = solve_second(flags, (own, answer), (own_hop, across), inverse)
 
     rows = [slice(0, quarter), slice(quarter, half)]
     mine0 = jnp.where(odd, jnp.where(outer, last, answer), jnp.where(middle, across, mine0))
-    far = [swap(part, far_step(1), "y") for part in second]
-    heads, step, mine1, other1 = [], [], [], []
-    for part, r, head in zip(far, rows, second):
+    far, heads, step, mine1, other1 = [], [], [], [], []
+    for part, r in zip(second, rows):
+        far.append(swap(jnp.where(first_core, mine0[r], part), far_step(1) + side_step(0), "y"))
+    for part, head in zip(far, second):
         heads.append(jnp.where(middle, after(part, *heads), head))
-        step.append(swap(jnp.where(first_core, mine0[r], heads[-1]), near_step(1) + side_step(0), "y"))
+        step.append(swap(heads[-1], near_step(1), "y"))
     for part, head in zip(step, heads):
         mine1.append(jnp.where(odd, after(part, *mine1), head))
         other1.append(swap(mine1[-1], side_step(1), "y"))
     mine0_here = core_swap(mine0)
-    step_here = [core_swap(s) for s in step]
+    far_here = [core_swap(f) for f in far]
 
     current, solved = update_first(
-        flags, share, scale, panel0, ([mine0], [mine0_here]), (step, step_here)
-    )
-    remaining, solved = update_second(flipped, current, scale, panel1, mine1, [core_swap(m) for m in mine1], solved)
+        flags, share, scale0, panel0, ([mine0], [mine0_here]), (far, far_here)
+    )
+    remaining, solved = update_second(flipped, current, scale1, after(panel1, other1[0]), mine1, [core_swap(m) for m in mine1], solved)
     other1 = [after(m, remaining) for m in other1]
     remaining, solved = update_second(
-        flags, current, scale, panel1, other1, [core_swap(m) for m in other1], solved, remaining
+        flags, current, scale1, panel1, other1, [core_swap(m) for m in other1], solved, remaining
     )
     return remaining[:, None, :], solved
 

time: 82.3 us -> 75.9 us (0.922)
  waiting for transfers between devices: 38.9 us -> 27.8 us
  starting transfers between devices: 23.3 us -> 28.6 us
    ppermute x14 -> x16, starting transfers between devices: 7.62 us -> 17.6 us  [swap(): return lax.ppermute(value, AXES, paired(wanted, side))]
    ppermute x3 -> x1, waiting for transfers between devices: 12.5 us -> 6.57 us  [swap_some(): lax.ppermute(value, AXES, [(device(*p), device(*q)) for a, b in wanted fo...]
    ppermute x3 -> x1, starting transfers between devices: 8.98 us -> 3.3 us  [swap_some(): lax.ppermute(value, AXES, [(device(*p), device(*q)) for a, b in wanted fo...]
    ppermute x14 -> x16, waiting for transfers between devices: 14.7 us -> 12 us  [swap(): return lax.ppermute(value, AXES, paired(wanted, side))]
    ppermute x7 -> x8, waiting for transfers between devices: 11.7 us -> 9.19 us  [send(): lax.ppermute(value, AXES, [(device(*a), device(*b)) for a, b in wanted])]
    ppermute x7 -> x8, starting transfers between devices: 6.73 us -> 7.73 us  [send(): lax.ppermute(value, AXES, [(device(*a), device(*b)) for a, b in wanted])]
    pallas_call x10 -> x11, Pallas kernels: 11.9 us -> 11.4 us  [call(): pl.pallas_call(kernel, in_specs=ins, out_specs=outs, out_shape=shapes, sc...]
  transfers between devices with their start and end apart: 24 -> 25, of which waited for: 13 -> 11; matrix products, arithmetic and copies ran while one was open for 5% -> 5% of each run, Pallas kernels for 9% -> 12%
where the time goes in v5:
time: 75.9 us; the launch traced here: 75.6 us
  starting transfers between devices  28.6 us (38%)
  waiting for transfers between devices  27.8 us (37%)
  Pallas kernels  11.4 us (15%)
  local copies, waits for them, and re-layouts  6.16 us (8%)
  between operations  1.01 us (1%)
    ppermute x16, starting transfers between devices, swap(): return lax.ppermute(value, AXES, paired(wanted, side))  17.6 us
    ppermute x16, waiting for transfers between devices, swap(): return lax.ppermute(value, AXES, paired(wanted, side))  12 us
    pallas_call x11, Pallas kernels, call(): pl.pallas_call(kernel, in_specs=ins, out_specs=outs, out_shape=shapes, sc...  11.4 us
    ppermute x8, waiting for transfers between devices, send(): lax.ppermute(value, AXES, [(device(*a), device(*b)) for a, b in wanted])  9.19 us
    ppermute x8, starting transfers between devices, send(): lax.ppermute(value, AXES, [(device(*a), device(*b)) for a, b in wanted])  7.73 us
    ppermute x1, waiting for transfers between devices, swap_some(): lax.ppermute(value, AXES, [(device(*p), device(*q)) for a, b in wanted fo...  6.57 us
    ppermute x1, starting transfers between devices, swap_some(): lax.ppermute(value, AXES, [(device(*p), device(*q)) for a, b in wanted fo...  3.3 us
    slice x1, local copies, waits for them, and re-layouts, body(): panel[:, 1, :]  2.98 us
  transfers between devices with their start and end apart: 25, of which 11 were waited for; matrix products, arithmetic and copies ran while one was open for 5% of the time, Pallas kernels for 12%

profile of v5, /device:TPU:0, one launch (start us, length us, event | category | flops | bytes accessed | tf_op | source)
XLA Modules:
  0.0 75.6 jit_solution(17564258018114582839)
XLA Ops:
  0.7 1.6 %copy-done = bf16[1024,1,1024]{2,0,1:T(8,128)(2,1)S(1)} copy-done((bf16[1024,1,1024]{2,0,1:T(8,128)(2,1)S(1)}, bf16[1024,1,1024]{2,0,1:T(8,128)(2,1)}, u32[]{:S(2)}) %copy-start) | copy-done | bytes 2097176
  2.4 3.0 %collective-permute-start.1 = (bf16[1024,512]{1,0:T(8,128)(2,1)S(1)}, bf16[1024,512]{1,0:T(8,128)(2,1)S(1)}, u32[]{:S(2)}, u32[]{:S(2)}) collective-permute-start(bf16[1024,512]{1,0:T(8,128)(2,1)S(1)} %shard_map.59), channel_id=1, source_target_pairs={{0,1},{1,0},{2,10},{10,2},{3,11},{11,3},{8,12},{12,8},{9,13},{13,9... | collective-permute-start | bytes 3145736 | tf_op jit(solution)/shard_map/ppermute | solution.py:58
  6.2 3.0 %fusion = (bf16[1024,1,512]{2,1,0:T(2,128)(2,1)S(1)}, bf16[1024,1,512]{2,1,0:T(2,128)(2,1)S(1)}) fusion(bf16[1024,2,512]{2,1,0:T(2,128)(2,1)S(1)} %copy-done.4), kind=kLoop, calls=%fused_computation.16 | loop fusion | bytes 4194304 | tf_op jit(solution)/shard_map/slice | solution.py:321
  11.0 3.3 %collective-permute-start = (bf16[1024,512]{1,0:T(8,128)(2,1)S(1)}, bf16[1024,512]{1,0:T(8,128)(2,1)S(1)}, u32[]{:S(2)}, u32[]{:S(2)}) collective-permute-start(bf16[1024,512]{1,0:T(8,128)(2,1)S(1)} %shard_map.61), channel_id=1, source_target_pairs={{0,1},{1,0}} | collective-permute-start | bytes 3145736 | tf_op jit(solution)/shard_map/ppermute | solution.py:62
  15.7 2.6 %collective-permute-done.1.got = bf16[1024,512]{1,0:T(8,128)(2,1)S(1)} collective-permute-done((bf16[1024,512]{1,0:T(8,128)(2,1)S(1)}, bf16[1024,512]{1,0:T(8,128)(2,1)S(1)}, u32[]{:S(2)}, u32[]{:S(2)}) %collective-permute-start.1) | collective-permute-done | bytes 1048608 | tf_op jit(solution)/shard_map/ppermute | solution.py:58
  18.3 1.3 %shard_map.62 = bf16[512,512]{1,0:T(8,128)(2,1)S(1)} custom-call(s32[4]{0:T(128)S(1)} %get-tuple-element.41.flags, bf16[1024,1024]{1,0:T(8,128)(2,1)S(1)} %bitcast.16, bf16[1024,512]{1,0:T(8,128)(2,1)S(1)} %collective-permute-done.1.got, bf16[2,512,1024]{2,1,0:T(8,128)(2,1)S(1)} %copy-done.2), custom_call_target="tpu_custom_call" | custom-call | tf_op jit(solution)/shard_map/pallas_call | solution.py:94
  19.6 1.6 %collective-permute-start.6 = (bf16[512,512]{1,0:T(8,128)(2,1)S(1)}, bf16[512,512]{1,0:T(8,128)(2,1)S(1)}, u32[]{:S(2)}, u32[]{:S(2)}) collective-permute-start(bf16[512,512]{1,0:T(8,128)(2,1)S(1)} %shard_map.62), channel_id=1, source_target_pairs={{0,4},{1,5}} | collective-permute-start | bytes 1572872 | tf_op jit(solution)/shard_map/ppermute | solution.py:66
  22.9 6.6 %collective-permute-done.got = bf16[1024,512]{1,0:T(8,128)(2,1)S(1)} collective-permute-done((bf16[1024,512]{1,0:T(8,128)(2,1)S(1)}, bf16[1024,512]{1,0:T(8,128)(2,1)S(1)}, u32[]{:S(2)}, u32[]{:S(2)}) %collective-permute-start) | collective-permute-done | bytes 1048608 | tf_op jit(solution)/shard_map/ppermute | solution.py:62
  29.5 1.3 %shard_map.64 = bf16[512,512]{1,0:T(8,128)(2,1)S(1)} custom-call(s32[4]{0:T(128)S(1)} %get-tuple-element.41.flags, bf16[1024,1024]{1,0:T(8,128)(2,1)S(1)} %bitcast.18, bf16[1024,512]{1,0:T(8,128)(2,1)S(1)} %collective-permute-done.got, bf16[2,512,1024]{2,1,0:T(8,128)(2,1)S(1)} %copy-done.2), custom_call_target="tpu_custom_call" | custom-call | tf_op jit(solution)/shard_map/pallas_call | solution.py:94
  31.0 1.3 %collective-permute-start.7 = (bf16[512,512]{1,0:T(8,128)(2,1)S(1)}, bf16[512,512]{1,0:T(8,128)(2,1)S(1)}, u32[]{:S(2)}, u32[]{:S(2)}) collective-permute-start(bf16[512,512]{1,0:T(8,128)(2,1)S(1)} %broadcast_select_fusion.2), channel_id=1, source_target_pairs={{0,16},{1,17},{4,20},{5,21},{2,7},{3,6}} | collective-permute-start | bytes 1572872 | tf_op jit(solution)/shard_map/ppermute | solution.py:66
  33.4 1.3 %collective-permute-start.11 = (bf16[512,512]{1,0:T(8,128)(2,1)S(1)}, bf16[512,512]{1,0:T(8,128)(2,1)S(1)}, u32[]{:S(2)}, u32[]{:S(2)}) collective-permute-start(bf16[512,512]{1,0:T(8,128)(2,1)S(1)} %broadcast_select_fusion.1), channel_id=1, source_target_pairs={{0,8},{1,9},{4,12},{5,13},{2,3},{3,2}} | collective-permute-start | bytes 1572872 | tf_op jit(solution)/shard_map/ppermute | solution.py:66
  34.7 4.3 %collective-permute-done.7.b1 = bf16[512,512]{1,0:T(8,128)(2,1)S(1)} collective-permute-done((bf16[512,512]{1,0:T(8,128)(2,1)S(1)}, bf16[512,512]{1,0:T(8,128)(2,1)S(1)}, u32[]{:S(2)}, u32[]{:S(2)}) %collective-permute-start.7) | collective-permute-done | bytes 524320 | tf_op jit(solution)/shard_map/ppermute | solution.py:66
  39.7 4.9 %collective-permute-done.11.b0 = bf16[512,512]{1,0:T(8,128)(2,1)S(1)} collective-permute-done((bf16[512,512]{1,0:T(8,128)(2,1)S(1)}, bf16[512,512]{1,0:T(8,128)(2,1)S(1)}, u32[]{:S(2)}, u32[]{:S(2)}) %collective-permute-start.11) | collective-permute-done | bytes 524320 | tf_op jit(solution)/shard_map/ppermute | solution.py:66
  45.6 1.9 %collective-permute-start.14 = (bf16[256,512]{1,0:T(8,128)(2,1)S(1)}, bf16[256,512]{1,0:T(8,128)(2,1)S(1)}, u32[]{:S(2)}, u32[]{:S(2)}) collective-permute-start(bf16[256,512]{1,0:T(8,128)(2,1)S(1)} %get-tuple-element.82), channel_id=1, source_target_pairs={{2,18},{18,2},{6,22},{22,6},{3,19},{19,3},{7,23},{23,7},{0,4},{4,0... | collective-permute-start | bytes 786440 | tf_op jit(solution)/shard_map/ppermute | solution.py:58
  47.5 4.3 %collective-permute-done.13.refs_2_ = bf16[256,512]{1,0:T(8,128)(2,1)S(1)} collective-permute-done((bf16[256,512]{1,0:T(8,128)(2,1)S(1)}, bf16[256,512]{1,0:T(8,128)(2,1)S(1)}, u32[]{:S(2)}, u32[]{:S(2)}) %collective-permute-start.13) | collective-permute-done | bytes 262176 | tf_op jit(solution)/shard_map/ppermute | solution.py:58
  51.8 2.1 %collective-permute-start.17 = (bf16[256,512]{1,0:T(8,128)(2,1)S(1)}, bf16[256,512]{1,0:T(8,128)(2,1)S(1)}, u32[]{:S(2)}, u32[]{:S(2)}) collective-permute-start(bf16[256,512]{1,0:T(8,128)(2,1)S(1)} %broadcast_select_fusion.4), channel_id=1, source_target_pairs={{2,10},{10,2},{18,26},{26,18},{6,14},{14,6},{22,30},{30,22},{3,11}... | collective-permute-start | bytes 786440 | tf_op jit(solution)/shard_map/ppermute | solution.py:58
  54.6 2.1 %collective-permute-start.19 = (bf16[256,512]{1,0:T(8,128)(2,1)S(1)}, bf16[256,512]{1,0:T(8,128)(2,1)S(1)}, u32[]{:S(2)}, u32[]{:S(2)}) collective-permute-start(bf16[256,512]{1,0:T(8,128)(2,1)S(1)} %broadcast_select_fusion.3), channel_id=1, source_target_pairs={{2,10},{10,2},{18,26},{26,18},{6,14},{14,6},{22,30},{30,22},{3,11}... | collective-permute-start | bytes 786440 | tf_op jit(solution)/shard_map/ppermute | solution.py:58
  56.7 2.5 %collective-permute-start.12 = (bf16[512,512]{1,0:T(8,128)(2,1)S(1)}, bf16[512,512]{1,0:T(8,128)(2,1)S(1)}, u32[]{:S(2)}, u32[]{:S(2)}) collective-permute-start(bf16[512,512]{1,0:T(8,128)(2,1)S(1)} %select_select_fusion.refs_0_), channel_id=1, source_target_pairs={{0,2},{2,0},{1,3},{3,1},{4,6},{6,4},{5,7},{7,5},{8,10},{10,8},{9,1... | collective-permute-start | bytes 1572872 | tf_op jit(solution)/shard_map/ppermute | solution.py:58
  61.1 3.9 %collective-permute-start.21 = (bf16[256,512]{1,0:T(8,128)(2,1)S(1)}, bf16[256,512]{1,0:T(8,128)(2,1)S(1)}, u32[]{:S(2)}, u32[]{:S(2)}) collective-permute-start(bf16[256,512]{1,0:T(8,128)(2,1)S(1)} %broadcast_select_fusion.5.refs_1_), channel_id=1, source_target_pairs={{0,2},{2,0},{1,3},{3,1},{4,6},{6,4},{5,7},{7,5},{8,10},{10,8},{9,1... | collective-permute-start | bytes 786440 | tf_op jit(solution)/shard_map/ppermute | solution.py:58
  65.2 2.3 %shard_map.67 = (bf16[1024,1024]{1,0:T(8,128)(2,1)S(1)}, bf16[2,512,1024]{2,1,0:T(8,128)(2,1)}) custom-call(s32[4]{0:T(128)S(1)} %get-tuple-element.41.flags, bf16[1024,1024]{1,0:T(8,128)(2,1)S(1)} %bitcast.20, f32[1024,1]{1,0:T(8,128)S(1)} %get-tuple-element.46.scl, bf16[1024,512]{1,0:T(8,128)(2,1)S(1)} %get-tuple-element.58.pan, ...), custom_call_target="tpu_custom_call" | custom-call | tf_op jit(solution)/shard_map/pallas_call | solution.py:94
  67.5 2.1 %shard_map.68 = (bf16[1024,1024]{1,0:T(8,128)(2,1)}, bf16[2,512,1024]{2,1,0:T(8,128)(2,1)}) custom-call(s32[4]{0:T(128)S(1)} %get-tuple-element.69.flags, bf16[1024,1024]{1,0:T(8,128)(2,1)S(1)} %get-tuple-element.66.cur, f32[1024,1]{1,0:T(8,128)S(1)} %get-tuple-element.67.scl, ...), custom_call_target="tpu_custom_call", output_to_operand_aliasing={{1}: (8, {})} | custom-call | tf_op jit(solution)/shard_map/pallas_call | solution.py:94
  69.6 1.9 %collective-permute-done.22.refs_1_ = bf16[256,512]{1,0:T(8,128)(2,1)S(1)} collective-permute-done((bf16[256,512]{1,0:T(8,128)(2,1)S(1)}, bf16[256,512]{1,0:T(8,128)(2,1)S(1)}, u32[]{:S(2)}, u32[]{:S(2)}) %collective-permute-start.22) | collective-permute-done | bytes 262176 | tf_op jit(solution)/shard_map/ppermute | solution.py:58
  72.0 1.0 %collective-permute-done.23.refs_2_ = bf16[256,512]{1,0:T(8,128)(2,1)S(1)} collective-permute-done((bf16[256,512]{1,0:T(8,128)(2,1)S(1)}, bf16[256,512]{1,0:T(8,128)(2,1)S(1)}, u32[]{:S(2)}, u32[]{:S(2)}) %collective-permute-start.23) | collective-permute-done | bytes 262176 | tf_op jit(solution)/shard_map/ppermute | solution.py:58
  73.4 2.1 %shard_map.69 = (bf16[1024,1024]{1,0:T(8,128)(2,1)}, bf16[2,512,1024]{2,1,0:T(8,128)(2,1)}) custom-call(s32[4]{0:T(128)S(1)} %get-tuple-element.41.flags, bf16[1024,1024]{1,0:T(8,128)(2,1)S(1)} %get-tuple-element.66.cur, f32[1024,1]{1,0:T(8,128)S(1)} %get-tuple-element.67.scl, ...), custom_call_target="tpu_custom_call", output_to_operand_aliasing={{1}: (8, {}), {0}: (9, {})} | custom-call | tf_op jit(solution)/shard_map/pallas_call | solution.py:94
  (60 shorter events, 12.2 us)
Async XLA Ops:
  2.4 15.8 %collective-permute-start.1 = (bf16[1024,512]{1,0:T(8,128)(2,1)S(1)}, bf16[1024,512]{1,0:T(8,128)(2,1)S(1)}, u32[]{:S(2)}, u32[]{:S(2)}) collective-permute-start(bf16[1024,512]{1,0:T(8,128)(2,1)S(1)} %shard_map.59), channel_id=1, source_target_pairs={{0,1},{1,0},{2,10},{10,2},{3,11},{11,3},{8,12},{12,8},{9,13},{13,9... | collective-permute-start | bytes 3145736 | tf_op jit(solution)/shard_map/ppermute | solution.py:58
  5.5 8.7 %collective-permute-start.3 = (bf16[256,1024]{1,0:T(8,128)(2,1)S(1)}, bf16[256,1024]{1,0:T(8,128)(2,1)S(1)}, u32[]{:S(2)}, u32[]{:S(2)}) collective-permute-start(bf16[256,1024]{1,0:T(8,128)(2,1)S(1)} %select_bitcast_fusion), channel_id=1, source_target_pairs={{7,6},{11,10}} | collective-permute-start | bytes 1572872 | tf_op jit(solution)/shard_map/ppermute | solution.py:66
  11.0 18.5 %collective-permute-start = (bf16[1024,512]{1,0:T(8,128)(2,1)S(1)}, bf16[1024,512]{1,0:T(8,128)(2,1)S(1)}, u32[]{:S(2)}, u32[]{:S(2)}) collective-permute-start(bf16[1024,512]{1,0:T(8,128)(2,1)S(1)} %shard_map.61), channel_id=1, source_target_pairs={{0,1},{1,0}} | collective-permute-start | bytes 3145736 | tf_op jit(solution)/shard_map/ppermute | solution.py:62
  14.3 7.3 %collective-permute-start.5 = (bf16[256,1024]{1,0:T(8,128)(2,1)S(1)}, bf16[256,1024]{1,0:T(8,128)(2,1)S(1)}, u32[]{:S(2)}, u32[]{:S(2)}) collective-permute-start(bf16[256,1024]{1,0:T(8,128)(2,1)S(1)} %collective-permute-done.3), channel_id=1, source_target_pairs={{10,2}} | collective-permute-start | bytes 1572872 | tf_op jit(solution)/shard_map/ppermute | solution.py:66
  15.0 6.6 %collective-permute-start.4 = (bf16[256,1024]{1,0:T(8,128)(2,1)S(1)}, bf16[256,1024]{1,0:T(8,128)(2,1)S(1)}, u32[]{:S(2)}, u32[]{:S(2)}) collective-permute-start(bf16[256,1024]{1,0:T(8,128)(2,1)S(1)} %collective-permute-done.3), channel_id=1, source_target_pairs={{6,2}} | collective-permute-start | bytes 1572872 | tf_op jit(solution)/shard_map/ppermute | solution.py:66
  19.5 2.1 %collective-permute-start.2 = (bf16[512,512]{1,0:T(8,128)(2,1)S(1)}, bf16[512,512]{1,0:T(8,128)(2,1)S(1)}, u32[]{:S(2)}, u32[]{:S(2)}) collective-permute-start(bf16[512,512]{1,0:T(8,128)(2,1)S(1)} %shard_map.62), channel_id=1, source_target_pairs={{0,2},{2,0},{1,3},{3,1},{4,6},{6,4},{5,7},{7,5},{8,10},{10,8},{9,1... | collective-permute-start | bytes 1572872 | tf_op jit(solution)/shard_map/ppermute | solution.py:58
  19.6 9.9 %collective-permute-start.6 = (bf16[512,512]{1,0:T(8,128)(2,1)S(1)}, bf16[512,512]{1,0:T(8,128)(2,1)S(1)}, u32[]{:S(2)}, u32[]{:S(2)}) collective-permute-start(bf16[512,512]{1,0:T(8,128)(2,1)S(1)} %shard_map.62), channel_id=1, source_target_pairs={{0,4},{1,5}} | collective-permute-start | bytes 1572872 | tf_op jit(solution)/shard_map/ppermute | solution.py:66
  22.2 11.1 %collective-permute-start.10 = (bf16[512,512]{1,0:T(8,128)(2,1)S(1)}, bf16[512,512]{1,0:T(8,128)(2,1)S(1)}, u32[]{:S(2)}, u32[]{:S(2)}) collective-permute-start(bf16[512,512]{1,0:T(8,128)(2,1)S(1)} %get-tuple-element.55), channel_id=1, source_target_pairs={{2,6},{3,7}} | collective-permute-start | bytes 1572872 | tf_op jit(solution)/shard_map/ppermute | solution.py:66
  30.8 2.0 %collective-permute-start.8 = (bf16[512,512]{1,0:T(8,128)(2,1)S(1)}, bf16[512,512]{1,0:T(8,128)(2,1)S(1)}, u32[]{:S(2)}, u32[]{:S(2)}) collective-permute-start(bf16[512,512]{1,0:T(8,128)(2,1)S(1)} %shard_map.64), channel_id=1, source_target_pairs={{0,2},{2,0},{1,3},{3,1},{4,6},{6,4},{5,7},{7,5},{8,10},{10,8},{9,1... | collective-permute-start | bytes 1572872 | tf_op jit(solution)/shard_map/ppermute | solution.py:58
  31.0 8.0 %collective-permute-start.7 = (bf16[512,512]{1,0:T(8,128)(2,1)S(1)}, bf16[512,512]{1,0:T(8,128)(2,1)S(1)}, u32[]{:S(2)}, u32[]{:S(2)}) collective-permute-start(bf16[512,512]{1,0:T(8,128)(2,1)S(1)} %broadcast_select_fusion.2), channel_id=1, source_target_pairs={{0,16},{1,17},{4,20},{5,21},{2,7},{3,6}} | collective-permute-start | bytes 1572872 | tf_op jit(solution)/shard_map/ppermute | solution.py:66
  33.4 11.2 %collective-permute-start.11 = (bf16[512,512]{1,0:T(8,128)(2,1)S(1)}, bf16[512,512]{1,0:T(8,128)(2,1)S(1)}, u32[]{:S(2)}, u32[]{:S(2)}) collective-permute-start(bf16[512,512]{1,0:T(8,128)(2,1)S(1)} %broadcast_select_fusion.1), channel_id=1, source_target_pairs={{0,8},{1,9},{4,12},{5,13},{2,3},{3,2}} | collective-permute-start | bytes 1572872 | tf_op jit(solution)/shard_map/ppermute | solution.py:66
  39.0 6.2 %collective-permute-start.9 = (bf16[512,512]{1,0:T(8,128)(2,1)S(1)}, bf16[512,512]{1,0:T(8,128)(2,1)S(1)}, u32[]{:S(2)}, u32[]{:S(2)}) collective-permute-start(bf16[512,512]{1,0:T(8,128)(2,1)S(1)} %collective-permute-done.7.b1), channel_id=1, source_target_pairs={{16,24},{17,25},{20,28},{21,29}} | collective-permute-start | bytes 1572872 | tf_op jit(solution)/shard_map/ppermute | solution.py:66
  45.4 6.4 %collective-permute-start.13 = (bf16[256,512]{1,0:T(8,128)(2,1)S(1)}, bf16[256,512]{1,0:T(8,128)(2,1)S(1)}, u32[]{:S(2)}, u32[]{:S(2)}) collective-permute-start(bf16[256,512]{1,0:T(8,128)(2,1)S(1)} %get-tuple-element.83), channel_id=1, source_target_pairs={{2,18},{18,2},{6,22},{22,6},{3,19},{19,3},{7,23},{23,7},{0,4},{4,0... | collective-permute-start | bytes 786440 | tf_op jit(solution)/shard_map/ppermute | solution.py:58
  45.6 9.0 %collective-permute-start.14 = (bf16[256,512]{1,0:T(8,128)(2,1)S(1)}, bf16[256,512]{1,0:T(8,128)(2,1)S(1)}, u32[]{:S(2)}, u32[]{:S(2)}) collective-permute-start(bf16[256,512]{1,0:T(8,128)(2,1)S(1)} %get-tuple-element.82), channel_id=1, source_target_pairs={{2,18},{18,2},{6,22},{22,6},{3,19},{19,3},{7,23},{23,7},{0,4},{4,0... | collective-permute-start | bytes 786440 | tf_op jit(solution)/shard_map/ppermute | solution.py:58
  51.8 7.9 %collective-permute-start.17 = (bf16[256,512]{1,0:T(8,128)(2,1)S(1)}, bf16[256,512]{1,0:T(8,128)(2,1)S(1)}, u32[]{:S(2)}, u32[]{:S(2)}) collective-permute-start(bf16[256,512]{1,0:T(8,128)(2,1)S(1)} %broadcast_select_fusion.4), channel_id=1, source_target_pairs={{2,10},{10,2},{18,26},{26,18},{6,14},{14,6},{22,30},{30,22},{3,11}... | collective-permute-start | bytes 786440 | tf_op jit(solution)/shard_map/ppermute | solution.py:58
  54.6 6.4 %collective-permute-start.19 = (bf16[256,512]{1,0:T(8,128)(2,1)S(1)}, bf16[256,512]{1,0:T(8,128)(2,1)S(1)}, u32[]{:S(2)}, u32[]{:S(2)}) collective-permute-start(bf16[256,512]{1,0:T(8,128)(2,1)S(1)} %broadcast_select_fusion.3), channel_id=1, source_target_pairs={{2,10},{10,2},{18,26},{26,18},{6,14},{14,6},{22,30},{30,22},{3,11}... | collective-permute-start | bytes 786440 | tf_op jit(solution)/shard_map/ppermute | solution.py:58
  56.7 8.4 %collective-permute-start.12 = (bf16[512,512]{1,0:T(8,128)(2,1)S(1)}, bf16[512,512]{1,0:T(8,128)(2,1)S(1)}, u32[]{:S(2)}, u32[]{:S(2)}) collective-permute-start(bf16[512,512]{1,0:T(8,128)(2,1)S(1)} %select_select_fusion.refs_0_), channel_id=1, source_target_pairs={{0,2},{2,0},{1,3},{3,1},{4,6},{6,4},{5,7},{7,5},{8,10},{10,8},{9,1... | collective-permute-start | bytes 1572872 | tf_op jit(solution)/shard_map/ppermute | solution.py:58
  59.2 5.8 %collective-permute-start.16 = (bf16[256,512]{1,0:T(8,128)(2,1)S(1)}, bf16[256,512]{1,0:T(8,128)(2,1)S(1)}, u32[]{:S(2)}, u32[]{:S(2)}) collective-permute-start(bf16[256,512]{1,0:T(8,128)(2,1)S(1)} %collective-permute-done.14.refs_3_), channel_id=1, source_target_pairs={{0,2},{2,0},{1,3},{3,1},{4,6},{6,4},{5,7},{7,5},{8,10},{10,8},{9,1... | collective-permute-start | bytes 786440 | tf_op jit(solution)/shard_map/ppermute | solution.py:58
  59.3 5.8 %collective-permute-start.15 = (bf16[256,512]{1,0:T(8,128)(2,1)S(1)}, bf16[256,512]{1,0:T(8,128)(2,1)S(1)}, u32[]{:S(2)}, u32[]{:S(2)}) collective-permute-start(bf16[256,512]{1,0:T(8,128)(2,1)S(1)} %collective-permute-done.13.refs_2_), channel_id=1, source_target_pairs={{0,2},{2,0},{1,3},{3,1},{4,6},{6,4},{5,7},{7,5},{8,10},{10,8},{9,1... | collective-permute-start | bytes 786440 | tf_op jit(solution)/shard_map/ppermute | solution.py:58
  59.8 7.7 %collective-permute-start.18 = (bf16[256,512]{1,0:T(8,128)(2,1)S(1)}, bf16[256,512]{1,0:T(8,128)(2,1)S(1)}, u32[]{:S(2)}, u32[]{:S(2)}) collective-permute-start(bf16[256,512]{1,0:T(8,128)(2,1)S(1)} %broadcast_select_fusion.6.refs_0_), channel_id=1, source_target_pairs={{2,6},{6,2},{10,14},{14,10},{18,22},{22,18},{26,30},{30,26},{3,7},... | collective-permute-start | bytes 786440 | tf_op jit(solution)/shard_map/ppermute | solution.py:58
  61.1 6.4 %collective-permute-start.21 = (bf16[256,512]{1,0:T(8,128)(2,1)S(1)}, bf16[256,512]{1,0:T(8,128)(2,1)S(1)}, u32[]{:S(2)}, u32[]{:S(2)}) collective-permute-start(bf16[256,512]{1,0:T(8,128)(2,1)S(1)} %broadcast_select_fusion.5.refs_1_), channel_id=1, source_target_pairs={{0,2},{2,0},{1,3},{3,1},{4,6},{6,4},{5,7},{7,5},{8,10},{10,8},{9,1... | collective-permute-start | bytes 786440 | tf_op jit(solution)/shard_map/ppermute | solution.py:58
  65.1 2.4 %collective-permute-start.20 = (bf16[256,512]{1,0:T(8,128)(2,1)S(1)}, bf16[256,512]{1,0:T(8,128)(2,1)S(1)}, u32[]{:S(2)}, u32[]{:S(2)}) collective-permute-start(bf16[256,512]{1,0:T(8,128)(2,1)S(1)} %broadcast_select_fusion.6.refs_0_), channel_id=1, source_target_pairs={{0,2},{2,0},{1,3},{3,1},{4,6},{6,4},{5,7},{7,5},{8,10},{10,8},{9,1... | collective-permute-start | bytes 786440 | tf_op jit(solution)/shard_map/ppermute | solution.py:58
  65.1 6.4 %collective-permute-start.22 = (bf16[256,512]{1,0:T(8,128)(2,1)S(1)}, bf16[256,512]{1,0:T(8,128)(2,1)S(1)}, u32[]{:S(2)}, u32[]{:S(2)}) collective-permute-start(bf16[256,512]{1,0:T(8,128)(2,1)S(1)} %broadcast_select_fusion.5.refs_1_), channel_id=1, source_target_pairs={{2,6},{6,2},{10,14},{14,10},{18,22},{22,18},{26,30},{30,26},{3,7},... | collective-permute-start | bytes 786440 | tf_op jit(solution)/shard_map/ppermute | solution.py:58
  71.5 1.9 %collective-permute-start.24 = (bf16[256,512]{1,0:T(8,128)(2,1)S(1)}, bf16[256,512]{1,0:T(8,128)(2,1)S(1)}, u32[]{:S(2)}, u32[]{:S(2)}) collective-permute-start(bf16[256,512]{1,0:T(8,128)(2,1)S(1)} %collective-permute-done.22.refs_1_), channel_id=1, source_target_pairs={{0,2},{2,0},{1,3},{3,1},{4,6},{6,4},{5,7},{7,5},{8,10},{10,8},{9,1... | collective-permute-start | bytes 786440 | tf_op jit(solution)/shard_map/ppermute | solution.py:58
  (6 other events, 22.1 us)

commit v6 on v5

--- a/solution.py
+++ b/solution.py
@@ -330,9 +330,9 @@
     far_top, far_bottom = lax.optimization_barrier((far_top, far_bottom, first_left))[:2]
     own, message = second_block(flags, share, scale0, panel0, left_here, inverse, far_top, far_bottom, 0)
 
-    first_right = solve_first(flags, share, after(far_right, own, first_hop), inverse, half)
+    first_right = solve_first(flags, share, after(far_right, own), inverse, half)
     own_hop = send(own, [((0, c_, 0, 1), (1, c_, 0, 1)) for c_ in COLS])
-    inward = core_swap(first_right)
+    inward = after(core_swap(first_right), first_hop)
     mine0 = lax.optimization_barrier(jnp.where(near, first_right, first_hop))
     outward = jnp.where(first_core, mine0, message)
     across = send(

time: 75.9 us -> 75.3 us (level)
  the two profiles are of different devices: /device:TPU:0 before, /device:TPU:29 now
where the time goes in v6:
time: 75.3 us; the launch traced here: 74.9 us
  starting transfers between devices  49.8 us (66%)
  Pallas kernels  9.92 us (13%)
  local copies, waits for them, and re-layouts  6.89 us (9%)
  waiting for transfers between devices  6.72 us (9%)
  between operations  1.01 us (1%)
    ppermute x16, starting transfers between devices, swap(): return lax.ppermute(value, AXES, paired(wanted, side))  43.5 us
    pallas_call x11, Pallas kernels, call(): pl.pallas_call(kernel, in_specs=ins, out_specs=outs, out_shape=shapes, sc...  9.92 us
    ppermute x16, waiting for transfers between devices, swap(): return lax.ppermute(value, AXES, paired(wanted, side))  6.7 us
    ppermute x8, starting transfers between devices, send(): lax.ppermute(value, AXES, [(device(*a), device(*b)) for a, b in wanted])  5.54 us
    unnamed x10, local copies, waits for them, and re-layouts  3.3 us
    slice x1, local copies, waits for them, and re-layouts, body(): panel[:, 1, :]  2.98 us
  transfers between devices with their start and end apart: 25, of which 6 were waited for; matrix products, arithmetic and copies ran while one was open for 5% of the time, Pallas kernels for 10%

profile of v6, /device:TPU:29, one launch (start us, length us, event | category | flops | bytes accessed | tf_op | source)
XLA Modules:
  0.0 74.9 jit_solution(6836172815722429560)
XLA Ops:
  0.7 1.6 %copy-done = bf16[1024,1,1024]{2,0,1:T(8,128)(2,1)S(1)} copy-done((bf16[1024,1,1024]{2,0,1:T(8,128)(2,1)S(1)}, bf16[1024,1,1024]{2,0,1:T(8,128)(2,1)}, u32[]{:S(2)}) %copy-start) | copy-done | bytes 2097176
  2.4 0.7 collective-permute-start.1
  3.2 0.7 copy-done.2
  4.0 0.7 collective-permute-start.3
  4.7 3.0 %fusion = (bf16[1024,1,512]{2,1,0:T(2,128)(2,1)S(1)}, bf16[1024,1,512]{2,1,0:T(2,128)(2,1)S(1)}) fusion(bf16[1024,2,512]{2,1,0:T(2,128)(2,1)S(1)} %copy-done.4), kind=kLoop, calls=%fused_computation.16 | loop fusion | bytes 4194304 | tf_op jit(solution)/shard_map/slice | solution.py:321
  8.3 1.0 %copy-done.1 = bf16[1024,1,1024]{2,0,1:T(8,128)(2,1)S(1)} copy-done((bf16[1024,1,1024]{2,0,1:T(8,128)(2,1)S(1)}, bf16[1024,1,1024]{2,0,1:T(8,128)(2,1)}, u32[]{:S(2)}) %copy-start.1) | copy-done | bytes 2097176
  9.4 0.7 collective-permute-start
  10.1 0.7 collective-permute-start.5
  12.1 0.7 collective-permute-start.2
  14.9 0.7 collective-permute-start.10
  17.5 0.7 collective-permute-done.8.sol
  21.3 1.2 %collective-permute-start.14 = (bf16[256,512]{1,0:T(8,128)(2,1)S(1)}, bf16[256,512]{1,0:T(8,128)(2,1)S(1)}, u32[]{:S(2)}, u32[]{:S(2)}) collective-permute-start(bf16[256,512]{1,0:T(8,128)(2,1)S(1)} %get-tuple-element.84), channel_id=1, source_target_pairs={{2,18},{18,2},{6,22},{22,6},{3,19},{19,3},{7,23},{23,7},{0,4},{4,0... | collective-permute-start | bytes 786440 | tf_op jit(solution)/shard_map/ppermute | solution.py:58
  22.5 3.8 %collective-permute-done.13.refs_2_ = bf16[256,512]{1,0:T(8,128)(2,1)S(1)} collective-permute-done((bf16[256,512]{1,0:T(8,128)(2,1)S(1)}, bf16[256,512]{1,0:T(8,128)(2,1)S(1)}, u32[]{:S(2)}, u32[]{:S(2)}) %collective-permute-start.13) | collective-permute-done | bytes 262176 | tf_op jit(solution)/shard_map/ppermute | solution.py:58
  26.3 23.2 %collective-permute-start.17 = (bf16[256,512]{1,0:T(8,128)(2,1)S(1)}, bf16[256,512]{1,0:T(8,128)(2,1)S(1)}, u32[]{:S(2)}, u32[]{:S(2)}) collective-permute-start(bf16[256,512]{1,0:T(8,128)(2,1)S(1)} %broadcast_select_fusion.4), channel_id=1, source_target_pairs={{2,10},{10,2},{18,26},{26,18},{6,14},{14,6},{22,30},{30,22},{3,11}... | collective-permute-start | bytes 786440 | tf_op jit(solution)/shard_map/ppermute | solution.py:58
  49.6 2.8 %collective-permute-start.19 = (bf16[256,512]{1,0:T(8,128)(2,1)S(1)}, bf16[256,512]{1,0:T(8,128)(2,1)S(1)}, u32[]{:S(2)}, u32[]{:S(2)}) collective-permute-start(bf16[256,512]{1,0:T(8,128)(2,1)S(1)} %broadcast_select_fusion.3), channel_id=1, source_target_pairs={{2,10},{10,2},{18,26},{26,18},{6,14},{14,6},{22,30},{30,22},{3,11}... | collective-permute-start | bytes 786440 | tf_op jit(solution)/shard_map/ppermute | solution.py:58
  52.3 5.6 %collective-permute-start.12 = (bf16[512,512]{1,0:T(8,128)(2,1)S(1)}, bf16[512,512]{1,0:T(8,128)(2,1)S(1)}, u32[]{:S(2)}, u32[]{:S(2)}) collective-permute-start(bf16[512,512]{1,0:T(8,128)(2,1)S(1)} %select_select_fusion.refs_0_), channel_id=1, source_target_pairs={{0,2},{2,0},{1,3},{3,1},{4,6},{6,4},{5,7},{7,5},{8,10},{10,8},{9,1... | collective-permute-start | bytes 1572872 | tf_op jit(solution)/shard_map/ppermute | solution.py:58
  58.5 0.9 %collective-permute-start.18 = (bf16[256,512]{1,0:T(8,128)(2,1)S(1)}, bf16[256,512]{1,0:T(8,128)(2,1)S(1)}, u32[]{:S(2)}, u32[]{:S(2)}) collective-permute-start(bf16[256,512]{1,0:T(8,128)(2,1)S(1)} %broadcast_select_fusion.6.refs_0_), channel_id=1, source_target_pairs={{2,6},{6,2},{10,14},{14,10},{18,22},{22,18},{26,30},{30,26},{3,7},... | collective-permute-start | bytes 786440 | tf_op jit(solution)/shard_map/ppermute | solution.py:58
  59.4 4.9 %collective-permute-start.21 = (bf16[256,512]{1,0:T(8,128)(2,1)S(1)}, bf16[256,512]{1,0:T(8,128)(2,1)S(1)}, u32[]{:S(2)}, u32[]{:S(2)}) collective-permute-start(bf16[256,512]{1,0:T(8,128)(2,1)S(1)} %broadcast_select_fusion.5.refs_1_), channel_id=1, source_target_pairs={{0,2},{2,0},{1,3},{3,1},{4,6},{6,4},{5,7},{7,5},{8,10},{10,8},{9,1... | collective-permute-start | bytes 786440 | tf_op jit(solution)/shard_map/ppermute | solution.py:58
  64.5 0.8 %collective-permute-start.22 = (bf16[256,512]{1,0:T(8,128)(2,1)S(1)}, bf16[256,512]{1,0:T(8,128)(2,1)S(1)}, u32[]{:S(2)}, u32[]{:S(2)}) collective-permute-start(bf16[256,512]{1,0:T(8,128)(2,1)S(1)} %broadcast_select_fusion.5.refs_1_), channel_id=1, source_target_pairs={{2,6},{6,2},{10,14},{14,10},{18,22},{22,18},{26,30},{30,26},{3,7},... | collective-permute-start | bytes 786440 | tf_op jit(solution)/shard_map/ppermute | solution.py:58
  65.3 2.3 %shard_map.67 = (bf16[1024,1024]{1,0:T(8,128)(2,1)S(1)}, bf16[2,512,1024]{2,1,0:T(8,128)(2,1)}) custom-call(s32[4]{0:T(128)S(1)} %get-tuple-element.42.flags, bf16[1024,1024]{1,0:T(8,128)(2,1)S(1)} %bitcast.20, f32[1024,1]{1,0:T(8,128)S(1)} %get-tuple-element.47.scl, bf16[1024,512]{1,0:T(8,128)(2,1)S(1)} %get-tuple-element.59.pan, ...), custom_call_target="tpu_custom_call" | custom-call | tf_op jit(solution)/shard_map/pallas_call | solution.py:94
  67.6 2.1 %shard_map.68 = (bf16[1024,1024]{1,0:T(8,128)(2,1)}, bf16[2,512,1024]{2,1,0:T(8,128)(2,1)}) custom-call(s32[4]{0:T(128)S(1)} %get-tuple-element.71.flags, bf16[1024,1024]{1,0:T(8,128)(2,1)S(1)} %get-tuple-element.68.cur, f32[1024,1]{1,0:T(8,128)S(1)} %get-tuple-element.69.scl, ...), custom_call_target="tpu_custom_call", output_to_operand_aliasing={{1}: (8, {})} | custom-call | tf_op jit(solution)/shard_map/pallas_call | solution.py:94
  70.0 1.3 %collective-permute-start.23 = (bf16[256,512]{1,0:T(8,128)(2,1)S(1)}, bf16[256,512]{1,0:T(8,128)(2,1)S(1)}, u32[]{:S(2)}, u32[]{:S(2)}) collective-permute-start(bf16[256,512]{1,0:T(8,128)(2,1)S(1)} %collective-permute-done.18.refs_0_), channel_id=1, source_target_pairs={{0,2},{2,0},{1,3},{3,1},{4,6},{6,4},{5,7},{7,5},{8,10},{10,8},{9,1... | collective-permute-start | bytes 786440 | tf_op jit(solution)/shard_map/ppermute | solution.py:58
  71.3 1.2 %collective-permute-done.23.refs_2_ = bf16[256,512]{1,0:T(8,128)(2,1)S(1)} collective-permute-done((bf16[256,512]{1,0:T(8,128)(2,1)S(1)}, bf16[256,512]{1,0:T(8,128)(2,1)S(1)}, u32[]{:S(2)}, u32[]{:S(2)}) %collective-permute-start.23) | collective-permute-done | bytes 262176 | tf_op jit(solution)/shard_map/ppermute | solution.py:58
  72.8 2.1 %shard_map.69 = (bf16[1024,1024]{1,0:T(8,128)(2,1)}, bf16[2,512,1024]{2,1,0:T(8,128)(2,1)}) custom-call(s32[4]{0:T(128)S(1)} %get-tuple-element.42.flags, bf16[1024,1024]{1,0:T(8,128)(2,1)S(1)} %get-tuple-element.68.cur, f32[1024,1]{1,0:T(8,128)S(1)} %get-tuple-element.69.scl, ...), custom_call_target="tpu_custom_call", output_to_operand_aliasing={{1}: (8, {}), {0}: (9, {})} | custom-call | tf_op jit(solution)/shard_map/pallas_call | solution.py:94
  (60 shorter events, 10.4 us)
Async XLA Ops:
  2.4 9.1 %collective-permute-start.1 = (bf16[1024,512]{1,0:T(8,128)(2,1)S(1)}, bf16[1024,512]{1,0:T(8,128)(2,1)S(1)}, u32[]{:S(2)}, u32[]{:S(2)}) collective-permute-start(bf16[1024,512]{1,0:T(8,128)(2,1)S(1)} %shard_map.59), channel_id=1, source_target_pairs={{0,1},{1,0},{2,10},{10,2},{3,11},{11,3},{8,12},{12,8},{9,13},{13,9... | collective-permute-start | bytes 3145736 | tf_op jit(solution)/shard_map/ppermute | solution.py:58
  4.0 6.2 %collective-permute-start.3 = (bf16[256,1024]{1,0:T(8,128)(2,1)S(1)}, bf16[256,1024]{1,0:T(8,128)(2,1)S(1)}, u32[]{:S(2)}, u32[]{:S(2)}) collective-permute-start(bf16[256,1024]{1,0:T(8,128)(2,1)S(1)} %select_bitcast_fusion), channel_id=1, source_target_pairs={{7,6},{11,10}} | collective-permute-start | bytes 1572872 | tf_op jit(solution)/shard_map/ppermute | solution.py:66
  9.4 6.3 %collective-permute-start = (bf16[1024,512]{1,0:T(8,128)(2,1)S(1)}, bf16[1024,512]{1,0:T(8,128)(2,1)S(1)}, u32[]{:S(2)}, u32[]{:S(2)}) collective-permute-start(bf16[1024,512]{1,0:T(8,128)(2,1)S(1)} %shard_map.61), channel_id=1, source_target_pairs={{0,1},{1,0}} | collective-permute-start | bytes 3145736 | tf_op jit(solution)/shard_map/ppermute | solution.py:62
  10.1 3.8 %collective-permute-start.5 = (bf16[256,1024]{1,0:T(8,128)(2,1)S(1)}, bf16[256,1024]{1,0:T(8,128)(2,1)S(1)}, u32[]{:S(2)}, u32[]{:S(2)}) collective-permute-start(bf16[256,1024]{1,0:T(8,128)(2,1)S(1)} %collective-permute-done.3), channel_id=1, source_target_pairs={{10,2}} | collective-permute-start | bytes 1572872 | tf_op jit(solution)/shard_map/ppermute | solution.py:66
  10.8 3.1 %collective-permute-start.4 = (bf16[256,1024]{1,0:T(8,128)(2,1)S(1)}, bf16[256,1024]{1,0:T(8,128)(2,1)S(1)}, u32[]{:S(2)}, u32[]{:S(2)}) collective-permute-start(bf16[256,1024]{1,0:T(8,128)(2,1)S(1)} %collective-permute-done.3), channel_id=1, source_target_pairs={{6,2}} | collective-permute-start | bytes 1572872 | tf_op jit(solution)/shard_map/ppermute | solution.py:66
  12.1 2.3 %collective-permute-start.2 = (bf16[512,512]{1,0:T(8,128)(2,1)S(1)}, bf16[512,512]{1,0:T(8,128)(2,1)S(1)}, u32[]{:S(2)}, u32[]{:S(2)}) collective-permute-start(bf16[512,512]{1,0:T(8,128)(2,1)S(1)} %shard_map.62), channel_id=1, source_target_pairs={{0,2},{2,0},{1,3},{3,1},{4,6},{6,4},{5,7},{7,5},{8,10},{10,8},{9,1... | collective-permute-start | bytes 1572872 | tf_op jit(solution)/shard_map/ppermute | solution.py:58
  12.9 3.8 %collective-permute-start.6 = (bf16[512,512]{1,0:T(8,128)(2,1)S(1)}, bf16[512,512]{1,0:T(8,128)(2,1)S(1)}, u32[]{:S(2)}, u32[]{:S(2)}) collective-permute-start(bf16[512,512]{1,0:T(8,128)(2,1)S(1)} %shard_map.62), channel_id=1, source_target_pairs={{0,4},{1,5}} | collective-permute-start | bytes 1572872 | tf_op jit(solution)/shard_map/ppermute | solution.py:66
  14.9 3.8 %collective-permute-start.10 = (bf16[512,512]{1,0:T(8,128)(2,1)S(1)}, bf16[512,512]{1,0:T(8,128)(2,1)S(1)}, u32[]{:S(2)}, u32[]{:S(2)}) collective-permute-start(bf16[512,512]{1,0:T(8,128)(2,1)S(1)} %get-tuple-element.56), channel_id=1, source_target_pairs={{2,6},{3,7}} | collective-permute-start | bytes 1572872 | tf_op jit(solution)/shard_map/ppermute | solution.py:66
  16.2 2.0 %collective-permute-start.8 = (bf16[512,512]{1,0:T(8,128)(2,1)S(1)}, bf16[512,512]{1,0:T(8,128)(2,1)S(1)}, u32[]{:S(2)}, u32[]{:S(2)}) collective-permute-start(bf16[512,512]{1,0:T(8,128)(2,1)S(1)} %shard_map.64), channel_id=1, source_target_pairs={{0,2},{2,0},{1,3},{3,1},{4,6},{6,4},{5,7},{7,5},{8,10},{10,8},{9,1... | collective-permute-start | bytes 1572872 | tf_op jit(solution)/shard_map/ppermute | solution.py:58
  16.8 2.7 %collective-permute-start.7 = (bf16[512,512]{1,0:T(8,128)(2,1)S(1)}, bf16[512,512]{1,0:T(8,128)(2,1)S(1)}, u32[]{:S(2)}, u32[]{:S(2)}) collective-permute-start(bf16[512,512]{1,0:T(8,128)(2,1)S(1)} %broadcast_select_fusion.2), channel_id=1, source_target_pairs={{0,16},{1,17},{4,20},{5,21},{2,7},{3,6}} | collective-permute-start | bytes 1572872 | tf_op jit(solution)/shard_map/ppermute | solution.py:66
  18.8 1.4 %collective-permute-start.11 = (bf16[512,512]{1,0:T(8,128)(2,1)S(1)}, bf16[512,512]{1,0:T(8,128)(2,1)S(1)}, u32[]{:S(2)}, u32[]{:S(2)}) collective-permute-start(bf16[512,512]{1,0:T(8,128)(2,1)S(1)} %broadcast_select_fusion.1), channel_id=1, source_target_pairs={{0,8},{1,9},{4,12},{5,13},{2,3},{3,2}} | collective-permute-start | bytes 1572872 | tf_op jit(solution)/shard_map/ppermute | solution.py:66
  21.0 5.3 %collective-permute-start.13 = (bf16[256,512]{1,0:T(8,128)(2,1)S(1)}, bf16[256,512]{1,0:T(8,128)(2,1)S(1)}, u32[]{:S(2)}, u32[]{:S(2)}) collective-permute-start(bf16[256,512]{1,0:T(8,128)(2,1)S(1)} %get-tuple-element.85), channel_id=1, source_target_pairs={{2,18},{18,2},{6,22},{22,6},{3,19},{19,3},{7,23},{23,7},{0,4},{4,0... | collective-permute-start | bytes 786440 | tf_op jit(solution)/shard_map/ppermute | solution.py:58
  21.3 28.2 %collective-permute-start.14 = (bf16[256,512]{1,0:T(8,128)(2,1)S(1)}, bf16[256,512]{1,0:T(8,128)(2,1)S(1)}, u32[]{:S(2)}, u32[]{:S(2)}) collective-permute-start(bf16[256,512]{1,0:T(8,128)(2,1)S(1)} %get-tuple-element.84), channel_id=1, source_target_pairs={{2,18},{18,2},{6,22},{22,6},{3,19},{19,3},{7,23},{23,7},{0,4},{4,0... | collective-permute-start | bytes 786440 | tf_op jit(solution)/shard_map/ppermute | solution.py:58
  26.3 32.2 %collective-permute-start.17 = (bf16[256,512]{1,0:T(8,128)(2,1)S(1)}, bf16[256,512]{1,0:T(8,128)(2,1)S(1)}, u32[]{:S(2)}, u32[]{:S(2)}) collective-permute-start(bf16[256,512]{1,0:T(8,128)(2,1)S(1)} %broadcast_select_fusion.4), channel_id=1, source_target_pairs={{2,10},{10,2},{18,26},{26,18},{6,14},{14,6},{22,30},{30,22},{3,11}... | collective-permute-start | bytes 786440 | tf_op jit(solution)/shard_map/ppermute | solution.py:58
  49.6 9.8 %collective-permute-start.19 = (bf16[256,512]{1,0:T(8,128)(2,1)S(1)}, bf16[256,512]{1,0:T(8,128)(2,1)S(1)}, u32[]{:S(2)}, u32[]{:S(2)}) collective-permute-start(bf16[256,512]{1,0:T(8,128)(2,1)S(1)} %broadcast_select_fusion.3), channel_id=1, source_target_pairs={{2,10},{10,2},{18,26},{26,18},{6,14},{14,6},{22,30},{30,22},{3,11}... | collective-permute-start | bytes 786440 | tf_op jit(solution)/shard_map/ppermute | solution.py:58
  52.3 12.9 %collective-permute-start.12 = (bf16[512,512]{1,0:T(8,128)(2,1)S(1)}, bf16[512,512]{1,0:T(8,128)(2,1)S(1)}, u32[]{:S(2)}, u32[]{:S(2)}) collective-permute-start(bf16[512,512]{1,0:T(8,128)(2,1)S(1)} %select_select_fusion.refs_0_), channel_id=1, source_target_pairs={{0,2},{2,0},{1,3},{3,1},{4,6},{6,4},{5,7},{7,5},{8,10},{10,8},{9,1... | collective-permute-start | bytes 1572872 | tf_op jit(solution)/shard_map/ppermute | solution.py:58
  58.0 6.4 %collective-permute-start.16 = (bf16[256,512]{1,0:T(8,128)(2,1)S(1)}, bf16[256,512]{1,0:T(8,128)(2,1)S(1)}, u32[]{:S(2)}, u32[]{:S(2)}) collective-permute-start(bf16[256,512]{1,0:T(8,128)(2,1)S(1)} %collective-permute-done.14.refs_3_), channel_id=1, source_target_pairs={{0,2},{2,0},{1,3},{3,1},{4,6},{6,4},{5,7},{7,5},{8,10},{10,8},{9,1... | collective-permute-start | bytes 786440 | tf_op jit(solution)/shard_map/ppermute | solution.py:58
  58.1 6.4 %collective-permute-start.15 = (bf16[256,512]{1,0:T(8,128)(2,1)S(1)}, bf16[256,512]{1,0:T(8,128)(2,1)S(1)}, u32[]{:S(2)}, u32[]{:S(2)}) collective-permute-start(bf16[256,512]{1,0:T(8,128)(2,1)S(1)} %collective-permute-done.13.refs_2_), channel_id=1, source_target_pairs={{0,2},{2,0},{1,3},{3,1},{4,6},{6,4},{5,7},{7,5},{8,10},{10,8},{9,1... | collective-permute-start | bytes 786440 | tf_op jit(solution)/shard_map/ppermute | solution.py:58
  58.5 9.1 %collective-permute-start.18 = (bf16[256,512]{1,0:T(8,128)(2,1)S(1)}, bf16[256,512]{1,0:T(8,128)(2,1)S(1)}, u32[]{:S(2)}, u32[]{:S(2)}) collective-permute-start(bf16[256,512]{1,0:T(8,128)(2,1)S(1)} %broadcast_select_fusion.6.refs_0_), channel_id=1, source_target_pairs={{2,6},{6,2},{10,14},{14,10},{18,22},{22,18},{26,30},{30,26},{3,7},... | collective-permute-start | bytes 786440 | tf_op jit(solution)/shard_map/ppermute | solution.py:58
  59.4 8.2 %collective-permute-start.21 = (bf16[256,512]{1,0:T(8,128)(2,1)S(1)}, bf16[256,512]{1,0:T(8,128)(2,1)S(1)}, u32[]{:S(2)}, u32[]{:S(2)}) collective-permute-start(bf16[256,512]{1,0:T(8,128)(2,1)S(1)} %broadcast_select_fusion.5.refs_1_), channel_id=1, source_target_pairs={{0,2},{2,0},{1,3},{3,1},{4,6},{6,4},{5,7},{7,5},{8,10},{10,8},{9,1... | collective-permute-start | bytes 786440 | tf_op jit(solution)/shard_map/ppermute | solution.py:58
  64.4 3.2 %collective-permute-start.20 = (bf16[256,512]{1,0:T(8,128)(2,1)S(1)}, bf16[256,512]{1,0:T(8,128)(2,1)S(1)}, u32[]{:S(2)}, u32[]{:S(2)}) collective-permute-start(bf16[256,512]{1,0:T(8,128)(2,1)S(1)} %broadcast_select_fusion.6.refs_0_), channel_id=1, source_target_pairs={{0,2},{2,0},{1,3},{3,1},{4,6},{6,4},{5,7},{7,5},{8,10},{10,8},{9,1... | collective-permute-start | bytes 786440 | tf_op jit(solution)/shard_map/ppermute | solution.py:58
  64.5 5.5 %collective-permute-start.22 = (bf16[256,512]{1,0:T(8,128)(2,1)S(1)}, bf16[256,512]{1,0:T(8,128)(2,1)S(1)}, u32[]{:S(2)}, u32[]{:S(2)}) collective-permute-start(bf16[256,512]{1,0:T(8,128)(2,1)S(1)} %broadcast_select_fusion.5.refs_1_), channel_id=1, source_target_pairs={{2,6},{6,2},{10,14},{14,10},{18,22},{22,18},{26,30},{30,26},{3,7},... | collective-permute-start | bytes 786440 | tf_op jit(solution)/shard_map/ppermute | solution.py:58
  70.0 2.4 %collective-permute-start.23 = (bf16[256,512]{1,0:T(8,128)(2,1)S(1)}, bf16[256,512]{1,0:T(8,128)(2,1)S(1)}, u32[]{:S(2)}, u32[]{:S(2)}) collective-permute-start(bf16[256,512]{1,0:T(8,128)(2,1)S(1)} %collective-permute-done.18.refs_0_), channel_id=1, source_target_pairs={{0,2},{2,0},{1,3},{3,1},{4,6},{6,4},{5,7},{7,5},{8,10},{10,8},{9,1... | collective-permute-start | bytes 786440 | tf_op jit(solution)/shard_map/ppermute | solution.py:58
  71.3 1.5 %collective-permute-start.24 = (bf16[256,512]{1,0:T(8,128)(2,1)S(1)}, bf16[256,512]{1,0:T(8,128)(2,1)S(1)}, u32[]{:S(2)}, u32[]{:S(2)}) collective-permute-start(bf16[256,512]{1,0:T(8,128)(2,1)S(1)} %collective-permute-done.22.refs_1_), channel_id=1, source_target_pairs={{0,2},{2,0},{1,3},{3,1},{4,6},{6,4},{5,7},{7,5},{8,10},{10,8},{9,1... | collective-permute-start | bytes 786440 | tf_op jit(solution)/shard_map/ppermute | solution.py:58
  (6 other events, 12.6 us)

commit v7 on v6

--- a/solution.py
+++ b/solution.py
@@ -130,10 +130,10 @@
     def kernel(flags, cur, got, inv, out):
         @pl.when(flags[0] == 0)
         def _():
-            for t in range(0, half, TILE):
-                here = cur[:, start + t : start + t + TILE]
-                fan = (here.astype(F32) + got[:, t : t + TILE].astype(F32)).astype(BF)
-                out[:, t : t + TILE] = dot(inv[0], fan).astype(BF)
+            for t in range(0, half, half):
+                here = cur[:, start + t : start + t + half]
+                fan = (here.astype(F32) + got[:, t : t + half].astype(F32)).astype(BF)
+                out[:, t : t + half] = dot(inv[0], fan).astype(BF)
 
     return call(
         kernel, (flags, share, far, inverse), jax.ShapeDtypeStruct((half, half), BF), [SMEM] + [VMEM] * 3, VMEM
@@ -147,9 +147,9 @@
     def kernel(flags, cur, scl, pan, sol, inv, top, bottom, own, message):
         @pl.when(flags[0] == 1)
         def _():
-            for t in range(0, half, TILE):
-                cols = slice(t, t + TILE)
-                here = cur[:, start + t : start + t + TILE]
+            for t in range(0, half, half):
+                cols = slice(t, t + half)
+                here = cur[:, start + t : start + t + half]
                 newer = (here.astype(F32) - scl[...] * dot(pan[...], sol[:, cols])).astype(BF)
 
                 @pl.when(flags[1] == 0)
@@ -341,10 +341,10 @@
         + [((0, c_, 0, 1), (1, 1 - c_, 0, 1)) for c_ in COLS],
     )
     own, message = second_block(flags, share, scale0, after(panel0, outward), inward, inverse, far_top, far_bottom, half)
-    answer = send(
+    answer = swap(
         jnp.where(first_core, mine0, after(message, own_hop)),
-        [((x_, c_, 0, 0), (x_, c_, 1, 0)) for x_ in (0, 1) for c_ in COLS]
-        + [((0, c_, 0, 1), (0, 1 - c_, 0, 1)) for c_ in COLS],
+        seconds + [((x_, c_, 0, 0), (x_, c_, 1, 0)) for x_ in (0, 1) for c_ in COLS],
+        "x",
     )
     last = send(after(across, message), [((x_, c_, 2, 0), (x_, c_, 3, 0)) for x_ in (0, 1) for c_ in COLS])
 

time: 75.3 us -> 75.2 us (level)
    ppermute x8 -> x7, starting transfers between devices: 5.54 us -> 4.84 us  [send(): lax.ppermute(value, AXES, [(device(*a), device(*b)) for a, b in wanted])]
    ppermute x16 -> x17, waiting for transfers between devices: 6.7 us -> 7.32 us  [swap(): return lax.ppermute(value, AXES, paired(wanted, side))]
    ppermute x16 -> x17, starting transfers between devices: 43.5 us -> 43.6 us  [swap(): return lax.ppermute(value, AXES, paired(wanted, side))]
where the time goes in v7:
time: 75.2 us; the launch traced here: 74.9 us
  starting transfers between devices  49.2 us (65%)
  Pallas kernels  9.92 us (13%)
  waiting for transfers between devices  7.34 us (10%)
  local copies, waits for them, and re-layouts  6.89 us (9%)
  between operations  1 us (1%)
    ppermute x17, starting transfers between devices, swap(): return lax.ppermute(value, AXES, paired(wanted, side))  43.6 us
    pallas_call x11, Pallas kernels, call(): pl.pallas_call(kernel, in_specs=ins, out_specs=outs, out_shape=shapes, sc...  9.92 us
    ppermute x17, waiting for transfers between devices, swap(): return lax.ppermute(value, AXES, paired(wanted, side))  7.32 us
    ppermute x7, starting transfers between devices, send(): lax.ppermute(value, AXES, [(device(*a), device(*b)) for a, b in wanted])  4.84 us
    unnamed x10, local copies, waits for them, and re-layouts  3.3 us
    slice x1, local copies, waits for them, and re-layouts, body(): panel[:, 1, :]  2.98 us
  transfers between devices with their start and end apart: 25, of which 6 were waited for; matrix products, arithmetic and copies ran while one was open for 5% of the time, Pallas kernels for 10%

profile of v7, /device:TPU:29, one launch (start us, length us, event | category | flops | bytes accessed | tf_op | source)
XLA Modules:
  0.0 74.9 jit_solution(9611030196665091745)
XLA Ops:
  0.7 1.6 %copy-done = bf16[1024,1,1024]{2,0,1:T(8,128)(2,1)S(1)} copy-done((bf16[1024,1,1024]{2,0,1:T(8,128)(2,1)S(1)}, bf16[1024,1,1024]{2,0,1:T(8,128)(2,1)}, u32[]{:S(2)}) %copy-start) | copy-done | bytes 2097176
  2.4 0.7 collective-permute-start.1
  3.2 0.7 copy-done.2
  4.0 0.7 collective-permute-start.3
  4.7 3.0 %fusion = (bf16[1024,1,512]{2,1,0:T(2,128)(2,1)S(1)}, bf16[1024,1,512]{2,1,0:T(2,128)(2,1)S(1)}) fusion(bf16[1024,2,512]{2,1,0:T(2,128)(2,1)S(1)} %copy-done.4), kind=kLoop, calls=%fused_computation.16 | loop fusion | bytes 4194304 | tf_op jit(solution)/shard_map/slice | solution.py:321
  8.3 1.0 %copy-done.1 = bf16[1024,1,1024]{2,0,1:T(8,128)(2,1)S(1)} copy-done((bf16[1024,1,1024]{2,0,1:T(8,128)(2,1)S(1)}, bf16[1024,1,1024]{2,0,1:T(8,128)(2,1)}, u32[]{:S(2)}) %copy-start.1) | copy-done | bytes 2097176
  9.4 0.7 collective-permute-start
  10.1 0.7 collective-permute-start.5
  12.1 0.7 collective-permute-start.2
  17.5 0.7 collective-permute-done.8.sol
  20.0 0.8 %collective-permute-done.11.b0 = bf16[512,512]{1,0:T(8,128)(2,1)S(1)} collective-permute-done((bf16[512,512]{1,0:T(8,128)(2,1)S(1)}, bf16[512,512]{1,0:T(8,128)(2,1)S(1)}, u32[]{:S(2)}, u32[]{:S(2)}) %collective-permute-start.11) | collective-permute-done | bytes 524320 | tf_op jit(solution)/shard_map/ppermute | solution.py:58
  21.9 1.2 %collective-permute-start.14 = (bf16[256,512]{1,0:T(8,128)(2,1)S(1)}, bf16[256,512]{1,0:T(8,128)(2,1)S(1)}, u32[]{:S(2)}, u32[]{:S(2)}) collective-permute-start(bf16[256,512]{1,0:T(8,128)(2,1)S(1)} %get-tuple-element.84), channel_id=1, source_target_pairs={{2,18},{18,2},{6,22},{22,6},{3,19},{19,3},{7,23},{23,7},{0,4},{4,0... | collective-permute-start | bytes 786440 | tf_op jit(solution)/shard_map/ppermute | solution.py:58
  23.1 3.8 %collective-permute-done.13.refs_2_ = bf16[256,512]{1,0:T(8,128)(2,1)S(1)} collective-permute-done((bf16[256,512]{1,0:T(8,128)(2,1)S(1)}, bf16[256,512]{1,0:T(8,128)(2,1)S(1)}, u32[]{:S(2)}, u32[]{:S(2)}) %collective-permute-start.13) | collective-permute-done | bytes 262176 | tf_op jit(solution)/shard_map/ppermute | solution.py:58
  26.9 20.6 %collective-permute-start.17 = (bf16[256,512]{1,0:T(8,128)(2,1)S(1)}, bf16[256,512]{1,0:T(8,128)(2,1)S(1)}, u32[]{:S(2)}, u32[]{:S(2)}) collective-permute-start(bf16[256,512]{1,0:T(8,128)(2,1)S(1)} %broadcast_select_fusion.4), channel_id=1, source_target_pairs={{2,10},{10,2},{18,26},{26,18},{6,14},{14,6},{22,30},{30,22},{3,11}... | collective-permute-start | bytes 786440 | tf_op jit(solution)/shard_map/ppermute | solution.py:58
  47.6 2.8 %collective-permute-start.19 = (bf16[256,512]{1,0:T(8,128)(2,1)S(1)}, bf16[256,512]{1,0:T(8,128)(2,1)S(1)}, u32[]{:S(2)}, u32[]{:S(2)}) collective-permute-start(bf16[256,512]{1,0:T(8,128)(2,1)S(1)} %broadcast_select_fusion.3), channel_id=1, source_target_pairs={{2,10},{10,2},{18,26},{26,18},{6,14},{14,6},{22,30},{30,22},{3,11}... | collective-permute-start | bytes 786440 | tf_op jit(solution)/shard_map/ppermute | solution.py:58
  50.3 7.6 %collective-permute-start.12 = (bf16[512,512]{1,0:T(8,128)(2,1)S(1)}, bf16[512,512]{1,0:T(8,128)(2,1)S(1)}, u32[]{:S(2)}, u32[]{:S(2)}) collective-permute-start(bf16[512,512]{1,0:T(8,128)(2,1)S(1)} %select_select_fusion.refs_0_), channel_id=1, source_target_pairs={{0,2},{2,0},{1,3},{3,1},{4,6},{6,4},{5,7},{7,5},{8,10},{10,8},{9,1... | collective-permute-start | bytes 1572872 | tf_op jit(solution)/shard_map/ppermute | solution.py:58
  58.5 1.2 %collective-permute-start.18 = (bf16[256,512]{1,0:T(8,128)(2,1)S(1)}, bf16[256,512]{1,0:T(8,128)(2,1)S(1)}, u32[]{:S(2)}, u32[]{:S(2)}) collective-permute-start(bf16[256,512]{1,0:T(8,128)(2,1)S(1)} %broadcast_select_fusion.6.refs_0_), channel_id=1, source_target_pairs={{2,6},{6,2},{10,14},{14,10},{18,22},{22,18},{26,30},{30,26},{3,7},... | collective-permute-start | bytes 786440 | tf_op jit(solution)/shard_map/ppermute | solution.py:58
  59.8 4.6 %collective-permute-start.21 = (bf16[256,512]{1,0:T(8,128)(2,1)S(1)}, bf16[256,512]{1,0:T(8,128)(2,1)S(1)}, u32[]{:S(2)}, u32[]{:S(2)}) collective-permute-start(bf16[256,512]{1,0:T(8,128)(2,1)S(1)} %broadcast_select_fusion.5.refs_1_), channel_id=1, source_target_pairs={{0,2},{2,0},{1,3},{3,1},{4,6},{6,4},{5,7},{7,5},{8,10},{10,8},{9,1... | collective-permute-start | bytes 786440 | tf_op jit(solution)/shard_map/ppermute | solution.py:58
  64.5 1.1 %collective-permute-start.22 = (bf16[256,512]{1,0:T(8,128)(2,1)S(1)}, bf16[256,512]{1,0:T(8,128)(2,1)S(1)}, u32[]{:S(2)}, u32[]{:S(2)}) collective-permute-start(bf16[256,512]{1,0:T(8,128)(2,1)S(1)} %broadcast_select_fusion.5.refs_1_), channel_id=1, source_target_pairs={{2,6},{6,2},{10,14},{14,10},{18,22},{22,18},{26,30},{30,26},{3,7},... | collective-permute-start | bytes 786440 | tf_op jit(solution)/shard_map/ppermute | solution.py:58
  65.6 2.3 %shard_map.67 = (bf16[1024,1024]{1,0:T(8,128)(2,1)S(1)}, bf16[2,512,1024]{2,1,0:T(8,128)(2,1)}) custom-call(s32[4]{0:T(128)S(1)} %get-tuple-element.42.flags, bf16[1024,1024]{1,0:T(8,128)(2,1)S(1)} %bitcast.20, f32[1024,1]{1,0:T(8,128)S(1)} %get-tuple-element.47.scl, bf16[1024,512]{1,0:T(8,128)(2,1)S(1)} %get-tuple-element.59.pan, ...), custom_call_target="tpu_custom_call" | custom-call | tf_op jit(solution)/shard_map/pallas_call | solution.py:94
  68.0 2.1 %shard_map.68 = (bf16[1024,1024]{1,0:T(8,128)(2,1)}, bf16[2,512,1024]{2,1,0:T(8,128)(2,1)}) custom-call(s32[4]{0:T(128)S(1)} %get-tuple-element.71.flags, bf16[1024,1024]{1,0:T(8,128)(2,1)S(1)} %get-tuple-element.68.cur, f32[1024,1]{1,0:T(8,128)S(1)} %get-tuple-element.69.scl, ...), custom_call_target="tpu_custom_call", output_to_operand_aliasing={{1}: (8, {})} | custom-call | tf_op jit(solution)/shard_map/pallas_call | solution.py:94
  70.1 1.2 %collective-permute-start.23 = (bf16[256,512]{1,0:T(8,128)(2,1)S(1)}, bf16[256,512]{1,0:T(8,128)(2,1)S(1)}, u32[]{:S(2)}, u32[]{:S(2)}) collective-permute-start(bf16[256,512]{1,0:T(8,128)(2,1)S(1)} %collective-permute-done.18.refs_0_), channel_id=1, source_target_pairs={{0,2},{2,0},{1,3},{3,1},{4,6},{6,4},{5,7},{7,5},{8,10},{10,8},{9,1... | collective-permute-start | bytes 786440 | tf_op jit(solution)/shard_map/ppermute | solution.py:58
  71.3 1.2 %collective-permute-done.23.refs_2_ = bf16[256,512]{1,0:T(8,128)(2,1)S(1)} collective-permute-done((bf16[256,512]{1,0:T(8,128)(2,1)S(1)}, bf16[256,512]{1,0:T(8,128)(2,1)S(1)}, u32[]{:S(2)}, u32[]{:S(2)}) %collective-permute-start.23) | collective-permute-done | bytes 262176 | tf_op jit(solution)/shard_map/ppermute | solution.py:58
  72.8 2.1 %shard_map.69 = (bf16[1024,1024]{1,0:T(8,128)(2,1)}, bf16[2,512,1024]{2,1,0:T(8,128)(2,1)}) custom-call(s32[4]{0:T(128)S(1)} %get-tuple-element.42.flags, bf16[1024,1024]{1,0:T(8,128)(2,1)S(1)} %get-tuple-element.68.cur, f32[1024,1]{1,0:T(8,128)S(1)} %get-tuple-element.69.scl, ...), custom_call_target="tpu_custom_call", output_to_operand_aliasing={{1}: (8, {}), {0}: (9, {})} | custom-call | tf_op jit(solution)/shard_map/pallas_call | solution.py:94
  (60 shorter events, 10.6 us)
Async XLA Ops:
  2.4 9.1 %collective-permute-start.1 = (bf16[1024,512]{1,0:T(8,128)(2,1)S(1)}, bf16[1024,512]{1,0:T(8,128)(2,1)S(1)}, u32[]{:S(2)}, u32[]{:S(2)}) collective-permute-start(bf16[1024,512]{1,0:T(8,128)(2,1)S(1)} %shard_map.59), channel_id=1, source_target_pairs={{0,1},{1,0},{2,10},{10,2},{3,11},{11,3},{8,12},{12,8},{9,13},{13,9... | collective-permute-start | bytes 3145736 | tf_op jit(solution)/shard_map/ppermute | solution.py:58
  4.0 6.2 %collective-permute-start.3 = (bf16[256,1024]{1,0:T(8,128)(2,1)S(1)}, bf16[256,1024]{1,0:T(8,128)(2,1)S(1)}, u32[]{:S(2)}, u32[]{:S(2)}) collective-permute-start(bf16[256,1024]{1,0:T(8,128)(2,1)S(1)} %select_bitcast_fusion), channel_id=1, source_target_pairs={{7,6},{11,10}} | collective-permute-start | bytes 1572872 | tf_op jit(solution)/shard_map/ppermute | solution.py:66
  9.4 6.3 %collective-permute-start = (bf16[1024,512]{1,0:T(8,128)(2,1)S(1)}, bf16[1024,512]{1,0:T(8,128)(2,1)S(1)}, u32[]{:S(2)}, u32[]{:S(2)}) collective-permute-start(bf16[1024,512]{1,0:T(8,128)(2,1)S(1)} %shard_map.61), channel_id=1, source_target_pairs={{0,1},{1,0}} | collective-permute-start | bytes 3145736 | tf_op jit(solution)/shard_map/ppermute | solution.py:62
  10.1 3.8 %collective-permute-start.5 = (bf16[256,1024]{1,0:T(8,128)(2,1)S(1)}, bf16[256,1024]{1,0:T(8,128)(2,1)S(1)}, u32[]{:S(2)}, u32[]{:S(2)}) collective-permute-start(bf16[256,1024]{1,0:T(8,128)(2,1)S(1)} %collective-permute-done.3), channel_id=1, source_target_pairs={{10,2}} | collective-permute-start | bytes 1572872 | tf_op jit(solution)/shard_map/ppermute | solution.py:66
  10.8 3.1 %collective-permute-start.4 = (bf16[256,1024]{1,0:T(8,128)(2,1)S(1)}, bf16[256,1024]{1,0:T(8,128)(2,1)S(1)}, u32[]{:S(2)}, u32[]{:S(2)}) collective-permute-start(bf16[256,1024]{1,0:T(8,128)(2,1)S(1)} %collective-permute-done.3), channel_id=1, source_target_pairs={{6,2}} | collective-permute-start | bytes 1572872 | tf_op jit(solution)/shard_map/ppermute | solution.py:66
  12.1 2.3 %collective-permute-start.2 = (bf16[512,512]{1,0:T(8,128)(2,1)S(1)}, bf16[512,512]{1,0:T(8,128)(2,1)S(1)}, u32[]{:S(2)}, u32[]{:S(2)}) collective-permute-start(bf16[512,512]{1,0:T(8,128)(2,1)S(1)} %shard_map.62), channel_id=1, source_target_pairs={{0,2},{2,0},{1,3},{3,1},{4,6},{6,4},{5,7},{7,5},{8,10},{10,8},{9,1... | collective-permute-start | bytes 1572872 | tf_op jit(solution)/shard_map/ppermute | solution.py:58
  12.9 3.8 %collective-permute-start.6 = (bf16[512,512]{1,0:T(8,128)(2,1)S(1)}, bf16[512,512]{1,0:T(8,128)(2,1)S(1)}, u32[]{:S(2)}, u32[]{:S(2)}) collective-permute-start(bf16[512,512]{1,0:T(8,128)(2,1)S(1)} %shard_map.62), channel_id=1, source_target_pairs={{0,4},{1,5}} | collective-permute-start | bytes 1572872 | tf_op jit(solution)/shard_map/ppermute | solution.py:66
  14.9 3.8 %collective-permute-start.10 = (bf16[512,512]{1,0:T(8,128)(2,1)S(1)}, bf16[512,512]{1,0:T(8,128)(2,1)S(1)}, u32[]{:S(2)}, u32[]{:S(2)}) collective-permute-start(bf16[512,512]{1,0:T(8,128)(2,1)S(1)} %get-tuple-element.56), channel_id=1, source_target_pairs={{2,6},{3,7}} | collective-permute-start | bytes 1572872 | tf_op jit(solution)/shard_map/ppermute | solution.py:66
  16.2 2.0 %collective-permute-start.8 = (bf16[512,512]{1,0:T(8,128)(2,1)S(1)}, bf16[512,512]{1,0:T(8,128)(2,1)S(1)}, u32[]{:S(2)}, u32[]{:S(2)}) collective-permute-start(bf16[512,512]{1,0:T(8,128)(2,1)S(1)} %shard_map.64), channel_id=1, source_target_pairs={{0,2},{2,0},{1,3},{3,1},{4,6},{6,4},{5,7},{7,5},{8,10},{10,8},{9,1... | collective-permute-start | bytes 1572872 | tf_op jit(solution)/shard_map/ppermute | solution.py:58
  16.8 2.5 %collective-permute-start.7 = (bf16[512,512]{1,0:T(8,128)(2,1)S(1)}, bf16[512,512]{1,0:T(8,128)(2,1)S(1)}, u32[]{:S(2)}, u32[]{:S(2)}) collective-permute-start(bf16[512,512]{1,0:T(8,128)(2,1)S(1)} %broadcast_select_fusion.2), channel_id=1, source_target_pairs={{0,16},{1,17},{4,20},{5,21},{2,7},{3,6}} | collective-permute-start | bytes 1572872 | tf_op jit(solution)/shard_map/ppermute | solution.py:66
  18.8 2.0 %collective-permute-start.11 = (bf16[512,512]{1,0:T(8,128)(2,1)S(1)}, bf16[512,512]{1,0:T(8,128)(2,1)S(1)}, u32[]{:S(2)}, u32[]{:S(2)}) collective-permute-start(bf16[512,512]{1,0:T(8,128)(2,1)S(1)} %broadcast_select_fusion.1), channel_id=1, source_target_pairs={{2,3},{3,2},{0,8},{8,0},{1,9},{9,1},{4,12},{12,4},{5,13},{13,5},{1... | collective-permute-start | bytes 1572872 | tf_op jit(solution)/shard_map/ppermute | solution.py:58
  19.3 2.1 %collective-permute-start.9 = (bf16[512,512]{1,0:T(8,128)(2,1)S(1)}, bf16[512,512]{1,0:T(8,128)(2,1)S(1)}, u32[]{:S(2)}, u32[]{:S(2)}) collective-permute-start(bf16[512,512]{1,0:T(8,128)(2,1)S(1)} %collective-permute-done.7.b1), channel_id=1, source_target_pairs={{16,24},{17,25},{20,28},{21,29}} | collective-permute-start | bytes 1572872 | tf_op jit(solution)/shard_map/ppermute | solution.py:66
  21.6 5.3 %collective-permute-start.13 = (bf16[256,512]{1,0:T(8,128)(2,1)S(1)}, bf16[256,512]{1,0:T(8,128)(2,1)S(1)}, u32[]{:S(2)}, u32[]{:S(2)}) collective-permute-start(bf16[256,512]{1,0:T(8,128)(2,1)S(1)} %get-tuple-element.85), channel_id=1, source_target_pairs={{2,18},{18,2},{6,22},{22,6},{3,19},{19,3},{7,23},{23,7},{0,4},{4,0... | collective-permute-start | bytes 786440 | tf_op jit(solution)/shard_map/ppermute | solution.py:58
  21.9 25.7 %collective-permute-start.14 = (bf16[256,512]{1,0:T(8,128)(2,1)S(1)}, bf16[256,512]{1,0:T(8,128)(2,1)S(1)}, u32[]{:S(2)}, u32[]{:S(2)}) collective-permute-start(bf16[256,512]{1,0:T(8,128)(2,1)S(1)} %get-tuple-element.84), channel_id=1, source_target_pairs={{2,18},{18,2},{6,22},{22,6},{3,19},{19,3},{7,23},{23,7},{0,4},{4,0... | collective-permute-start | bytes 786440 | tf_op jit(solution)/shard_map/ppermute | solution.py:58
  26.9 31.6 %collective-permute-start.17 = (bf16[256,512]{1,0:T(8,128)(2,1)S(1)}, bf16[256,512]{1,0:T(8,128)(2,1)S(1)}, u32[]{:S(2)}, u32[]{:S(2)}) collective-permute-start(bf16[256,512]{1,0:T(8,128)(2,1)S(1)} %broadcast_select_fusion.4), channel_id=1, source_target_pairs={{2,10},{10,2},{18,26},{26,18},{6,14},{14,6},{22,30},{30,22},{3,11}... | collective-permute-start | bytes 786440 | tf_op jit(solution)/shard_map/ppermute | solution.py:58
  47.6 12.2 %collective-permute-start.19 = (bf16[256,512]{1,0:T(8,128)(2,1)S(1)}, bf16[256,512]{1,0:T(8,128)(2,1)S(1)}, u32[]{:S(2)}, u32[]{:S(2)}) collective-permute-start(bf16[256,512]{1,0:T(8,128)(2,1)S(1)} %broadcast_select_fusion.3), channel_id=1, source_target_pairs={{2,10},{10,2},{18,26},{26,18},{6,14},{14,6},{22,30},{30,22},{3,11}... | collective-permute-start | bytes 786440 | tf_op jit(solution)/shard_map/ppermute | solution.py:58
  50.3 15.3 %collective-permute-start.12 = (bf16[512,512]{1,0:T(8,128)(2,1)S(1)}, bf16[512,512]{1,0:T(8,128)(2,1)S(1)}, u32[]{:S(2)}, u32[]{:S(2)}) collective-permute-start(bf16[512,512]{1,0:T(8,128)(2,1)S(1)} %select_select_fusion.refs_0_), channel_id=1, source_target_pairs={{0,2},{2,0},{1,3},{3,1},{4,6},{6,4},{5,7},{7,5},{8,10},{10,8},{9,1... | collective-permute-start | bytes 1572872 | tf_op jit(solution)/shard_map/ppermute | solution.py:58
  58.0 6.4 %collective-permute-start.16 = (bf16[256,512]{1,0:T(8,128)(2,1)S(1)}, bf16[256,512]{1,0:T(8,128)(2,1)S(1)}, u32[]{:S(2)}, u32[]{:S(2)}) collective-permute-start(bf16[256,512]{1,0:T(8,128)(2,1)S(1)} %collective-permute-done.14.refs_3_), channel_id=1, source_target_pairs={{0,2},{2,0},{1,3},{3,1},{4,6},{6,4},{5,7},{7,5},{8,10},{10,8},{9,1... | collective-permute-start | bytes 786440 | tf_op jit(solution)/shard_map/ppermute | solution.py:58
  58.1 6.4 %collective-permute-start.15 = (bf16[256,512]{1,0:T(8,128)(2,1)S(1)}, bf16[256,512]{1,0:T(8,128)(2,1)S(1)}, u32[]{:S(2)}, u32[]{:S(2)}) collective-permute-start(bf16[256,512]{1,0:T(8,128)(2,1)S(1)} %collective-permute-done.13.refs_2_), channel_id=1, source_target_pairs={{0,2},{2,0},{1,3},{3,1},{4,6},{6,4},{5,7},{7,5},{8,10},{10,8},{9,1... | collective-permute-start | bytes 786440 | tf_op jit(solution)/shard_map/ppermute | solution.py:58
  58.5 9.4 %collective-permute-start.18 = (bf16[256,512]{1,0:T(8,128)(2,1)S(1)}, bf16[256,512]{1,0:T(8,128)(2,1)S(1)}, u32[]{:S(2)}, u32[]{:S(2)}) collective-permute-start(bf16[256,512]{1,0:T(8,128)(2,1)S(1)} %broadcast_select_fusion.6.refs_0_), channel_id=1, source_target_pairs={{2,6},{6,2},{10,14},{14,10},{18,22},{22,18},{26,30},{30,26},{3,7},... | collective-permute-start | bytes 786440 | tf_op jit(solution)/shard_map/ppermute | solution.py:58
  59.8 8.2 %collective-permute-start.21 = (bf16[256,512]{1,0:T(8,128)(2,1)S(1)}, bf16[256,512]{1,0:T(8,128)(2,1)S(1)}, u32[]{:S(2)}, u32[]{:S(2)}) collective-permute-start(bf16[256,512]{1,0:T(8,128)(2,1)S(1)} %broadcast_select_fusion.5.refs_1_), channel_id=1, source_target_pairs={{0,2},{2,0},{1,3},{3,1},{4,6},{6,4},{5,7},{7,5},{8,10},{10,8},{9,1... | collective-permute-start | bytes 786440 | tf_op jit(solution)/shard_map/ppermute | solution.py:58
  64.4 3.6 %collective-permute-start.20 = (bf16[256,512]{1,0:T(8,128)(2,1)S(1)}, bf16[256,512]{1,0:T(8,128)(2,1)S(1)}, u32[]{:S(2)}, u32[]{:S(2)}) collective-permute-start(bf16[256,512]{1,0:T(8,128)(2,1)S(1)} %broadcast_select_fusion.6.refs_0_), channel_id=1, source_target_pairs={{0,2},{2,0},{1,3},{3,1},{4,6},{6,4},{5,7},{7,5},{8,10},{10,8},{9,1... | collective-permute-start | bytes 786440 | tf_op jit(solution)/shard_map/ppermute | solution.py:58
  64.5 5.6 %collective-permute-start.22 = (bf16[256,512]{1,0:T(8,128)(2,1)S(1)}, bf16[256,512]{1,0:T(8,128)(2,1)S(1)}, u32[]{:S(2)}, u32[]{:S(2)}) collective-permute-start(bf16[256,512]{1,0:T(8,128)(2,1)S(1)} %broadcast_select_fusion.5.refs_1_), channel_id=1, source_target_pairs={{2,6},{6,2},{10,14},{14,10},{18,22},{22,18},{26,30},{30,26},{3,7},... | collective-permute-start | bytes 786440 | tf_op jit(solution)/shard_map/ppermute | solution.py:58
  70.1 2.3 %collective-permute-start.23 = (bf16[256,512]{1,0:T(8,128)(2,1)S(1)}, bf16[256,512]{1,0:T(8,128)(2,1)S(1)}, u32[]{:S(2)}, u32[]{:S(2)}) collective-permute-start(bf16[256,512]{1,0:T(8,128)(2,1)S(1)} %collective-permute-done.18.refs_0_), channel_id=1, source_target_pairs={{0,2},{2,0},{1,3},{3,1},{4,6},{6,4},{5,7},{7,5},{8,10},{10,8},{9,1... | collective-permute-start | bytes 786440 | tf_op jit(solution)/shard_map/ppermute | solution.py:58
  (6 other events, 12.8 us)
